TPU v7x, 32 devices: a whole 2x2x4 slice. The times are simulated.
32 devices in a mesh: group: 2 (over x), row: 16 (over z, y, core).
Axes of the slice: x: 2, y: 2, z: 4, core: 2. Of those that a mesh axis runs over, the one named last changes fastest.
Arguments:
- fine_features: bfloat16 [256, 256, 192], P(None, ('group', 'row')), parts along dimension 1, may hold values from -6 to 6
- section_two: bfloat16 [128, 128, 384], P('row', 'group'), parts along dimension 1, may hold values from -6 to 6
- section_three: bfloat16 [64, 64, 768], P('row', 'group'), parts along dimension 1, may hold values from -6 to 6
- section_four: bfloat16 [32, 32, 1536], P('row', 'group'), parts along dimension 1, may hold values from -6 to 6
- strip_map: int32 [32], P('group'), parts along dimension 0, may hold values from 0 to 15, each once
- lateral_one: bfloat16 [192, 512], replicated, may hold values from -0.4375 to 0.4375
- lateral_two: bfloat16 [384, 512], replicated, may hold values from -0.3125 to 0.3125
- lateral_three: bfloat16 [768, 512], replicated, may hold values from -0.21875 to 0.21875
- lateral_four: bfloat16 [1536, 512], replicated, may hold values from -0.15625 to 0.15625
- join_weight: bfloat16 [512, 512], replicated, may hold values from -0.25 to 0.25
- cotangent: bfloat16 [256, 256, 512], P(None, ('group', 'row')), parts along dimension 1, may hold values from -6 to 6
Outputs:
- grad_fine: bfloat16 [256, 256, 192], P(None, ('group', 'row')), parts along dimension 1
- grad_two: bfloat16 [128, 128, 384], P('row', 'group'), parts along dimension 1
- grad_three: bfloat16 [64, 64, 768], P('row', 'group'), parts along dimension 1
- grad_four: bfloat16 [32, 32, 1536], P('row', 'group'), parts along dimension 1
- grad_join: float32 [1024, 512], P('group', 'row'), parts along dimension 0
- grad_lateral_one: float32 [384, 512], P(('group', 'row')), parts along dimension 0
- grad_lateral_two: float32 [768, 512], P(('group', 'row')), parts along dimension 0
- grad_lateral_three: float32 [1536, 512], P(('group', 'row')), parts along dimension 0
- grad_lateral_four: float32 [3072, 512], P(('group', 'row')), parts along dimension 0
There are 2 independent parts, one for each index of `group`. A program takes and returns all parts, laid end to end along the dimension named above; an argument that names none is the same for every part. Nothing has to cross between parts.
Inputs may be any that keep to these rules, and one draw needn't show every extreme that they name: strip_map holds each strip number of 0 to 15 once.
All inputs are finite; a program needn't handle non-finite values.
Results may differ from a plain program's by a relative error of at most 0.01.
Values may be sent and summed in bfloat16 or wider, within the bound.
No kernel may reach another device: no remote copies, remote signals or barrier semaphores. Data moves between devices by JAX's collectives and lax.ppermute only.
A program may use at most 128 MiB of HBM per device.

v0:
```python
import functools

import jax
import jax.numpy as jnp
import numpy as np
from jax import lax
from jax.experimental import pallas as pl
from jax.experimental.pallas import tpu as pltpu
from jax.sharding import PartitionSpec as P

F32 = jnp.float32
BF16 = jnp.bfloat16
FACTORS = (2, 4, 8)
LANES = 128
VMEM = pl.BlockSpec(memory_space=pltpu.VMEM)
SMEM = pl.BlockSpec(memory_space=pltpu.SMEM)
MEBI = 1024 * 1024


def round_up(value, multiple):
    return -(-value // multiple) * multiple


class Plan:
    def __init__(self, owners, depth, strip_width, channels, width):
        self.owners, self.depth, self.strip_width = owners, depth, strip_width
        self.width = width
        self.rows = [depth * 8 // k for k in FACTORS]
        self.columns = [strip_width // k for k in FACTORS]
        self.two = [(0, r, c) for r in range(self.rows[0]) for c in range(self.columns[0] + 2)]
        self.rest = [
            (s, r, c) for s in (1, 2) for r in range(self.rows[s]) for c in range(self.columns[s] + 2)
        ]
        self.n_two = round_up(len(self.two), 8)
        self.n_rest = round_up(len(self.rest), 8)
        self.two += [None] * (self.n_two - len(self.two))
        self.rest += [None] * (self.n_rest - len(self.rest))
        self.chunks_two = channels[0] // LANES
        self.chunks_rest = width // LANES
        self.coarse = [r * c * owners for r, c in zip(self.rows, self.columns)]
        self.rest_at = self.chunks_two * self.n_two
        self.slice_at = self.rest_at + self.chunks_rest * self.n_rest
        self.slice_width = channels[2] // owners
        self.sent = self.slice_at + round_up(self.coarse[2], 8)
        self.per_owner = round_up(self.n_two + self.n_rest, 16)
        self.positions = self.two + self.rest
        self.positions += [None] * (self.per_owner - len(self.positions))


def axis_weights(fine_count, factor):
    matrix = np.zeros((fine_count, fine_count // factor + 2), np.float32)
    for fine in range(fine_count):
        base, phase = divmod(fine, factor)
        offset = (phase + 0.5) / factor - 0.5
        if offset < 0:
            matrix[fine, base] += -offset
            matrix[fine, base + 1] += 1.0 + offset
        else:
            matrix[fine, base + 1] += 1.0 - offset
            matrix[fine, base + 2] += offset
    return matrix


def clamp_rows(matrix):
    folded = matrix[:, 1:-1].copy()
    folded[:, 0] += matrix[:, 0]
    folded[:, -1] += matrix[:, -1]
    return folded


def window_matrices(plan):
    owners, strip_width = plan.owners, plan.strip_width
    block_rows = plan.depth * 8
    fine_rows = owners * block_rows
    whole = np.zeros((fine_rows, strip_width, owners, plan.per_owner), np.float32)
    row_mats = [clamp_rows(axis_weights(fine_rows, k)) for k in FACTORS]
    col_mats = [axis_weights(strip_width, k) for k in FACTORS]
    for owner in range(owners):
        for index, entry in enumerate(plan.positions):
            if entry is not None:
                section, row, column = entry
                at = owner * plan.rows[section] + row
                whole[:, :, owner, index] = np.outer(
                    row_mats[section][:, at], col_mats[section][:, column]
                )
    up, down = [], []
    for owner in (0, 1, owners - 1):
        start = min(max(owner - 1, 0), owners - 3)
        rows = slice(owner * block_rows, (owner + 1) * block_rows)
        up.append(
            whole[rows, :, start : start + 3].reshape(block_rows * strip_width, 3 * plan.per_owner)
        )
        window = block_rows + 8
        low = min(max(owner * block_rows - 4, 0), fine_rows - window)
        piece = whole[low : low + window, :, owner]
        down.append(piece.reshape(window * strip_width, plan.per_owner).T)
    return np.stack(up).astype(BF16), np.stack(down).astype(BF16)


def selection(strip_map, plan, entries, sections):
    as_int = functools.partial(np.array, dtype=np.int32)
    strips = plan.owners
    offsets, at = {}, 0
    for s in sections:
        offsets[s] = at
        at += plan.coarse[s]
    start, base, span, limit = [], [], [], []
    for entry in entries:
        if entry is None:
            start.append(-1)
            base.append(0)
            span.append(0)
            limit.append(0)
            continue
        section, row, column = entry
        start.append(offsets[section] + row * plan.columns[section] * strips)
        base.append(column - 1)
        span.append(plan.columns[section])
        limit.append(strips * plan.columns[section] - 1)
    column = jnp.clip(strip_map[:, None] * as_int(span) + as_int(base), 0, as_int(limit))
    target = (column + as_int(start)).reshape(-1)
    places = np.arange(at, dtype=np.int32)
    pick = (target[:, None] == places[None]).astype(BF16)
    fold = (places[:, None] == target[None]).astype(BF16)
    return pick, fold


def contract(left, right, left_dim, right_dim):
    return lax.dot_general(
        left, right, (((left_dim,), (right_dim,)), ((), ())), preferred_element_type=F32
    )


def put_pieces(ref, at, values, count):
    owners = ref.shape[0]
    for piece in range(values.shape[1] // LANES):
        part = values[:, piece * LANES : (piece + 1) * LANES]
        ref[:, at + piece * count : at + (piece + 1) * count, :] = part.reshape(owners, count, LANES)


def take_pieces(ref, at, pieces, count):
    owners = ref.shape[0]
    return jnp.concatenate(
        [
            ref[:, at + p * count : at + (p + 1) * count, :].reshape(owners * count, LANES)
            for p in range(pieces)
        ],
        axis=1,
    )


def pack_kernel(plan, two_ref, three_ref, four_ref, l3_ref, l4_ref, pick_two_ref, pick_rest_ref, out_ref):
    picked = contract(pick_two_ref[...], two_ref[...], 1, 0).astype(BF16)
    put_pieces(out_ref, 0, picked, plan.n_two)
    projected = jnp.concatenate(
        [
            contract(three_ref[...], l3_ref[...], 1, 0).astype(BF16),
            contract(four_ref[...], l4_ref[...], 1, 0).astype(BF16),
        ]
    )
    picked = contract(pick_rest_ref[...], projected, 1, 0).astype(BF16)
    put_pieces(out_ref, plan.rest_at, picked, plan.n_rest)
    count = four_ref.shape[0]
    for owner in range(plan.owners):
        part = four_ref[:, owner * plan.slice_width : (owner + 1) * plan.slice_width]
        fill = jnp.zeros((count, LANES - plan.slice_width), BF16)
        out_ref[owner, plan.slice_at : plan.slice_at + count, :] = jnp.concatenate([part, fill], axis=1)


def put_parts(core, keep_ref, give_ref, at, part_ref):
    owners = 2 * keep_ref.shape[0]
    height = part_ref.shape[0] // owners
    for owner in range(owners):
        rows = part_ref[owner * height : (owner + 1) * height, :].astype(BF16)

        @pl.when(core == owner % 2)
        def _():
            keep_ref[owner // 2, at : at + height, :] = rows

        @pl.when(core != owner % 2)
        def _():
            give_ref[owner // 2, at : at + height, :] = rows


def strip_kernel(
    plan,
    core_ref,
    up_ref,
    down_ref,
    arrived_ref,
    fine_ref,
    cot_ref,
    l1_ref,
    l2_ref,
    join_ref,
    grad_fine_ref,
    back_ref,
    keep_a_ref,
    give_a_ref,
    keep_b_ref,
    give_b_ref,
    coarse_ref,
    hidden_ref,
    joined_grad_ref,
    two_grad_ref,
    join_part_ref,
    one_part_ref,
    two_part_ref,
):
    owners, n_two, n_rest, per_owner = plan.owners, plan.n_two, plan.n_rest, plan.per_owner
    core = core_ref[0]
    block = up_ref.shape[1]
    reach = up_ref.shape[2]
    window = down_ref.shape[2]
    total = cot_ref.shape[0]
    width = plan.width

    def variant(owner):
        return jnp.where(owner == 0, 0, jnp.where(owner == owners - 1, 2, 1))

    features = take_pieces(arrived_ref, 0, plan.chunks_two, n_two)
    projected = contract(features, l2_ref[...], 1, 0).astype(BF16).reshape(owners, n_two, width)
    rest = take_pieces(arrived_ref, plan.rest_at, plan.chunks_rest, n_rest).reshape(owners, n_rest, width)
    tail = per_owner - n_two - n_rest
    filled = [projected, rest] + ([jnp.zeros((owners, tail, width), BF16)] if tail else [])
    coarse_ref[...] = jnp.concatenate(filled, axis=1).reshape(owners * per_owner, width)

    @pl.loop(0, owners)
    def _(owner):
        start = pl.multiple_of(jnp.clip(owner - 1, 0, owners - 3) * per_owner, 16)
        rows = pl.ds(pl.multiple_of(owner * block, block), block)
        joined = contract(fine_ref[rows, :], l1_ref[...], 1, 0)
        joined += contract(up_ref[variant(owner)], coarse_ref[pl.ds(start, reach), :], 1, 0)
        gate = 0.5 + 0.5 * jnp.tanh(0.5 * joined)
        hidden = joined * gate
        hidden_ref[rows, :] = hidden.astype(BF16)
        slope = gate + hidden * (1.0 - gate)
        hidden_grad = contract(cot_ref[rows, :], join_ref[...], 1, 1)
        joined_grad = (hidden_grad * slope).astype(BF16)
        joined_grad_ref[rows, :] = joined_grad
        grad_fine_ref[rows, :] = contract(joined_grad, l1_ref[...], 1, 1).astype(BF16)

    @pl.loop(0, owners)
    def _(owner):
        low = pl.multiple_of(jnp.clip(owner * block - 32, 0, total - window), 32)
        strip_grad = contract(
            down_ref[variant(owner)], joined_grad_ref[pl.ds(low, window), :], 1, 0
        ).astype(BF16)
        two_grad_ref[owner] = strip_grad[:n_two]
        for piece in range(plan.chunks_rest):
            at = plan.rest_at + piece * n_rest
            back_ref[owner, at : at + n_rest, :] = strip_grad[
                n_two : n_two + n_rest, piece * LANES : (piece + 1) * LANES
            ]

    two_grad = two_grad_ref[...].reshape(owners * n_two, width)
    put_pieces(back_ref, 0, contract(two_grad, l2_ref[...], 1, 1).astype(BF16), n_two)
    join_part_ref[...] = contract(cot_ref[...], hidden_ref[...], 0, 0)
    one_part_ref[...] = contract(fine_ref[...], joined_grad_ref[...], 0, 0)
    two_part_ref[...] = contract(features, two_grad, 0, 0)
    put_parts(core, keep_a_ref, give_a_ref, 0, join_part_ref)
    two_height = two_part_ref.shape[0] // owners
    put_parts(core, keep_b_ref, give_b_ref, 0, two_part_ref)
    put_parts(core, keep_b_ref, give_b_ref, two_height, one_part_ref)
    used = two_height + one_part_ref.shape[0] // owners
    if used < keep_b_ref.shape[1]:
        fill = jnp.zeros((owners // 2, keep_b_ref.shape[1] - used, width), BF16)
        keep_b_ref[:, used:, :] = fill
        give_b_ref[:, used:, :] = fill


def fold_kernel(plan, core_ref, returned_ref, fold_ref, three_ref, g3_ref, g4_ref, keep_a_ref, give_a_ref, keep_b_ref, give_b_ref, part_ref):
    core = core_ref[0]
    rest = take_pieces(returned_ref, plan.rest_at, plan.chunks_rest, plan.n_rest)
    folded = contract(fold_ref[...], rest, 1, 0).astype(BF16)
    count = three_ref.shape[0]
    g3_ref[...] = folded[:count]
    g4_ref[...] = folded[count:]
    part_ref[...] = contract(three_ref[...], folded[:count], 0, 0)
    owners = plan.owners
    height = part_ref.shape[0] // owners
    half = height // 2
    for owner in range(owners):
        rows = part_ref[owner * height : (owner + 1) * height, :].astype(BF16)

        @pl.when(core == owner % 2)
        def _():
            keep_a_ref[owner // 2] = rows[:half]
            keep_b_ref[owner // 2] = rows[half:]

        @pl.when(core != owner % 2)
        def _():
            give_a_ref[owner // 2] = rows[:half]
            give_b_ref[owner // 2] = rows[half:]


def section_kernel(plan, returned_ref, fold_ref, g3_ref, g4_ref, l3_ref, l4_ref, two_ref, three_ref, four_ref):
    features = take_pieces(returned_ref, 0, plan.chunks_two, plan.n_two)
    two_ref[...] = contract(fold_ref[...], features, 1, 0).astype(BF16)
    three_ref[...] = contract(g3_ref[...], l3_ref[...], 1, 1).astype(BF16)
    four_ref[...] = contract(g4_ref[...], l4_ref[...], 1, 1).astype(BF16)


def swap(values, bit):
    owners = lax.axis_size("row")
    return lax.ppermute(values, "row", [(i, i ^ (1 << bit)) for i in range(owners)])


def plus(left, right):
    return (left.astype(F32) + right.astype(F32)).astype(BF16)


class Halving:
    def __init__(self, values, order):
        bits = len(order)
        self.values = values.reshape((2,) * bits + values.shape[1:])
        self.left = sorted(order, reverse=True)
        self.order = list(order)

    def step(self):
        bit = self.order.pop(0)
        axis = self.left.index(bit)
        self.left.pop(axis)
        mine = (lax.axis_index("row") >> bit) & 1
        keep = lax.dynamic_index_in_dim(self.values, mine, axis, keepdims=False)
        give = lax.dynamic_index_in_dim(self.values, 1 - mine, axis, keepdims=False)
        self.values = plus(keep, swap(give, bit))


def reduce_pair(first, second, bits):
    orders = list(range(1, bits)), list(range(1, bits))
    if bits > 2:
        orders[1][0], orders[1][1] = orders[1][1], orders[1][0]
    chains = [Halving(plus(keep, swap(give, 0)), order) for (keep, give), order in zip((first, second), orders)]
    for _ in range(1, bits):
        for chain in chains:
            chain.step()
    return [chain.values for chain in chains]


def gather_blocks(values, bits):
    stacked, pattern = values[None], np.zeros((1,), np.int32)
    for bit in bits:
        stacked = jnp.concatenate([stacked, swap(stacked, bit)])
        pattern = np.concatenate([pattern, pattern ^ (1 << bit)])
    return stacked, pattern


def shape_of(*dims, dtype=BF16):
    return jax.ShapeDtypeStruct(dims, dtype)


def body(
    fine_features,
    section_two,
    section_three,
    section_four,
    strip_map,
    lateral_one,
    lateral_two,
    lateral_three,
    lateral_four,
    join_weight,
    cotangent,
):
    owners = lax.axis_size("row")
    bits = owners.bit_length() - 1
    fine_height, strip_width, c1 = fine_features.shape
    width = join_weight.shape[0]
    sections = (section_two, section_three, section_four)
    channels = [s.shape[-1] for s in sections]
    plan = Plan(owners, section_four.shape[0], strip_width, channels, width)
    flats = [s.reshape(-1, s.shape[-1]) for s in sections]
    fine = fine_features.reshape(-1, c1)
    cot = cotangent.reshape(-1, width)
    total = fine.shape[0]
    me = lax.axis_index("row")
    core = (me & 1).astype(jnp.int32).reshape(1)
    pick_two, fold_two = selection(strip_map, plan, plan.two, (0,))
    pick_rest, fold_rest = selection(strip_map, plan, plan.rest, (1, 2))
    up, down = window_matrices(plan)
    exchange = functools.partial(lax.all_to_all, axis_name="row", split_axis=0, concat_axis=0, tiled=True)

    outgoing = pl.pallas_call(
        functools.partial(pack_kernel, plan),
        out_shape=shape_of(owners, plan.sent, LANES),
        in_specs=[VMEM] * 7,
        out_specs=VMEM,
        compiler_params=pltpu.CompilerParams(vmem_limit_bytes=32 * MEBI),
        name="pack",
    )(*flats, lateral_three, lateral_four, pick_two, pick_rest)
    arrived = exchange(outgoing)

    half = owners // 2
    heights = [width // owners, c1 // owners, channels[0] // owners]
    b_height = round_up(heights[1] + heights[2], 8)
    grad_fine, back, keep_a, give_a, keep_b, give_b = pl.pallas_call(
        functools.partial(strip_kernel, plan),
        out_shape=(
            shape_of(total, c1),
            shape_of(owners, plan.slice_at, LANES),
            shape_of(half, heights[0], width),
            shape_of(half, heights[0], width),
            shape_of(half, b_height, width),
            shape_of(half, b_height, width),
        ),
        in_specs=[SMEM] + [VMEM] * 8,
        out_specs=(VMEM,) * 6,
        scratch_shapes=[
            pltpu.VMEM((owners * plan.per_owner, width), BF16),
            pltpu.VMEM((total, width), BF16),
            pltpu.VMEM((total, width), BF16),
            pltpu.VMEM((owners, plan.n_two, width), BF16),
            pltpu.VMEM((width, width), F32),
            pltpu.VMEM((c1, width), F32),
            pltpu.VMEM((channels[0], width), F32),
        ],
        compiler_params=pltpu.CompilerParams(vmem_limit_bytes=48 * MEBI),
        cost_estimate=pl.CostEstimate(
            flops=5_000_000_000, bytes_accessed=9_000_000, transcendentals=total * width
        ),
        name="strip_work",
    )(core, up, down, arrived, fine, cot, lateral_one, lateral_two, join_weight)

    returned = exchange(back)
    early = reduce_pair((keep_a, give_a), (keep_b, give_b), bits)

    late_height = channels[1] // owners // 2
    g3, g4, keep_a, give_a, keep_b, give_b = pl.pallas_call(
        functools.partial(fold_kernel, plan),
        out_shape=(shape_of(plan.coarse[1], width), shape_of(plan.coarse[2], width))
        + (shape_of(half, late_height, width),) * 4,
        in_specs=[SMEM] + [VMEM] * 3,
        out_specs=(VMEM,) * 6,
        scratch_shapes=[pltpu.VMEM((channels[1], width), F32)],
        compiler_params=pltpu.CompilerParams(vmem_limit_bytes=32 * MEBI),
        name="fold_rest",
    )(core, returned, fold_rest, flats[1])
    gathered, pattern = gather_blocks(g4, list(range(bits))[::-1])
    late = reduce_pair((keep_a, give_a), (keep_b, give_b), bits)

    grads = pl.pallas_call(
        functools.partial(section_kernel, plan),
        out_shape=tuple(shape_of(*f.shape) for f in flats),
        in_specs=[VMEM] * 6,
        out_specs=(VMEM,) * 3,
        compiler_params=pltpu.CompilerParams(vmem_limit_bytes=32 * MEBI),
        cost_estimate=pl.CostEstimate(flops=500_000_000, bytes_accessed=6_000_000, transcendentals=0),
        name="section_grads",
    )(returned, fold_two, g3, g4, lateral_three, lateral_four)

    slices = arrived[:, plan.slice_at : plan.slice_at + plan.coarse[2], : plan.slice_width]
    slices = jnp.take(slices, me ^ pattern, axis=0).reshape(-1, plan.slice_width)
    grad_four_weight = contract(slices, gathered.reshape(-1, width), 0, 0)
    wide = [x.astype(F32) for x in early]
    return (
        grad_fine.reshape(fine_features.shape),
        *[g.reshape(s.shape) for g, s in zip(grads, sections)],
        wide[0].T,
        wide[1][heights[2] : heights[2] + heights[1]],
        wide[1][: heights[2]],
        jnp.concatenate(late, axis=0).astype(F32),
        grad_four_weight,
    )


def solution(mesh):
    fine_spec = P(None, ("group", "row"), None)
    coarse_spec = P("row", "group", None)
    weight_spec = P(("group", "row"), None)
    return jax.shard_map(
        body,
        mesh=mesh,
        in_specs=(fine_spec,) + (coarse_spec,) * 3 + (P("group"),) + (P(),) * 5 + (fine_spec,),
        out_specs=(fine_spec,) + (coarse_spec,) * 3 + (P("group", "row"),) + (weight_spec,) * 4,
        check_vma=False,
    )
```

profile of v0, /device:TPU:0, one launch (start us, length us, event | category | flops | bytes accessed | tf_op | source)
XLA Modules:
  0.0 140.0 jit_solution(3855440258887198858)
XLA Ops:
  0.7 0.7 broadcast_multiply_fusion
  1.4 0.7 clamp_add_fusion
  2.2 0.8 minimum_add_fusion
  3.0 0.1 reshape.265
  3.1 0.1 fusion.2.pick_rest_ref
  3.2 0.2 fusion.pick_two_ref
  3.4 1.4 copy-done
  4.8 0.9 copy-done.4
  5.8 1.0 copy-done.7
  6.8 0.9 copy-done.10
  7.7 2.1 %pack.1 = bf16[16,272,128]{2,1,0:T(8,128)(2,1)} custom-call(bf16[512,384]{1,0:T(8,128)(2,1)S(1)} %bitcast.101, bf16[128,768]{1,0:T(8,128)(2,1)S(1)} %bitcast.99, bf16[32,1536]{1,0:T(8,128)(2,1)S(1)} %bitcast.102, bf16[768,512]{1,0:T(8,128)(2,1)S(1)} %copy-done.2, bf16[1536,512]{1,0:T(8,128)(2,1)S(1)} %copy-done, bf16[768,512]{1,0:T(8,128)(2,1)S(1)} %fusion.pick_two_ref, ...), custom_call_target="tpu_custom_call" | custom-call | tf_op jit(solution)/shard_map/pack/pallas_call | solution.py:384
  9.8 7.6 %all-to-all-start = ((bf16[16,272,128]{2,1,0:T(8,128)(2,1)}), bf16[16,272,128]{2,1,0:T(8,128)(2,1)}, u32[]{:S(2)}, u32[]{:S(2)}) async-start(bf16[16,272,128]{2,1,0:T(8,128)(2,1)} %pack.1), calls=%async_computation | async-start | bytes 2228224 | tf_op jit(solution)/shard_map/all_to_all | solution.py:392
  17.4 1.0 copy.35
  18.4 0.7 fusion.5.fold_ref
  19.1 22.4 %all-to-all-done.arrived_ref = bf16[16,272,128]{2,1,0:T(8,128)(2,1)} async-done(((bf16[16,272,128]{2,1,0:T(8,128)(2,1)}), bf16[16,272,128]{2,1,0:T(8,128)(2,1)}, u32[]{:S(2)}, u32[]{:S(2)}) %all-to-all-start) | async-done | bytes 1114144 | tf_op jit(solution)/shard_map/all_to_all | solution.py:392
  41.5 1.0 copy-done.11
  42.5 1.0 copy-done.12
  43.5 0.9 copy-done.16
  44.4 17.5 %strip_work.1 = (bf16[2048,192]{1,0:T(8,128)(2,1)S(1)}, bf16[16,240,128]{2,1,0:T(8,128)(2,1)}, bf16[8,32,512]{2,1,0:T(8,128)(2,1)S(1)}, bf16[8,32,512]{2,1,0:T(8...) custom-call(s32[1]{0:T(128)} %bitcast.core_ref, bf16[3,128,240]{2,1,0:T(8,128)(2,1)S(1)} %copy-done.16, ...), custom_call_target="tpu_custom_call" | custom-call | flops 5000000000 | bytes 9000000 | tf_op jit(solution)/shard_map/strip_work/pallas_call | solution.py:397
  62.0 0.7 copy-done.8
  62.7 0.7 copy-done.13
  63.4 0.7 collective-permute-start
  64.1 1.1 fusion.1.fold_ref
  65.2 1.6 %copy.44 = bf16[256,8,192]{0,2,1:T(8,128)(2,1)} copy(bf16[256,8,192]{2,1,0:T(8,128)(2,1)S(1)} %bitcast.93) | data formatting | bytes 1572864
  66.8 6.9 %all-to-all-start.1 = ((bf16[16,240,128]{2,1,0:T(8,128)(2,1)}), bf16[16,240,128]{2,1,0:T(8,128)(2,1)S(1)}, u32[]{:S(2)}, u32[]{:S(2)}) async-start(bf16[16,240,128]{2,1,0:T(8,128)(2,1)} %get-tuple-element.25), calls=%async_computation.1 | async-start | bytes 1966080 | tf_op jit(solution)/shard_map/all_to_all | solution.py:425
  73.7 0.5 collective-permute-start.4
  74.2 0.9 slice.16
  75.1 1.2 gather_fusion
  76.5 1.7 %collective-permute-start.1 = (bf16[2,2,32,512]{3,2,0,1:T(8,128)(2,1)S(1)}, bf16[2,2,32,512]{3,2,0,1:T(8,128)(2,1)S(1)}, u32[]{:S(2)}, u32[]{:S(2)}) collective-permute-start(bf16[2,2,32,512]{3,2,0,1:T(8,128)(2,1)S(1)} %bitcast.108), channel_id=1, source_target_pairs={{0,2},{1,3},{2,0},{3,1},{4,6},{5,7},{6,4},{7,5},{8,10},{9,11},{10,... | collective-permute-start | bytes 393224 | tf_op jit(solution)/shard_map/ppermute | solution.py:306
  78.2 1.1 add_convert_fusion
  79.3 7.4 %collective-permute-done.1 = bf16[2,2,32,512]{3,2,0,1:T(8,128)(2,1)S(1)} collective-permute-done((bf16[2,2,32,512]{3,2,0,1:T(8,128)(2,1)S(1)}, bf16[2,2,32,512]{3,2,0,1:T(8,128)(2,1)S(1)}, u32[]{:S(2)}, u32[]{:S(2)}) %collective-permute-start.1) | collective-permute-done | bytes 131104 | tf_op jit(solution)/shard_map/ppermute | solution.py:306
  86.8 0.9 collective-permute-start.2
  87.7 1.3 collective-permute-start.5
  89.0 3.3 %collective-permute-done.2 = bf16[2,32,512]{2,1,0:T(8,128)(2,1)S(1)} collective-permute-done((bf16[2,32,512]{2,1,0:T(8,128)(2,1)S(1)}, bf16[2,32,512]{2,1,0:T(8,128)(2,1)S(1)}, u32[]{:S(2)}, u32[]{:S(2)}) %collective-permute-start.2) | collective-permute-done | bytes 65568 | tf_op jit(solution)/shard_map/ppermute | solution.py:306
  92.4 5.2 %collective-permute-done.5 = bf16[2,2,40,512]{3,2,0,1:T(8,128)(2,1)S(1)} collective-permute-done((bf16[2,2,40,512]{3,2,0,1:T(8,128)(2,1)S(1)}, bf16[2,2,40,512]{3,2,0,1:T(8,128)(2,1)S(1)}, u32[]{:S(2)}, u32[]{:S(2)}) %collective-permute-start.5) | collective-permute-done | bytes 163872 | tf_op jit(solution)/shard_map/ppermute | solution.py:306
  97.6 2.0 %collective-permute-start.6 = (bf16[2,40,512]{2,1,0:T(8,128)(2,1)S(1)}, bf16[2,40,512]{2,1,0:T(8,128)(2,1)S(1)}, u32[]{:S(2)}, u32[]{:S(2)}) collective-permute-start(bf16[2,40,512]{2,1,0:T(8,128)(2,1)S(1)} %dynamic-slice_bitcast_fusion), channel_id=1, source_target_pairs={{0,2},{1,3},{2,0},{3,1},{4,6},{5,7},{6,4},{7,5},{8,10},{9,11},{10,... | collective-permute-start | bytes 245768 | tf_op jit(solution)/shard_map/ppermute | solution.py:306
  99.6 2.1 %collective-permute-start.3 = (bf16[32,512]{1,0:T(8,128)(2,1)S(1)}, bf16[32,512]{1,0:T(8,128)(2,1)S(1)}, u32[]{:S(2)}, u32[]{:S(2)}) collective-permute-start(bf16[32,512]{1,0:T(8,128)(2,1)S(1)} %dynamic-slice_bitcast_fusion.5), channel_id=1, source_target_pairs={{0,8},{1,9},{2,10},{3,11},{4,12},{5,13},{6,14},{7,15},{8,0},{9,1},... | collective-permute-start | bytes 98312 | tf_op jit(solution)/shard_map/ppermute | solution.py:306
  101.7 0.5 collective-permute-done.6
  102.2 3.3 %collective-permute-start.7 = (bf16[40,512]{1,0:T(8,128)(2,1)S(1)}, bf16[40,512]{1,0:T(8,128)(2,1)S(1)}, u32[]{:S(2)}, u32[]{:S(2)}) collective-permute-start(bf16[40,512]{1,0:T(8,128)(2,1)S(1)} %dynamic-slice_bitcast_fusion.4), channel_id=1, source_target_pairs={{0,8},{1,9},{2,10},{3,11},{4,12},{5,13},{6,14},{7,15},{8,0},{9,1},... | collective-permute-start | bytes 122888 | tf_op jit(solution)/shard_map/ppermute | solution.py:306
  105.5 0.6 convert_bitcast_fusion
  106.2 1.8 %collective-permute-done.7 = bf16[40,512]{1,0:T(8,128)(2,1)S(1)} collective-permute-done((bf16[40,512]{1,0:T(8,128)(2,1)S(1)}, bf16[40,512]{1,0:T(8,128)(2,1)S(1)}, u32[]{:S(2)}, u32[]{:S(2)}) %collective-permute-start.7) | collective-permute-done | bytes 40992 | tf_op jit(solution)/shard_map/ppermute | solution.py:306
  108.0 0.6 slice.14
  108.6 0.6 slice.15
  109.2 0.9 copy-done.6
  110.1 0.7 fold_rest.1
  110.9 2.5 %collective-permute-start.16 = (bf16[1,32,512]{2,1,0:T(8,128)(2,1)S(1)}, bf16[1,32,512]{2,1,0:T(8,128)(2,1)S(1)}, u32[]{:S(2)}, u32[]{:S(2)}) collective-permute-start(bf16[1,32,512]{2,1,0:T(8,128)(2,1)S(1)} %bitcast.95), channel_id=1, source_target_pairs={{0,8},{1,9},{2,10},{3,11},{4,12},{5,13},{6,14},{7,15},{8,0},{9,1},... | collective-permute-start | bytes 98312 | tf_op jit(solution)/shard_map/ppermute | solution.py:306
  113.4 0.5 collective-permute-start.12
  113.9 1.9 %section_grads.1 = (bf16[512,384]{1,0:T(8,128)(2,1)}, bf16[128,768]{1,0:T(8,128)(2,1)}, bf16[32,1536]{1,0:T(8,128)(2,1)}) custom-call(bf16[16,240,128]{2,1,0:T(8,128)(2,1)S(1)} %all-to-all-done.1.returned_ref, bf16[512,768]{1,0:T(8,128)(2,1)S(1)} %copy-done.3, bf16[128,512]{1,0:T(8,128)(2,1)S(1)} %get-tuple-element.26.g3_ref, ...), custom_call_target="tpu_custom_call" | custom-call | flops 500000000 | bytes 6000000 | tf_op jit(solution)/shard_map/section_grads/pallas_call | solution.py:442
  115.8 2.6 %collective-permute-start.17 = (bf16[2,32,512]{2,1,0:T(8,128)(2,1)S(1)}, bf16[2,32,512]{2,1,0:T(8,128)(2,1)S(1)}, u32[]{:S(2)}, u32[]{:S(2)}) collective-permute-start(bf16[2,32,512]{2,1,0:T(8,128)(2,1)S(1)} %pad_maximum_fusion.2), channel_id=1, source_target_pairs={{0,4},{1,5},{2,6},{3,7},{4,0},{5,1},{6,2},{7,3},{8,12},{9,13},{10,... | collective-permute-start | bytes 196616 | tf_op jit(solution)/shard_map/ppermute | solution.py:306
  118.3 2.3 %collective-permute-done.17 = bf16[2,32,512]{2,1,0:T(8,128)(2,1)S(1)} collective-permute-done((bf16[2,32,512]{2,1,0:T(8,128)(2,1)S(1)}, bf16[2,32,512]{2,1,0:T(8,128)(2,1)S(1)}, u32[]{:S(2)}, u32[]{:S(2)}) %collective-permute-start.17) | collective-permute-done | bytes 65568 | tf_op jit(solution)/shard_map/ppermute | solution.py:306
  120.6 0.7 collective-permute-start.18
  121.4 1.5 %collective-permute-start.9 = (bf16[2,2,24,512]{3,2,0,1:T(8,128)(2,1)S(1)}, bf16[2,2,24,512]{3,2,0,1:T(8,128)(2,1)S(1)}, u32[]{:S(2)}, u32[]{:S(2)}) collective-permute-start(bf16[2,2,24,512]{3,2,0,1:T(8,128)(2,1)S(1)} %bitcast.109), channel_id=1, source_target_pairs={{0,2},{1,3},{2,0},{3,1},{4,6},{5,7},{6,4},{7,5},{8,10},{9,11},{10,... | collective-permute-start | bytes 294920 | tf_op jit(solution)/shard_map/ppermute | solution.py:306
  123.0 2.1 %collective-permute-start.13 = (bf16[2,2,24,512]{3,2,0,1:T(8,128)(2,1)S(1)}, bf16[2,2,24,512]{3,2,0,1:T(8,128)(2,1)S(1)}, u32[]{:S(2)}, u32[]{:S(2)}) collective-permute-start(bf16[2,2,24,512]{3,2,0,1:T(8,128)(2,1)S(1)} %bitcast.110), channel_id=1, source_target_pairs={{0,4},{1,5},{2,6},{3,7},{4,0},{5,1},{6,2},{7,3},{8,12},{9,13},{10,... | collective-permute-start | bytes 294920 | tf_op jit(solution)/shard_map/ppermute | solution.py:306
  125.1 1.6 %collective-permute-done.18 = bf16[4,32,512]{2,1,0:T(8,128)(2,1)S(1)} collective-permute-done((bf16[4,32,512]{2,1,0:T(8,128)(2,1)S(1)}, bf16[4,32,512]{2,1,0:T(8,128)(2,1)S(1)}, u32[]{:S(2)}, u32[]{:S(2)}) %collective-permute-start.18) | collective-permute-done | bytes 131104 | tf_op jit(solution)/shard_map/ppermute | solution.py:306
  126.8 0.9 collective-permute-done.9
  127.7 1.4 %collective-permute-start.10 = (bf16[2,24,512]{2,1,0:T(8,128)(2,1)S(1)}, bf16[2,24,512]{2,1,0:T(8,128)(2,1)S(1)}, u32[]{:S(2)}, u32[]{:S(2)}) collective-permute-start(bf16[2,24,512]{2,1,0:T(8,128)(2,1)S(1)} %dynamic-slice_bitcast_fusion.3), channel_id=1, source_target_pairs={{0,4},{1,5},{2,6},{3,7},{4,0},{5,1},{6,2},{7,3},{8,12},{9,13},{10,... | collective-permute-start | bytes 147464 | tf_op jit(solution)/shard_map/ppermute | solution.py:306
  129.2 0.6 collective-permute-start.14
  129.8 2.1 %collective-permute-done.10 = bf16[2,24,512]{2,1,0:T(8,128)(2,1)S(1)} collective-permute-done((bf16[2,24,512]{2,1,0:T(8,128)(2,1)S(1)}, bf16[2,24,512]{2,1,0:T(8,128)(2,1)S(1)}, u32[]{:S(2)}, u32[]{:S(2)}) %collective-permute-start.10) | collective-permute-done | bytes 49184 | tf_op jit(solution)/shard_map/ppermute | solution.py:306
  131.9 1.5 %collective-permute-start.11 = (bf16[24,512]{1,0:T(8,128)(2,1)S(1)}, bf16[24,512]{1,0:T(8,128)(2,1)S(1)}, u32[]{:S(2)}, u32[]{:S(2)}) collective-permute-start(bf16[24,512]{1,0:T(8,128)(2,1)S(1)} %dynamic-slice_bitcast_fusion.7), channel_id=1, source_target_pairs={{0,8},{1,9},{2,10},{3,11},{4,12},{5,13},{6,14},{7,15},{8,0},{9,1},... | collective-permute-start | bytes 73736 | tf_op jit(solution)/shard_map/ppermute | solution.py:306
  133.5 2.1 %collective-permute-start.15 = (bf16[24,512]{1,0:T(8,128)(2,1)S(1)}, bf16[24,512]{1,0:T(8,128)(2,1)S(1)}, u32[]{:S(2)}, u32[]{:S(2)}) collective-permute-start(bf16[24,512]{1,0:T(8,128)(2,1)S(1)} %dynamic-slice_bitcast_fusion.6), channel_id=1, source_target_pairs={{0,8},{1,9},{2,10},{3,11},{4,12},{5,13},{6,14},{7,15},{8,0},{9,1},... | collective-permute-start | bytes 73736 | tf_op jit(solution)/shard_map/ppermute | solution.py:306
  135.6 1.2 collective-permute-done.11
  136.7 1.5 %collective-permute-done.15 = bf16[24,512]{1,0:T(8,128)(2,1)S(1)} collective-permute-done((bf16[24,512]{1,0:T(8,128)(2,1)S(1)}, bf16[24,512]{1,0:T(8,128)(2,1)S(1)}, u32[]{:S(2)}, u32[]{:S(2)}) %collective-permute-start.15) | collective-permute-done | bytes 24608 | tf_op jit(solution)/shard_map/ppermute | solution.py:306
  138.3 0.7 maximum_convert_fusion
  139.0 1.0 convolution_bitcast_fusion
  (85 shorter events, 1.0 us)
Async XLA Ops:
  0.6 2.8 %copy-start.2 = (bf16[768,512]{1,0:T(8,128)(2,1)S(1)}, bf16[768,512]{1,0:T(8,128)(2,1)}, u32[]{:S(2)}) copy-start(bf16[768,512]{1,0:T(8,128)(2,1)} %l3_ref.3) | copy-start | bytes 2359300
  3.4 1.4 %copy-start = (bf16[1536,512]{1,0:T(8,128)(2,1)S(1)}, bf16[1536,512]{1,0:T(8,128)(2,1)}, u32[]{:S(2)}) copy-start(bf16[1536,512]{1,0:T(8,128)(2,1)} %l4_ref.3) | copy-start | bytes 4718596
  4.8 0.9 copy-start.4
  5.8 1.0 copy-start.7
  6.8 0.9 copy-start.10
  9.8 7.6 %copy-start.18 = (bf16[256,8,192]{0,2,1:T(8,128)(2,1)S(1)}, bf16[256,8,192]{0,2,1:T(8,128)(2,1)}, u32[]{:S(2)}) copy-start(bf16[256,8,192]{0,2,1:T(8,128)(2,1)} %param.26) | copy-start | bytes 2359300
  9.8 8.6 %copy-start.20 = (s32[16]{0:T(128)S(1)}, s32[16]{0:T(128)}, u32[]{:S(2)}) copy-start(s32[16]{0:T(128)} %constant.142.clone) | copy-start | bytes 196
  9.8 31.7 %copy-start.15 = (bf16[192,512]{1,0:T(8,128)(2,1)S(1)}, bf16[192,512]{1,0:T(8,128)(2,1)}, u32[]{:S(2)}) copy-start(bf16[192,512]{1,0:T(8,128)(2,1)} %l1_ref.1) | copy-start | bytes 589828
  9.8 31.7 %copy-start.17 = (bf16[3,80,192]{2,1,0:T(8,128)(2,1)S(1)}, bf16[3,80,192]{2,1,0:T(8,128)(2,1)}, u32[]{:S(2)}) copy-start(bf16[3,80,192]{2,1,0:T(8,128)(2,1)} %constant.141.clone.down_ref) | copy-start | bytes 276484
  9.8 31.7 %all-to-all-start = ((bf16[16,272,128]{2,1,0:T(8,128)(2,1)}), bf16[16,272,128]{2,1,0:T(8,128)(2,1)}, u32[]{:S(2)}, u32[]{:S(2)}) async-start(bf16[16,272,128]{2,1,0:T(8,128)(2,1)} %pack.1), calls=%async_computation | async-start | bytes 2228224 | tf_op jit(solution)/shard_map/all_to_all | solution.py:392
  41.5 1.0 copy-start.11
  42.5 1.0 copy-start.12
  43.5 0.9 copy-start.16
  62.0 0.7 copy-start.8
  62.7 0.7 copy-start.13
  63.4 13.0 %collective-permute-start = (bf16[8,32,512]{2,1,0:T(8,128)(2,1)}, bf16[8,32,512]{2,1,0:T(8,128)(2,1)S(1)}, u32[]{:S(2)}, u32[]{:S(2)}) collective-permute-start(bf16[8,32,512]{2,1,0:T(8,128)(2,1)} %get-tuple-element.32), channel_id=1, source_target_pairs={{0,1},{1,0},{2,3},{3,2},{4,5},{5,4},{6,7},{7,6},{8,9},{9,8},{10,11... | collective-permute-start | bytes 786440 | tf_op jit(solution)/shard_map/ppermute | solution.py:306
  65.2 8.5 %copy-start.14 = (bf16[8,40,512]{2,1,0:T(8,128)(2,1)S(1)}, bf16[8,40,512]{2,1,0:T(8,128)(2,1)}, u32[]{:S(2)}) copy-start(bf16[8,40,512]{2,1,0:T(8,128)(2,1)} %copy-done.13) | copy-start | bytes 983044
  66.8 9.5 %copy-start.9 = (bf16[8,32,512]{2,1,0:T(8,128)(2,1)S(1)}, bf16[8,32,512]{2,1,0:T(8,128)(2,1)}, u32[]{:S(2)}) copy-start(bf16[8,32,512]{2,1,0:T(8,128)(2,1)} %copy-done.8) | copy-start | bytes 786436
  66.8 42.4 %all-to-all-start.1 = ((bf16[16,240,128]{2,1,0:T(8,128)(2,1)}), bf16[16,240,128]{2,1,0:T(8,128)(2,1)S(1)}, u32[]{:S(2)}, u32[]{:S(2)}) async-start(bf16[16,240,128]{2,1,0:T(8,128)(2,1)} %get-tuple-element.25), calls=%async_computation.1 | async-start | bytes 1966080 | tf_op jit(solution)/shard_map/all_to_all | solution.py:425
  73.7 4.5 %collective-permute-start.4 = (bf16[8,40,512]{2,1,0:T(8,128)(2,1)S(1)}, bf16[8,40,512]{2,1,0:T(8,128)(2,1)}, u32[]{:S(2)}, u32[]{:S(2)}) collective-permute-start(bf16[8,40,512]{2,1,0:T(8,128)(2,1)S(1)} %copy-done.14), channel_id=1, source_target_pairs={{0,1},{1,0},{2,3},{3,2},{4,5},{5,4},{6,7},{7,6},{8,9},{9,8},{10,11... | collective-permute-start | bytes 983048 | tf_op jit(solution)/shard_map/ppermute | solution.py:306
  76.5 10.2 %collective-permute-start.1 = (bf16[2,2,32,512]{3,2,0,1:T(8,128)(2,1)S(1)}, bf16[2,2,32,512]{3,2,0,1:T(8,128)(2,1)S(1)}, u32[]{:S(2)}, u32[]{:S(2)}) collective-permute-start(bf16[2,2,32,512]{3,2,0,1:T(8,128)(2,1)S(1)} %bitcast.108), channel_id=1, source_target_pairs={{0,2},{1,3},{2,0},{3,1},{4,6},{5,7},{6,4},{7,5},{8,10},{9,11},{10,... | collective-permute-start | bytes 393224 | tf_op jit(solution)/shard_map/ppermute | solution.py:306
  86.7 22.5 %copy-start.5 = (bf16[4,32,768]{2,1,0:T(8,128)(2,1)S(1)}, bf16[4,32,768]{2,1,0:T(8,128)(2,1)}, u32[]{:S(2)}) copy-start(bf16[4,32,768]{2,1,0:T(8,128)(2,1)} %param.28) | copy-start | bytes 589828
  86.8 5.6 %collective-permute-start.2 = (bf16[2,32,512]{2,1,0:T(8,128)(2,1)S(1)}, bf16[2,32,512]{2,1,0:T(8,128)(2,1)S(1)}, u32[]{:S(2)}, u32[]{:S(2)}) collective-permute-start(bf16[2,32,512]{2,1,0:T(8,128)(2,1)S(1)} %dynamic-slice_bitcast_fusion.1), channel_id=1, source_target_pairs={{0,4},{1,5},{2,6},{3,7},{4,0},{5,1},{6,2},{7,3},{8,12},{9,13},{10,... | collective-permute-start | bytes 196616 | tf_op jit(solution)/shard_map/ppermute | solution.py:306
  87.7 26.2 %copy-start.1 = (bf16[1536,512]{1,0:T(8,128)(2,1)S(1)}, bf16[1536,512]{1,0:T(8,128)(2,1)}, u32[]{:S(2)}) copy-start(bf16[1536,512]{1,0:T(8,128)(2,1)} %l4_ref.3) | copy-start | bytes 4718596
  87.7 9.9 %collective-permute-start.5 = (bf16[2,2,40,512]{3,2,0,1:T(8,128)(2,1)S(1)}, bf16[2,2,40,512]{3,2,0,1:T(8,128)(2,1)S(1)}, u32[]{:S(2)}, u32[]{:S(2)}) collective-permute-start(bf16[2,2,40,512]{3,2,0,1:T(8,128)(2,1)S(1)} %bitcast.107), channel_id=1, source_target_pairs={{0,4},{1,5},{2,6},{3,7},{4,0},{5,1},{6,2},{7,3},{8,12},{9,13},{10,... | collective-permute-start | bytes 491528 | tf_op jit(solution)/shard_map/ppermute | solution.py:306
  97.6 4.5 %collective-permute-start.6 = (bf16[2,40,512]{2,1,0:T(8,128)(2,1)S(1)}, bf16[2,40,512]{2,1,0:T(8,128)(2,1)S(1)}, u32[]{:S(2)}, u32[]{:S(2)}) collective-permute-start(bf16[2,40,512]{2,1,0:T(8,128)(2,1)S(1)} %dynamic-slice_bitcast_fusion), channel_id=1, source_target_pairs={{0,2},{1,3},{2,0},{3,1},{4,6},{5,7},{6,4},{7,5},{8,10},{9,11},{10,... | collective-permute-start | bytes 245768 | tf_op jit(solution)/shard_map/ppermute | solution.py:306
  99.6 5.9 %collective-permute-start.3 = (bf16[32,512]{1,0:T(8,128)(2,1)S(1)}, bf16[32,512]{1,0:T(8,128)(2,1)S(1)}, u32[]{:S(2)}, u32[]{:S(2)}) collective-permute-start(bf16[32,512]{1,0:T(8,128)(2,1)S(1)} %dynamic-slice_bitcast_fusion.5), channel_id=1, source_target_pairs={{0,8},{1,9},{2,10},{3,11},{4,12},{5,13},{6,14},{7,15},{8,0},{9,1},... | collective-permute-start | bytes 98312 | tf_op jit(solution)/shard_map/ppermute | solution.py:306
  102.2 5.8 %collective-permute-start.7 = (bf16[40,512]{1,0:T(8,128)(2,1)S(1)}, bf16[40,512]{1,0:T(8,128)(2,1)S(1)}, u32[]{:S(2)}, u32[]{:S(2)}) collective-permute-start(bf16[40,512]{1,0:T(8,128)(2,1)S(1)} %dynamic-slice_bitcast_fusion.4), channel_id=1, source_target_pairs={{0,8},{1,9},{2,10},{3,11},{4,12},{5,13},{6,14},{7,15},{8,0},{9,1},... | collective-permute-start | bytes 122888 | tf_op jit(solution)/shard_map/ppermute | solution.py:306
  109.2 0.9 copy-start.6
  110.1 3.8 %copy-start.3 = (bf16[512,768]{1,0:T(8,128)(2,1)S(1)}, bf16[512,768]{1,0:T(8,128)(2,1)}, u32[]{:S(2)}) copy-start(bf16[512,768]{1,0:T(8,128)(2,1)} %fusion.1.fold_ref) | copy-start | bytes 2359300
  110.9 4.9 %collective-permute-start.16 = (bf16[1,32,512]{2,1,0:T(8,128)(2,1)S(1)}, bf16[1,32,512]{2,1,0:T(8,128)(2,1)S(1)}, u32[]{:S(2)}, u32[]{:S(2)}) collective-permute-start(bf16[1,32,512]{2,1,0:T(8,128)(2,1)S(1)} %bitcast.95), channel_id=1, source_target_pairs={{0,8},{1,9},{2,10},{3,11},{4,12},{5,13},{6,14},{7,15},{8,0},{9,1},... | collective-permute-start | bytes 98312 | tf_op jit(solution)/shard_map/ppermute | solution.py:306
  113.4 7.9 %collective-permute-start.8 = (bf16[8,24,512]{2,1,0:T(8,128)(2,1)S(1)}, bf16[8,24,512]{2,1,0:T(8,128)(2,1)S(1)}, u32[]{:S(2)}, u32[]{:S(2)}) collective-permute-start(bf16[8,24,512]{2,1,0:T(8,128)(2,1)S(1)} %get-tuple-element.36), channel_id=1, source_target_pairs={{0,1},{1,0},{2,3},{3,2},{4,5},{5,4},{6,7},{7,6},{8,9},{9,8},{10,11... | collective-permute-start | bytes 589832 | tf_op jit(solution)/shard_map/ppermute | solution.py:306
  113.4 9.5 %collective-permute-start.12 = (bf16[8,24,512]{2,1,0:T(8,128)(2,1)S(1)}, bf16[8,24,512]{2,1,0:T(8,128)(2,1)S(1)}, u32[]{:S(2)}, u32[]{:S(2)}) collective-permute-start(bf16[8,24,512]{2,1,0:T(8,128)(2,1)S(1)} %get-tuple-element.38), channel_id=1, source_target_pairs={{0,1},{1,0},{2,3},{3,2},{4,5},{5,4},{6,7},{7,6},{8,9},{9,8},{10,11... | collective-permute-start | bytes 589832 | tf_op jit(solution)/shard_map/ppermute | solution.py:306
  115.8 4.8 %collective-permute-start.17 = (bf16[2,32,512]{2,1,0:T(8,128)(2,1)S(1)}, bf16[2,32,512]{2,1,0:T(8,128)(2,1)S(1)}, u32[]{:S(2)}, u32[]{:S(2)}) collective-permute-start(bf16[2,32,512]{2,1,0:T(8,128)(2,1)S(1)} %pad_maximum_fusion.2), channel_id=1, source_target_pairs={{0,4},{1,5},{2,6},{3,7},{4,0},{5,1},{6,2},{7,3},{8,12},{9,13},{10,... | collective-permute-start | bytes 196616 | tf_op jit(solution)/shard_map/ppermute | solution.py:306
  120.6 6.0 %collective-permute-start.18 = (bf16[4,32,512]{2,1,0:T(8,128)(2,1)S(1)}, bf16[4,32,512]{2,1,0:T(8,128)(2,1)S(1)}, u32[]{:S(2)}, u32[]{:S(2)}) collective-permute-start(bf16[4,32,512]{2,1,0:T(8,128)(2,1)S(1)} %pad_maximum_fusion.1), channel_id=1, source_target_pairs={{0,2},{1,3},{2,0},{3,1},{4,6},{5,7},{6,4},{7,5},{8,10},{9,11},{10,... | collective-permute-start | bytes 393224 | tf_op jit(solution)/shard_map/ppermute | solution.py:306
  121.4 6.3 %collective-permute-start.9 = (bf16[2,2,24,512]{3,2,0,1:T(8,128)(2,1)S(1)}, bf16[2,2,24,512]{3,2,0,1:T(8,128)(2,1)S(1)}, u32[]{:S(2)}, u32[]{:S(2)}) collective-permute-start(bf16[2,2,24,512]{3,2,0,1:T(8,128)(2,1)S(1)} %bitcast.109), channel_id=1, source_target_pairs={{0,2},{1,3},{2,0},{3,1},{4,6},{5,7},{6,4},{7,5},{8,10},{9,11},{10,... | collective-permute-start | bytes 294920 | tf_op jit(solution)/shard_map/ppermute | solution.py:306
  123.0 16.0 %copy-start.19 = (bf16[16,32,96]{2,1,0:T(8,128)(2,1)S(1)}, bf16[16,32,96]{2,1,0:T(8,128)(2,1)}, u32[]{:S(2)}) copy-start(bf16[16,32,96]{2,1,0:T(8,128)(2,1)} %gather_fusion) | copy-start | bytes 294916
  123.0 6.2 %collective-permute-start.13 = (bf16[2,2,24,512]{3,2,0,1:T(8,128)(2,1)S(1)}, bf16[2,2,24,512]{3,2,0,1:T(8,128)(2,1)S(1)}, u32[]{:S(2)}, u32[]{:S(2)}) collective-permute-start(bf16[2,2,24,512]{3,2,0,1:T(8,128)(2,1)S(1)} %bitcast.110), channel_id=1, source_target_pairs={{0,4},{1,5},{2,6},{3,7},{4,0},{5,1},{6,2},{7,3},{8,12},{9,13},{10,... | collective-permute-start | bytes 294920 | tf_op jit(solution)/shard_map/ppermute | solution.py:306
  126.7 12.3 %collective-permute-start.19 = (bf16[8,32,512]{2,1,0:T(8,128)(2,1)S(1)}, bf16[8,32,512]{2,1,0:T(8,128)(2,1)S(1)}, u32[]{:S(2)}, u32[]{:S(2)}) collective-permute-start(bf16[8,32,512]{2,1,0:T(8,128)(2,1)S(1)} %pad_maximum_fusion), channel_id=1, source_target_pairs={{0,1},{1,0},{2,3},{3,2},{4,5},{5,4},{6,7},{7,6},{8,9},{9,8},{10,11... | collective-permute-start | bytes 786440 | tf_op jit(solution)/shard_map/ppermute | solution.py:306
  127.7 4.2 %collective-permute-start.10 = (bf16[2,24,512]{2,1,0:T(8,128)(2,1)S(1)}, bf16[2,24,512]{2,1,0:T(8,128)(2,1)S(1)}, u32[]{:S(2)}, u32[]{:S(2)}) collective-permute-start(bf16[2,24,512]{2,1,0:T(8,128)(2,1)S(1)} %dynamic-slice_bitcast_fusion.3), channel_id=1, source_target_pairs={{0,4},{1,5},{2,6},{3,7},{4,0},{5,1},{6,2},{7,3},{8,12},{9,13},{10,... | collective-permute-start | bytes 147464 | tf_op jit(solution)/shard_map/ppermute | solution.py:306
  129.2 4.2 %collective-permute-start.14 = (bf16[2,24,512]{2,1,0:T(8,128)(2,1)S(1)}, bf16[2,24,512]{2,1,0:T(8,128)(2,1)S(1)}, u32[]{:S(2)}, u32[]{:S(2)}) collective-permute-start(bf16[2,24,512]{2,1,0:T(8,128)(2,1)S(1)} %dynamic-slice_bitcast_fusion.2), channel_id=1, source_target_pairs={{0,2},{1,3},{2,0},{3,1},{4,6},{5,7},{6,4},{7,5},{8,10},{9,11},{10,... | collective-permute-start | bytes 147464 | tf_op jit(solution)/shard_map/ppermute | solution.py:306
  131.9 4.8 %collective-permute-start.11 = (bf16[24,512]{1,0:T(8,128)(2,1)S(1)}, bf16[24,512]{1,0:T(8,128)(2,1)S(1)}, u32[]{:S(2)}, u32[]{:S(2)}) collective-permute-start(bf16[24,512]{1,0:T(8,128)(2,1)S(1)} %dynamic-slice_bitcast_fusion.7), channel_id=1, source_target_pairs={{0,8},{1,9},{2,10},{3,11},{4,12},{5,13},{6,14},{7,15},{8,0},{9,1},... | collective-permute-start | bytes 73736 | tf_op jit(solution)/shard_map/ppermute | solution.py:306
  133.5 4.8 %collective-permute-start.15 = (bf16[24,512]{1,0:T(8,128)(2,1)S(1)}, bf16[24,512]{1,0:T(8,128)(2,1)S(1)}, u32[]{:S(2)}, u32[]{:S(2)}) collective-permute-start(bf16[24,512]{1,0:T(8,128)(2,1)S(1)} %dynamic-slice_bitcast_fusion.6), channel_id=1, source_target_pairs={{0,8},{1,9},{2,10},{3,11},{4,12},{5,13},{6,14},{7,15},{8,0},{9,1},... | collective-permute-start | bytes 73736 | tf_op jit(solution)/shard_map/ppermute | solution.py:306
where the time goes:
time: 141 us; the launch traced here: 140 us
  waiting for transfers between devices  50.1 us (36%)
  starting transfers between devices  42.4 us (30%)
  Pallas kernels  22.2 us (16%)
  local copies, waits for them, and re-layouts  16 us (11%)
  other arithmetic  7.16 us (5%)
    ppermute x20, starting transfers between devices, swap(): lax.ppermute(values, 'row', [(i, i ^ 1 << bit) for i in range(owners)])  28 us
    ppermute x20, waiting for transfers between devices, swap(): lax.ppermute(values, 'row', [(i, i ^ 1 << bit) for i in range(owners)])  27.8 us
    all_to_all x1, waiting for transfers between devices, body(): arrived = exchange(outgoing)  22.4 us
    pallas_call x1, Pallas kernels, body(): pl.pallas_call(functools.partial(strip_kernel, plan), out_shape=(shape_of...  17.5 us
    unnamed x48, local copies, waits for them, and re-layouts  12.2 us
    all_to_all x1, starting transfers between devices, body(): arrived = exchange(outgoing)  7.57 us
    all_to_all x1, starting transfers between devices, body(): returned = exchange(back)  6.88 us
  transfers between devices with their start and end apart: 22, of which 12 were waited for; matrix products, arithmetic and copies ran while one was open for 8% of the time, Pallas kernels for 1%

commit v1 on v0

v1 whole, which is shorter than its diff:
```python
import functools

import jax
import jax.numpy as jnp
import numpy as np
from jax import lax
from jax.experimental import pallas as pl
from jax.experimental.pallas import tpu as pltpu
from jax.sharding import PartitionSpec as P

F32 = jnp.float32
BF16 = jnp.bfloat16
FACTORS = (2, 4, 8)
LANES = 128
VMEM = pl.BlockSpec(memory_space=pltpu.VMEM)
SMEM = pl.BlockSpec(memory_space=pltpu.SMEM)
ANY = pl.BlockSpec(memory_space=pl.ANY)
MEBI = 1024 * 1024
LIMIT = 60 * MEBI
ORDERS = ((0, 1), (1, 0))


def round_up(value, multiple):
    return -(-value // multiple) * multiple


class Plan:
    def __init__(self, owners, depth, strip_width, channels, width):
        self.owners, self.depth, self.strip_width = owners, depth, strip_width
        self.channels, self.width = channels, width
        self.rows = [depth * 8 // k for k in FACTORS]
        self.columns = [strip_width // k for k in FACTORS]
        self.coarse = [r * c * owners for r, c in zip(self.rows, self.columns)]
        self.entries, self.counts, self.starts = [], [], []
        at = 0
        for rows, columns in zip(self.rows, self.columns):
            entries = [(r, c) for r in range(rows) for c in range(columns + 2)]
            entries += [None] * (-len(entries) % 8)
            self.entries.append(entries)
            self.counts.append(len(entries))
            self.starts.append(at)
            at += len(entries)
        self.per_owner = round_up(at, 16)
        self.out_at, self.back_at = [], []
        self.sent = self.returned = 0
        for section in range(3):
            self.out_at.append(self.sent)
            self.back_at.append(self.returned)
            self.sent += self.counts[section] * (channels[section] // LANES)
            self.returned += self.counts[section] * (self.back_width(section) // LANES)

    def back_width(self, section):
        return self.channels[0] if section == 0 else self.width


def axis_weights(fine_count, factor):
    matrix = np.zeros((fine_count, fine_count // factor + 2), np.float32)
    for fine in range(fine_count):
        base, phase = divmod(fine, factor)
        offset = (phase + 0.5) / factor - 0.5
        if offset < 0:
            matrix[fine, base] += -offset
            matrix[fine, base + 1] += 1.0 + offset
        else:
            matrix[fine, base + 1] += 1.0 - offset
            matrix[fine, base + 2] += offset
    return matrix


def clamp_rows(matrix):
    folded = matrix[:, 1:-1].copy()
    folded[:, 0] += matrix[:, 0]
    folded[:, -1] += matrix[:, -1]
    return folded


def window_matrices(plan):
    owners, strip_width = plan.owners, plan.strip_width
    block_rows = plan.depth * 8
    fine_rows = owners * block_rows
    whole = np.zeros((fine_rows, strip_width, owners, plan.per_owner), np.float32)
    row_mats = [clamp_rows(axis_weights(fine_rows, k)) for k in FACTORS]
    col_mats = [axis_weights(strip_width, k) for k in FACTORS]
    for owner in range(owners):
        for section in range(3):
            for index, entry in enumerate(plan.entries[section]):
                if entry is not None:
                    at = owner * plan.rows[section] + entry[0]
                    whole[:, :, owner, plan.starts[section] + index] = np.outer(
                        row_mats[section][:, at], col_mats[section][:, entry[1]]
                    )
    up, down = [], []
    for owner in (0, 1, owners - 1):
        start = min(max(owner - 1, 0), owners - 3)
        rows = slice(owner * block_rows, (owner + 1) * block_rows)
        up.append(
            whole[rows, :, start : start + 3].reshape(block_rows * strip_width, 3 * plan.per_owner)
        )
        window = block_rows + 8
        low = min(max(owner * block_rows - 4, 0), fine_rows - window)
        piece = whole[low : low + window, :, owner]
        down.append(piece.reshape(window * strip_width, plan.per_owner).T)
    return np.stack(up).astype(BF16), np.stack(down).astype(BF16)


def entry_tables(plan, section):
    entries, columns = plan.entries[section], plan.columns[section]
    start = [-(1 << 20) if e is None else e[0] * columns * plan.owners for e in entries]
    offset = [0 if e is None else e[1] - 1 for e in entries]
    return np.array(start, np.int32), np.array(offset, np.int32)


def fold_matrix(strip_map, plan, section):
    start, offset = entry_tables(plan, section)
    columns = plan.columns[section]
    column = jnp.clip(strip_map[:, None] * columns + offset, 0, plan.owners * columns - 1)
    target = (column + start).reshape(-1)
    places = np.arange(plan.coarse[section], dtype=np.int32)
    return (places[:, None] == target[None]).astype(BF16)


def contract(left, right, left_dim, right_dim):
    return lax.dot_general(
        left, right, (((left_dim,), (right_dim,)), ((), ())), preferred_element_type=F32
    )


def put_pieces(ref, at, values, count):
    owners = ref.shape[0]
    for piece in range(values.shape[1] // LANES):
        part = values[:, piece * LANES : (piece + 1) * LANES]
        ref[:, at + piece * count : at + (piece + 1) * count, :] = part.reshape(owners, count, LANES)


def take_pieces(ref, at, pieces, count):
    owners = ref.shape[0]
    return jnp.concatenate(
        [
            ref[:, at + p * count : at + (p + 1) * count, :].reshape(owners * count, LANES)
            for p in range(pieces)
        ],
        axis=1,
    )


def copies_in(pairs, sem_ref):
    copies = [pltpu.make_async_copy(src, dst, sem_ref.at[i]) for i, (src, dst) in enumerate(pairs)]
    for copy in copies:
        copy.start()
    return copies


def entry_vectors(plan, section, shape):
    entry = lax.broadcasted_iota(jnp.int32, shape, 0)
    columns = plan.columns[section]
    span = columns + 2
    scale = -(-65536 // span)
    assert all((q * scale) >> 16 == q // span for q in range(shape[0]))
    row = (entry * scale) >> 16
    start = jnp.where(row < plan.rows[section], row * (columns * plan.owners), -(1 << 20))
    return start, entry - row * span - 1


def pack_kernel(plan, map_ref, *refs):
    sources, out_ref = refs[:3], refs[3]
    held, picks, sem_ref = refs[4:7], refs[7:10], refs[10]
    copies = copies_in(list(zip(sources, held)), sem_ref)
    for section in range(3):
        columns, count, places = plan.columns[section], plan.counts[section], plan.coarse[section]
        start, offset = entry_vectors(plan, section, (count, min(LANES, places)))
        lane = lax.broadcasted_iota(jnp.int32, start.shape, 1) - start
        for device in range(plan.owners):
            column = jnp.clip(map_ref[device] * columns + offset, 0, plan.owners * columns - 1)
            ahead = lane - column
            for at in range(0, places, LANES):
                picks[section][device, :, at : at + LANES] = jnp.where(ahead == -at, 1.0, 0.0).astype(BF16)
    for section in range(3):
        count = plan.counts[section]
        pick = picks[section][...].reshape(plan.owners * count, plan.coarse[section])
        copies[section].wait()
        chosen = contract(pick, held[section][...], 1, 0).astype(BF16)
        put_pieces(out_ref, plan.out_at[section], chosen, count)


def put_parts(part_refs, even_refs, odd_refs):
    owners = 2 * even_refs[0].shape[0]
    for owner in range(owners):
        refs = (even_refs, odd_refs)[owner % 2]
        index, at = 0, 0
        for part_ref in part_refs:
            height = part_ref.shape[0] // owners
            done = 0
            while done < height:
                if at == refs[index].shape[1]:
                    index, at = index + 1, 0
                count = min(height - done, refs[index].shape[1] - at)
                first = owner * height + done
                refs[index][owner // 2, at : at + count, :] = part_ref[first : first + count, :].astype(BF16)
                done += count
                at += count
        if at < refs[index].shape[1]:
            fill = jnp.zeros((refs[index].shape[1] - at, refs[index].shape[2]), BF16)
            refs[index][owner // 2, at:, :] = fill


def ahead_kernel(*refs):
    sources, outs = refs[:4], refs[4:6]
    held, stage, in_sem, out_sem = refs[6:10], refs[10:12], refs[12], refs[13]
    l1_ref, fine_ref, join_ref, cot_ref = held
    copies = copies_in(list(zip(sources, held)), in_sem)
    copies[0].wait()
    copies[1].wait()
    stage[0][...] = contract(fine_ref[...], l1_ref[...], 1, 0)
    first = pltpu.make_async_copy(stage[0], outs[0], out_sem.at[0])
    first.start()
    copies[2].wait()
    copies[3].wait()
    stage[1][...] = contract(cot_ref[...], join_ref[...], 1, 1)
    second = pltpu.make_async_copy(stage[1], outs[1], out_sem.at[1])
    second.start()
    first.wait()
    second.wait()


def strip_kernel(plan, turns, chains, core_ref, *refs):
    sent = 2 + 2 * chains
    sources, outs, held = refs[:11], refs[11 : 11 + sent], refs[11 + sent : 22 + sent]
    stage, refs = refs[22 + sent : 22 + 2 * sent], refs[22 + 2 * sent :]
    arrived_ref, l2_ref, l3_ref, l4_ref, up_ref, down_ref = held[:6]
    straight_ref, hidden_grad_ref, cot_ref, fine_ref, l1_ref = held[6:]
    grad_fine_ref, back_ref = stage[:2]
    coarse_ref, hidden_ref, joined_grad_ref = refs[:3]
    grad_refs, join_part_ref, one_part_ref = refs[3:6], refs[6], refs[7]
    part_refs, sem_ref, in_sem, turn_sem = refs[8:11], refs[11], refs[12], refs[13]
    lateral_refs = (l2_ref, l3_ref, l4_ref)
    owners, per_owner, width = plan.owners, plan.per_owner, plan.width
    core = core_ref[0]
    block = up_ref.shape[1]
    reach = up_ref.shape[2]
    window = down_ref.shape[2]
    total = cot_ref.shape[0]
    group = owners // turns
    copies = copies_in(list(zip(sources[:6], held[:6])), in_sem)
    turn_copies = []
    for turn in range(turns):
        many = pl.ds(turn * group * block, group * block)
        for which in (0, 1):
            copy = pltpu.make_async_copy(
                sources[6 + which].at[many], held[6 + which].at[many], turn_sem.at[which, turn]
            )
            copy.start()
            turn_copies.append(copy)
    late_copies = []
    for index in (8, 9, 10):
        copy = pltpu.make_async_copy(sources[index], held[index], in_sem.at[index - 2])
        copy.start()
        late_copies.append(copy)

    def leave(index):
        copy = pltpu.make_async_copy(stage[index], outs[index], sem_ref.at[index])
        copy.start()
        return copy

    def features(section):
        return take_pieces(
            arrived_ref, plan.out_at[section], plan.channels[section] // LANES, plan.counts[section]
        )

    copies[0].wait()
    projected = []
    for section in range(3):
        copies[1 + section].wait()
        product = contract(features(section), lateral_refs[section][...], 1, 0).astype(BF16)
        projected.append(product.reshape(owners, plan.counts[section], width))
    tail = per_owner - sum(plan.counts)
    if tail:
        projected.append(jnp.zeros((owners, tail, width), BF16))
    coarse_ref[...] = jnp.concatenate(projected, axis=1).reshape(owners * per_owner, width)
    copies[4].wait()
    copies[5].wait()

    for turn in range(turns):
        turn_copies[2 * turn].wait()
        turn_copies[2 * turn + 1].wait()
        for owner in range(turn * group, (turn + 1) * group):
            kind = 0 if owner == 0 else 2 if owner == owners - 1 else 1
            start = min(max(owner - 1, 0), owners - 3) * per_owner
            rows = slice(owner * block, (owner + 1) * block)
            joined = straight_ref[rows, :] + contract(
                up_ref[kind], coarse_ref[start : start + reach, :], 1, 0
            )
            gate = 0.5 + 0.5 * jnp.tanh(0.5 * joined)
            hidden = joined * gate
            hidden_ref[rows, :] = hidden.astype(BF16)
            slope = gate + hidden * (1.0 - gate)
            joined_grad_ref[rows, :] = (hidden_grad_ref[rows, :] * slope).astype(BF16)

    for owner in range(owners):
        kind = 0 if owner == 0 else 2 if owner == owners - 1 else 1
        low = min(max(owner * block - 32, 0), total - window)
        strip_grad = contract(down_ref[kind], joined_grad_ref[low : low + window, :], 1, 0).astype(BF16)
        for section in range(3):
            at = plan.starts[section]
            grad_refs[section][owner] = strip_grad[at : at + plan.counts[section]]

    strip_grads = [
        ref[...].reshape(owners * count, width) for ref, count in zip(grad_refs, plan.counts)
    ]
    put_pieces(back_ref, 0, contract(strip_grads[0], l2_ref[...], 1, 1).astype(BF16), plan.counts[0])
    for section in (1, 2):
        put_pieces(back_ref, plan.back_at[section], strip_grads[section], plan.counts[section])
    leaving = [leave(1)]
    for section in range(3):
        part_refs[section][...] = contract(features(section), strip_grads[section], 0, 0)
    for copy in late_copies:
        copy.wait()
    join_part_ref[...] = contract(cot_ref[...], hidden_ref[...], 0, 0)
    one_part_ref[...] = contract(fine_ref[...], joined_grad_ref[...], 0, 0)

    kept, given = stage[2 : 2 + chains], stage[2 + chains :]
    ordered_parts = (join_part_ref, *part_refs, one_part_ref)

    @pl.when(core == 0)
    def _():
        put_parts(ordered_parts, kept, given)

    @pl.when(core != 0)
    def _():
        put_parts(ordered_parts, given, kept)

    leaving += [leave(index) for index in range(2, len(stage))]
    grad_fine_ref[...] = contract(joined_grad_ref[...], l1_ref[...], 1, 1).astype(BF16)
    leaving.append(leave(0))
    for copy in leaving:
        copy.wait()


def section_kernel(plan, *refs):
    sources, outs, held, sem_ref = refs[:6], refs[6:9], refs[9:15], refs[15]
    copies = copies_in(list(zip(sources, held)), sem_ref)
    returned_ref, folds, laterals = held[0], held[1:4], held[4:6]
    copies[0].wait()
    for section in range(3):
        arrived = take_pieces(
            returned_ref, plan.back_at[section], plan.back_width(section) // LANES, plan.counts[section]
        )
        copies[1 + section].wait()
        folded = contract(folds[section][...], arrived, 1, 0).astype(BF16)
        if section > 0:
            copies[3 + section].wait()
            folded = contract(folded, laterals[section - 1][...], 1, 1).astype(BF16)
        outs[section][...] = folded


def swap(values, bit):
    owners = lax.axis_size("row")
    return lax.ppermute(values, "row", [(i, i ^ (1 << bit)) for i in range(owners)])


def plus(left, right):
    return (left.astype(F32) + right.astype(F32)).astype(BF16)


class Halving:
    def __init__(self, values, order):
        bits = len(order)
        self.values = values.reshape((2,) * bits + values.shape[1:])
        self.left = sorted(order, reverse=True)
        self.order = list(order)

    def step(self):
        bit = self.order.pop(0)
        axis = self.left.index(bit)
        self.left.pop(axis)
        mine = (lax.axis_index("row") >> bit) & 1
        keep = lax.dynamic_index_in_dim(self.values, mine, axis, keepdims=False)
        give = lax.dynamic_index_in_dim(self.values, 1 - mine, axis, keepdims=False)
        self.values = plus(keep, swap(give, bit))


def reduce_chains(kept, given, bits):
    chains = []
    for keep, give, order in zip(kept, given, ORDERS):
        rest = list(range(1, bits))
        rest[: len(order)] = [rest[i] for i in order]
        chains.append(Halving(plus(keep, swap(give, 0)), rest))
    for _ in range(1, bits):
        for chain in chains:
            chain.step()
    return [chain.values for chain in chains]


def shape_of(*dims, dtype=BF16):
    return jax.ShapeDtypeStruct(dims, dtype)


def body(
    fine_features,
    section_two,
    section_three,
    section_four,
    strip_map,
    lateral_one,
    lateral_two,
    lateral_three,
    lateral_four,
    join_weight,
    cotangent,
):
    owners = lax.axis_size("row")
    bits = owners.bit_length() - 1
    fine_height, strip_width, c1 = fine_features.shape
    width = join_weight.shape[0]
    sections = (section_two, section_three, section_four)
    channels = [s.shape[-1] for s in sections]
    plan = Plan(owners, section_four.shape[0], strip_width, channels, width)
    flats = [s.reshape(-1, s.shape[-1]) for s in sections]
    fine = fine_features.reshape(-1, c1)
    cot = cotangent.reshape(-1, width)
    total = fine.shape[0]
    me = lax.axis_index("row")
    core = (me & 1).astype(jnp.int32).reshape(1)
    up, down = window_matrices(plan)
    exchange = functools.partial(lax.all_to_all, axis_name="row", split_axis=0, concat_axis=0, tiled=True)

    outgoing = pl.pallas_call(
        functools.partial(pack_kernel, plan),
        out_shape=shape_of(owners, plan.sent, LANES),
        in_specs=[SMEM] + [ANY] * 3,
        out_specs=VMEM,
        scratch_shapes=[pltpu.VMEM(f.shape, BF16) for f in flats]
        + [pltpu.VMEM((owners, count, places), BF16) for count, places in zip(plan.counts, plan.coarse)]
        + [pltpu.SemaphoreType.DMA((3,))],
        compiler_params=pltpu.CompilerParams(vmem_limit_bytes=LIMIT),
        name="pack",
    )(strip_map, *flats)
    arrived = exchange(outgoing)

    half = owners // 2
    heights = [x // owners for x in (width, *channels, c1)]
    chains = len(ORDERS)
    tall = round_up(sum(heights), 8)
    cuts = [round_up(tall * c // chains, 8) for c in range(chains)] + [tall]
    chain_heights = [high - low for low, high in zip(cuts, cuts[1:])]
    early = (lateral_one, fine, join_weight, cot)
    straight, hidden_grad = pl.pallas_call(
        ahead_kernel,
        out_shape=(shape_of(total, width, dtype=F32),) * 2,
        in_specs=[ANY] * 4,
        out_specs=(ANY,) * 2,
        scratch_shapes=[pltpu.VMEM(x.shape, BF16) for x in early]
        + [pltpu.VMEM((total, width), F32)] * 2
        + [pltpu.SemaphoreType.DMA((4,)), pltpu.SemaphoreType.DMA((2,))],
        compiler_params=pltpu.CompilerParams(vmem_limit_bytes=LIMIT),
        cost_estimate=pl.CostEstimate(
            flops=4 * total * width * (width + c1), bytes_accessed=14_000_000, transcendentals=0
        ),
        name="ahead",
    )(*early)
    operands = (
        arrived,
        lateral_two,
        lateral_three,
        lateral_four,
        up,
        down,
        straight,
        hidden_grad,
        cot,
        fine,
        lateral_one,
    )
    stage = (shape_of(total, c1), shape_of(owners, plan.returned, LANES))
    stage += tuple(shape_of(half, height, width) for height in chain_heights) * 2
    grad_fine, back, *halves = pl.pallas_call(
        functools.partial(strip_kernel, plan, 4, chains),
        out_shape=stage,
        in_specs=[SMEM] + [ANY] * 11,
        out_specs=(ANY,) * len(stage),
        scratch_shapes=[pltpu.VMEM(x.shape, x.dtype) for x in operands + stage]
        + [
            pltpu.VMEM((owners * plan.per_owner, width), BF16),
            pltpu.VMEM((total, width), BF16),
            pltpu.VMEM((total, width), BF16),
        ]
        + [pltpu.VMEM((owners, count, width), BF16) for count in plan.counts]
        + [pltpu.VMEM((x, width), F32) for x in (width, c1, *channels)]
        + [
            pltpu.SemaphoreType.DMA((len(stage),)),
            pltpu.SemaphoreType.DMA((9,)),
            pltpu.SemaphoreType.DMA((2, 4)),
        ],
        compiler_params=pltpu.CompilerParams(vmem_limit_bytes=LIMIT),
        cost_estimate=pl.CostEstimate(
            flops=4_000_000_000, bytes_accessed=9_000_000, transcendentals=total * width
        ),
        name="strip_work",
    )(core, *operands)

    returned = exchange(back)
    summed = reduce_chains(halves[:chains], halves[chains:], bits)
    summed = jnp.concatenate(summed, axis=0).astype(F32)
    ends = np.cumsum([0] + heights).tolist()
    weight_grads = [summed[low:high] for low, high in zip(ends, ends[1:])]

    operands = (
        returned,
        *[fold_matrix(strip_map, plan, section) for section in range(3)],
        lateral_three,
        lateral_four,
    )
    grads = pl.pallas_call(
        functools.partial(section_kernel, plan),
        out_shape=tuple(shape_of(*f.shape) for f in flats),
        in_specs=[ANY] * 6,
        out_specs=(VMEM,) * 3,
        scratch_shapes=[pltpu.VMEM(x.shape, BF16) for x in operands] + [pltpu.SemaphoreType.DMA((6,))],
        compiler_params=pltpu.CompilerParams(vmem_limit_bytes=LIMIT),
        cost_estimate=pl.CostEstimate(flops=500_000_000, bytes_accessed=6_000_000, transcendentals=0),
        name="section_grads",
    )(*operands)

    return (
        grad_fine.reshape(fine_features.shape),
        *[g.reshape(s.shape) for g, s in zip(grads, sections)],
        weight_grads[0].T,
        weight_grads[4],
        *weight_grads[1:4],
    )


def solution(mesh):
    fine_spec = P(None, ("group", "row"), None)
    coarse_spec = P("row", "group", None)
    weight_spec = P(("group", "row"), None)
    return jax.shard_map(
        body,
        mesh=mesh,
        in_specs=(fine_spec,) + (coarse_spec,) * 3 + (P("group"),) + (P(),) * 5 + (fine_spec,),
        out_specs=(fine_spec,) + (coarse_spec,) * 3 + (P("group", "row"),) + (weight_spec,) * 4,
        check_vma=False,
    )
```

time: 141 us -> 115 us (0.82)
  starting transfers between devices: 42.4 us -> 28.5 us
  local copies, waits for them, and re-layouts: 16 us -> 6.87 us
  waiting for transfers between devices: 50.1 us -> 42.1 us
  Pallas kernels: 22.2 us -> 26 us
  other arithmetic: 7.16 us -> 9.85 us
    ppermute x20 -> x8, starting transfers between devices: 28 us -> 16.8 us  [swap(): lax.ppermute(values, 'row', [(i, i ^ 1 << bit) for i in range(owners)])]
    ppermute x20 -> x8, waiting for transfers between devices: 27.8 us -> 21 us  [swap(): lax.ppermute(values, 'row', [(i, i ^ 1 << bit) for i in range(owners)])]
    unnamed x48 -> x26, local copies, waits for them, and re-layouts: 12.2 us -> 5.57 us
    all_to_all x1, starting transfers between devices: 6.88 us -> 4.11 us  [body(): returned = exchange(back)]
    convert_element_type x14 -> x8, other arithmetic: 1.44 us -> 4.08 us  [plus(): return (left.astype(F32) + right.astype(F32)).astype(BF16)]
    pallas_call x1, Pallas kernels: 1.86 us -> 4.1 us  [body(): pl.pallas_call(functools.partial(section_kernel, plan), out_shape=tuple((...]
    slice x3 -> x0, local copies, waits for them, and re-layouts: 2.16 us -> none  [the longest x1 0.91 us: body(): arrived[:, plan.slice_at:plan.slice_at + plan.coarse[2], :plan.slice_width]]
    slice x0 -> x3, other arithmetic: none -> 1.89 us  [body(): weight_grads = [summed[low:high] for low, high in zip(ends, ends[1:])]]
  transfers between devices with their start and end apart: 22 -> 10, of which waited for: 12 -> 8; matrix products, arithmetic and copies ran while one was open for 8% -> 13% of each run, Pallas kernels for 1% -> 5%
where the time goes in v1:
time: 115 us; the launch traced here: 114 us
  waiting for transfers between devices  42.1 us (37%)
  starting transfers between devices  28.5 us (25%)
  Pallas kernels  26 us (23%)
  other arithmetic  9.85 us (9%)
  local copies, waits for them, and re-layouts  6.87 us (6%)
    all_to_all x1, waiting for transfers between devices, body(): arrived = exchange(outgoing)  21.1 us
    ppermute x8, waiting for transfers between devices, swap(): lax.ppermute(values, 'row', [(i, i ^ 1 << bit) for i in range(owners)])  21 us
    ppermute x8, starting transfers between devices, swap(): lax.ppermute(values, 'row', [(i, i ^ 1 << bit) for i in range(owners)])  16.8 us
    pallas_call x1, Pallas kernels, body(): pl.pallas_call(functools.partial(strip_kernel, plan, 4, chains), out_shap...  12.4 us
    all_to_all x1, starting transfers between devices, body(): arrived = exchange(outgoing)  7.53 us
    unnamed x26, local copies, waits for them, and re-layouts  5.57 us
    pallas_call x1, Pallas kernels, body(): pl.pallas_call(ahead_kernel, out_shape=(shape_of(total, width, dtype=F32)...  5.54 us
    all_to_all x1, starting transfers between devices, body(): returned = exchange(back)  4.11 us
  transfers between devices with their start and end apart: 10, of which 8 were waited for; matrix products, arithmetic and copies ran while one was open for 13% of the time, Pallas kernels for 5%

profile of v1, /device:TPU:0, one launch (start us, length us, event | category | flops | bytes accessed | tf_op | source)
XLA Modules:
  0.0 114.4 jit_solution(2567922906419238267)
XLA Ops:
  0.6 4.0 %pack.1 = bf16[16,336,128]{2,1,0:T(8,128)(2,1)} custom-call(s32[16]{0:T(128)} %map_ref.1, bf16[512,384]{1,0:T(8,128)(2,1)} %bitcast.58, bf16[128,768]{1,0:T(8,128)(2,1)} %bitcast.59, bf16[32,1536]{1,0:T(8,128)(2,1)} %bitcast.60), custom_call_target="tpu_custom_call" | custom-call | tf_op jit(solution)/shard_map/pack/pallas_call | solution.py:426
  4.6 0.0 copy-start.4
  4.6 0.0 copy-start.5
  4.6 0.0 copy-start.10
  4.6 0.0 copy-start.11
  4.7 7.5 %all-to-all-start = ((bf16[16,336,128]{2,1,0:T(8,128)(2,1)}), bf16[16,336,128]{2,1,0:T(8,128)(2,1)S(1)}, u32[]{:S(2)}, u32[]{:S(2)}) async-start(bf16[16,336,128]{2,1,0:T(8,128)(2,1)} %pack.1), calls=%async_computation | async-start | bytes 2752512 | tf_op jit(solution)/shard_map/all_to_all | solution.py:437
  12.2 0.0 copy-done.4
  12.2 1.8 %copy.37 = bf16[256,8,192]{2,1,0:T(8,128)(2,1)} copy(bf16[256,8,192]{0,2,1:T(8,128)(2,1)S(1)} %copy-done.4) | data formatting | bytes 1572864 | tf_op args[0]
  14.0 0.0 copy-done.5
  14.0 0.0 copy-done.10
  14.0 0.0 copy-done.11
  14.0 0.1 clamp_add_fusion
  14.1 5.5 %ahead.1 = (f32[2048,512]{1,0:T(8,128)}, f32[2048,512]{1,0:T(8,128)}) custom-call(bf16[192,512]{1,0:T(8,128)(2,1)} %refs_10_.1, bf16[2048,192]{1,0:T(8,128)(2,1)} %bitcast.50, bf16[512,512]{1,0:T(8,128)(2,1)} %refs_2_.2, bf16[2048,512]{1,0:T(8,128)(2,1)} %bitcast.54), custom_call_target="tpu_custom_call" | custom-call | flops 2952790016 | bytes 14000000 | tf_op jit(solution)/shard_map/ahead/pallas_call | solution.py:446
  19.6 21.1 %all-to-all-done.refs_0_ = bf16[16,336,128]{2,1,0:T(8,128)(2,1)S(1)} async-done(((bf16[16,336,128]{2,1,0:T(8,128)(2,1)}), bf16[16,336,128]{2,1,0:T(8,128)(2,1)S(1)}, u32[]{:S(2)}, u32[]{:S(2)}) %all-to-all-start) | async-done | bytes 1376288 | tf_op jit(solution)/shard_map/all_to_all | solution.py:437
  40.8 1.1 copy-done
  41.9 12.4 %strip_work.1 = (bf16[2048,192]{1,0:T(8,128)(2,1)}, bf16[16,240,128]{2,1,0:T(8,128)(2,1)}, bf16[8,112,512]{2,1,0:T(8,128)(2,1)}, bf16[8,104,512]{2,1,0:T(8,128)(...) custom-call(s32[1]{0:T(128)} %bitcast.core_ref, bf16[16,336,128]{2,1,0:T(8,128)(2,1)} %copy-done, ...), custom_call_target="tpu_custom_call" | custom-call | flops 4000000000 | bytes 9000000 | tf_op jit(solution)/shard_map/strip_work/pallas_call | solution.py:475
  54.3 0.9 collective-permute-start.4
  55.2 0.0 copy-done.8
  55.2 0.0 copy-done.9
  55.2 0.1 clamp_add_fusion.2
  55.3 0.0 collective-permute-start
  55.3 0.0 copy-done.6
  55.4 0.1 clamp_add_fusion.1
  55.4 0.1 add.161
  55.5 0.1 add.167
  55.6 0.1 add.173
  55.7 0.6 fusion.7.refs_2_
  56.3 1.1 fusion.refs_1_
  57.4 0.1 collective-permute-done.4
  57.4 1.4 %add_convert_fusion.1 = bf16[8,104,512]{2,1,0:T(8,128)(2,1)S(1)} fusion(bf16[8,104,512]{2,1,0:T(8,128)(2,1)S(1)} %collective-permute-done.4, bf16[8,104,512]{2,1,0:T(8,128)(2,1)} %get-tuple-element.29), kind=kLoop, calls=%fused_computation.1 | loop fusion | flops 1703936 | bytes 2555904 | tf_op jit(solution)/shard_map/convert_element_type | solution.py:361
  58.8 0.1 constant_dynamic-slice_fusion.1
  58.9 0.8 copy.54
  59.7 4.2 %collective-permute-start.5 = (bf16[2,2,104,512]{3,2,0,1:T(8,128)(2,1)}, bf16[2,2,104,512]{3,2,0,1:T(8,128)(2,1)}, u32[]{:S(2)}, u32[]{:S(2)}) collective-permute-start(bf16[2,2,104,512]{3,2,0,1:T(8,128)(2,1)} %bitcast.49), channel_id=1, source_target_pairs={{0,4},{1,5},{2,6},{3,7},{4,0},{5,1},{6,2},{7,3},{8,12},{9,13},{10,... | collective-permute-start | bytes 1277960 | tf_op jit(solution)/shard_map/ppermute | solution.py:357
  63.9 0.0 collective-permute-done
  63.9 0.0 copy-done.3
  63.9 0.3 add_convert_fusion
  64.2 0.1 constant_dynamic-slice_fusion.3
  64.3 2.2 %collective-permute-start.1 = (bf16[2,2,112,512]{3,2,0,1:T(8,128)(2,1)S(1)}, bf16[2,2,112,512]{3,2,0,1:T(8,128)(2,1)}, u32[]{:S(2)}, u32[]{:S(2)}) collective-permute-start(bf16[2,2,112,512]{3,2,0,1:T(8,128)(2,1)S(1)} %bitcast.57), channel_id=1, source_target_pairs={{0,2},{1,3},{2,0},{3,1},{4,6},{5,7},{6,4},{7,5},{8,10},{9,11},{10,... | collective-permute-start | bytes 1376264 | tf_op jit(solution)/shard_map/ppermute | solution.py:357
  66.5 0.6 fusion.9.refs_3_
  67.1 4.1 %all-to-all-start.1 = ((bf16[16,240,128]{2,1,0:T(8,128)(2,1)}), bf16[16,240,128]{2,1,0:T(8,128)(2,1)S(1)}, u32[]{:S(2)}, u32[]{:S(2)}) async-start(bf16[16,240,128]{2,1,0:T(8,128)(2,1)} %get-tuple-element.23), calls=%async_computation.1 | async-start | bytes 1966080 | tf_op jit(solution)/shard_map/all_to_all | solution.py:500
  71.2 0.0 copy-done.2
  71.2 1.6 %copy.42 = bf16[256,8,192]{0,2,1:T(8,128)(2,1)} copy(bf16[256,8,192]{2,1,0:T(8,128)(2,1)S(1)} %bitcast.56) | data formatting | bytes 1572864
  72.9 1.9 %collective-permute-done.5 = bf16[2,2,104,512]{3,2,0,1:T(8,128)(2,1)} collective-permute-done((bf16[2,2,104,512]{3,2,0,1:T(8,128)(2,1)}, bf16[2,2,104,512]{3,2,0,1:T(8,128)(2,1)}, u32[]{:S(2)}, u32[]{:S(2)}) %collective-permute-start.5) | collective-permute-done | bytes 426016 | tf_op jit(solution)/shard_map/ppermute | solution.py:357
  74.8 1.1 fusion.2
  75.9 2.2 %collective-permute-start.6 = (bf16[2,104,512]{2,1,0:T(8,128)(2,1)S(1)}, bf16[2,104,512]{2,1,0:T(8,128)(2,1)S(1)}, u32[]{:S(2)}, u32[]{:S(2)}) collective-permute-start(bf16[2,104,512]{2,1,0:T(8,128)(2,1)S(1)} %dynamic-slice_bitcast_fusion.1), channel_id=1, source_target_pairs={{0,2},{1,3},{2,0},{3,1},{4,6},{5,7},{6,4},{7,5},{8,10},{9,11},{10,... | collective-permute-start | bytes 638984 | tf_op jit(solution)/shard_map/ppermute | solution.py:357
  78.1 2.0 %collective-permute-done.1 = bf16[2,2,112,512]{3,2,0,1:T(8,128)(2,1)} collective-permute-done((bf16[2,2,112,512]{3,2,0,1:T(8,128)(2,1)S(1)}, bf16[2,2,112,512]{3,2,0,1:T(8,128)(2,1)}, u32[]{:S(2)}, u32[]{:S(2)}) %collective-permute-start.1) | collective-permute-done | bytes 458784 | tf_op jit(solution)/shard_map/ppermute | solution.py:357
  80.2 1.1 fusion.1
  81.3 0.1 collective-permute-start.2
  81.4 8.8 %collective-permute-done.6 = bf16[2,104,512]{2,1,0:T(8,128)(2,1)S(1)} collective-permute-done((bf16[2,104,512]{2,1,0:T(8,128)(2,1)S(1)}, bf16[2,104,512]{2,1,0:T(8,128)(2,1)S(1)}, u32[]{:S(2)}, u32[]{:S(2)}) %collective-permute-start.6) | collective-permute-done | bytes 213024 | tf_op jit(solution)/shard_map/ppermute | solution.py:357
  90.2 0.1 fusion.4
  90.3 2.9 %collective-permute-start.7 = (bf16[104,512]{1,0:T(8,128)(2,1)S(1)}, bf16[104,512]{1,0:T(8,128)(2,1)S(1)}, u32[]{:S(2)}, u32[]{:S(2)}) collective-permute-start(bf16[104,512]{1,0:T(8,128)(2,1)S(1)} %dynamic-slice_bitcast_fusion.3), channel_id=1, source_target_pairs={{0,8},{1,9},{2,10},{3,11},{4,12},{5,13},{6,14},{7,15},{8,0},{9,1},... | collective-permute-start | bytes 319496 | tf_op jit(solution)/shard_map/ppermute | solution.py:357
  93.2 2.1 %collective-permute-done.2 = bf16[2,112,512]{2,1,0:T(8,128)(2,1)S(1)} collective-permute-done((bf16[2,112,512]{2,1,0:T(8,128)(2,1)S(1)}, bf16[2,112,512]{2,1,0:T(8,128)(2,1)S(1)}, u32[]{:S(2)}, u32[]{:S(2)}) %collective-permute-start.2) | collective-permute-done | bytes 229408 | tf_op jit(solution)/shard_map/ppermute | solution.py:357
  95.2 0.1 fusion.3
  95.3 4.3 %collective-permute-start.3 = (bf16[112,512]{1,0:T(8,128)(2,1)S(1)}, bf16[112,512]{1,0:T(8,128)(2,1)S(1)}, u32[]{:S(2)}, u32[]{:S(2)}) collective-permute-start(bf16[112,512]{1,0:T(8,128)(2,1)S(1)} %dynamic-slice_bitcast_fusion.2), channel_id=1, source_target_pairs={{0,8},{1,9},{2,10},{3,11},{4,12},{5,13},{6,14},{7,15},{8,0},{9,1},... | collective-permute-start | bytes 344072 | tf_op jit(solution)/shard_map/ppermute | solution.py:357
  99.7 4.2 %collective-permute-done.7 = bf16[104,512]{1,0:T(8,128)(2,1)S(1)} collective-permute-done((bf16[104,512]{1,0:T(8,128)(2,1)S(1)}, bf16[104,512]{1,0:T(8,128)(2,1)S(1)}, u32[]{:S(2)}, u32[]{:S(2)}) %collective-permute-start.7) | collective-permute-done | bytes 106528 | tf_op jit(solution)/shard_map/ppermute | solution.py:357
  103.9 2.0 %collective-permute-done.3 = bf16[112,512]{1,0:T(8,128)(2,1)S(1)} collective-permute-done((bf16[112,512]{1,0:T(8,128)(2,1)S(1)}, bf16[112,512]{1,0:T(8,128)(2,1)S(1)}, u32[]{:S(2)}, u32[]{:S(2)}) %collective-permute-start.3) | collective-permute-done | bytes 114720 | tf_op jit(solution)/shard_map/ppermute | solution.py:357
  105.9 0.6 maximum_convert_fusion.2
  106.5 0.6 maximum_convert_fusion.1
  107.2 0.6 convert_bitcast_fusion
  107.8 0.6 maximum_convert_fusion
  108.4 0.7 fusion.8
  109.1 0.0 all-to-all-done.1.refs_0_
  109.1 1.0 copy-done.1
  110.1 4.1 %section_grads.1 = (bf16[512,384]{1,0:T(8,128)(2,1)}, bf16[128,768]{1,0:T(8,128)(2,1)}, bf16[32,1536]{1,0:T(8,128)(2,1)}) custom-call(bf16[16,240,128]{2,1,0:T(8,128)(2,1)} %copy-done.1, bf16[512,768]{1,0:T(8,128)(2,1)} %fusion.refs_1_, bf16[128,256]{1,0:T(8,128)(2,1)} %fusion.7.refs_2_, bf16[32,128]{1,0:T(8,128)(2,1)} %fusion.9.refs_3_, ...), custom_call_target="tpu_custom_call" | custom-call | flops 500000000 | bytes 6000000 | tf_op jit(solution)/shard_map/section_grads/pallas_call | solution.py:512
  (17 shorter events, 0.2 us)
Async XLA Ops:
  4.6 7.6 %copy-start.4 = (bf16[256,8,192]{0,2,1:T(8,128)(2,1)S(1)}, bf16[256,8,192]{0,2,1:T(8,128)(2,1)}, u32[]{:S(2)}) copy-start(bf16[256,8,192]{0,2,1:T(8,128)(2,1)} %param.22) | copy-start | bytes 2359300
  4.6 9.4 %copy-start.5 = (s32[16]{0:T(128)S(1)}, s32[16]{0:T(128)}, u32[]{:S(2)}) copy-start(s32[16]{0:T(128)} %map_ref.1) | copy-start | bytes 196
  4.6 9.3 %copy-start.10 = (s32[8]{0:T(128)S(1)}, s32[8]{0:T(128)}, u32[]{:S(2)}) copy-start(s32[8]{0:T(128)} %constant.90.clone) | copy-start | bytes 100
  4.6 9.3 %copy-start.11 = (s32[8]{0:T(128)S(1)}, s32[8]{0:T(128)}, u32[]{:S(2)}) copy-start(s32[8]{0:T(128)} %constant.91.clone) | copy-start | bytes 100
  4.7 36.1 %all-to-all-start = ((bf16[16,336,128]{2,1,0:T(8,128)(2,1)}), bf16[16,336,128]{2,1,0:T(8,128)(2,1)S(1)}, u32[]{:S(2)}, u32[]{:S(2)}) async-start(bf16[16,336,128]{2,1,0:T(8,128)(2,1)} %pack.1), calls=%async_computation | async-start | bytes 2752512 | tf_op jit(solution)/shard_map/all_to_all | solution.py:437
  40.8 1.1 copy-start
  41.9 13.3 %copy-start.8 = (s32[48]{0:T(128)S(1)}, s32[48]{0:T(128)}, u32[]{:S(2)}) copy-start(s32[48]{0:T(128)} %constant.84.clone) | copy-start | bytes 580
  41.9 13.3 %copy-start.9 = (s32[48]{0:T(128)S(1)}, s32[48]{0:T(128)}, u32[]{:S(2)}) copy-start(s32[48]{0:T(128)} %constant.85.clone) | copy-start | bytes 580
  41.9 13.4 %copy-start.6 = (s32[16]{0:T(128)S(1)}, s32[16]{0:T(128)}, u32[]{:S(2)}) copy-start(s32[16]{0:T(128)} %constant.87.clone) | copy-start | bytes 196
  41.9 13.4 %copy-start.7 = (s32[16]{0:T(128)S(1)}, s32[16]{0:T(128)}, u32[]{:S(2)}) copy-start(s32[16]{0:T(128)} %constant.88.clone) | copy-start | bytes 196
  54.3 3.1 %collective-permute-start.4 = (bf16[8,104,512]{2,1,0:T(8,128)(2,1)}, bf16[8,104,512]{2,1,0:T(8,128)(2,1)S(1)}, u32[]{:S(2)}, u32[]{:S(2)}) collective-permute-start(bf16[8,104,512]{2,1,0:T(8,128)(2,1)} %get-tuple-element.30), channel_id=1, source_target_pairs={{0,1},{1,0},{2,3},{3,2},{4,5},{5,4},{6,7},{7,6},{8,9},{9,8},{10,11... | collective-permute-start | bytes 2555912 | tf_op jit(solution)/shard_map/ppermute | solution.py:357
  55.3 8.6 %collective-permute-start = (bf16[8,112,512]{2,1,0:T(8,128)(2,1)}, bf16[8,112,512]{2,1,0:T(8,128)(2,1)S(1)}, u32[]{:S(2)}, u32[]{:S(2)}) collective-permute-start(bf16[8,112,512]{2,1,0:T(8,128)(2,1)} %get-tuple-element.28), channel_id=1, source_target_pairs={{0,1},{1,0},{2,3},{3,2},{4,5},{5,4},{6,7},{7,6},{8,9},{9,8},{10,11... | collective-permute-start | bytes 2752520 | tf_op jit(solution)/shard_map/ppermute | solution.py:357
  58.8 5.1 %copy-start.3 = (bf16[8,112,512]{2,1,0:T(8,128)(2,1)S(1)}, bf16[8,112,512]{2,1,0:T(8,128)(2,1)}, u32[]{:S(2)}) copy-start(bf16[8,112,512]{2,1,0:T(8,128)(2,1)} %get-tuple-element.27) | copy-start | bytes 2752516
  59.7 15.0 %collective-permute-start.5 = (bf16[2,2,104,512]{3,2,0,1:T(8,128)(2,1)}, bf16[2,2,104,512]{3,2,0,1:T(8,128)(2,1)}, u32[]{:S(2)}, u32[]{:S(2)}) collective-permute-start(bf16[2,2,104,512]{3,2,0,1:T(8,128)(2,1)} %bitcast.49), channel_id=1, source_target_pairs={{0,4},{1,5},{2,6},{3,7},{4,0},{5,1},{6,2},{7,3},{8,12},{9,13},{10,... | collective-permute-start | bytes 1277960 | tf_op jit(solution)/shard_map/ppermute | solution.py:357
  64.3 6.9 %copy-start.2 = (bf16[2048,192]{1,0:T(8,128)(2,1)S(1)}, bf16[2048,192]{1,0:T(8,128)(2,1)}, u32[]{:S(2)}) copy-start(bf16[2048,192]{1,0:T(8,128)(2,1)} %get-tuple-element.22) | copy-start | bytes 2359300
  64.3 15.8 %collective-permute-start.1 = (bf16[2,2,112,512]{3,2,0,1:T(8,128)(2,1)S(1)}, bf16[2,2,112,512]{3,2,0,1:T(8,128)(2,1)}, u32[]{:S(2)}, u32[]{:S(2)}) collective-permute-start(bf16[2,2,112,512]{3,2,0,1:T(8,128)(2,1)S(1)} %bitcast.57), channel_id=1, source_target_pairs={{0,2},{1,3},{2,0},{3,1},{4,6},{5,7},{6,4},{7,5},{8,10},{9,11},{10,... | collective-permute-start | bytes 1376264 | tf_op jit(solution)/shard_map/ppermute | solution.py:357
  67.1 42.1 %all-to-all-start.1 = ((bf16[16,240,128]{2,1,0:T(8,128)(2,1)}), bf16[16,240,128]{2,1,0:T(8,128)(2,1)S(1)}, u32[]{:S(2)}, u32[]{:S(2)}) async-start(bf16[16,240,128]{2,1,0:T(8,128)(2,1)} %get-tuple-element.23), calls=%async_computation.1 | async-start | bytes 1966080 | tf_op jit(solution)/shard_map/all_to_all | solution.py:500
  75.9 14.3 %collective-permute-start.6 = (bf16[2,104,512]{2,1,0:T(8,128)(2,1)S(1)}, bf16[2,104,512]{2,1,0:T(8,128)(2,1)S(1)}, u32[]{:S(2)}, u32[]{:S(2)}) collective-permute-start(bf16[2,104,512]{2,1,0:T(8,128)(2,1)S(1)} %dynamic-slice_bitcast_fusion.1), channel_id=1, source_target_pairs={{0,2},{1,3},{2,0},{3,1},{4,6},{5,7},{6,4},{7,5},{8,10},{9,11},{10,... | collective-permute-start | bytes 638984 | tf_op jit(solution)/shard_map/ppermute | solution.py:357
  81.3 13.9 %collective-permute-start.2 = (bf16[2,112,512]{2,1,0:T(8,128)(2,1)S(1)}, bf16[2,112,512]{2,1,0:T(8,128)(2,1)S(1)}, u32[]{:S(2)}, u32[]{:S(2)}) collective-permute-start(bf16[2,112,512]{2,1,0:T(8,128)(2,1)S(1)} %dynamic-slice_bitcast_fusion), channel_id=1, source_target_pairs={{0,4},{1,5},{2,6},{3,7},{4,0},{5,1},{6,2},{7,3},{8,12},{9,13},{10,... | collective-permute-start | bytes 688136 | tf_op jit(solution)/shard_map/ppermute | solution.py:357
  90.3 13.6 %collective-permute-start.7 = (bf16[104,512]{1,0:T(8,128)(2,1)S(1)}, bf16[104,512]{1,0:T(8,128)(2,1)S(1)}, u32[]{:S(2)}, u32[]{:S(2)}) collective-permute-start(bf16[104,512]{1,0:T(8,128)(2,1)S(1)} %dynamic-slice_bitcast_fusion.3), channel_id=1, source_target_pairs={{0,8},{1,9},{2,10},{3,11},{4,12},{5,13},{6,14},{7,15},{8,0},{9,1},... | collective-permute-start | bytes 319496 | tf_op jit(solution)/shard_map/ppermute | solution.py:357
  95.3 10.5 %collective-permute-start.3 = (bf16[112,512]{1,0:T(8,128)(2,1)S(1)}, bf16[112,512]{1,0:T(8,128)(2,1)S(1)}, u32[]{:S(2)}, u32[]{:S(2)}) collective-permute-start(bf16[112,512]{1,0:T(8,128)(2,1)S(1)} %dynamic-slice_bitcast_fusion.2), channel_id=1, source_target_pairs={{0,8},{1,9},{2,10},{3,11},{4,12},{5,13},{6,14},{7,15},{8,0},{9,1},... | collective-permute-start | bytes 344072 | tf_op jit(solution)/shard_map/ppermute | solution.py:357
  109.1 1.0 copy-start.1

commit v2 on v1

--- a/solution.py
+++ b/solution.py
@@ -16,8 +16,10 @@
 SMEM = pl.BlockSpec(memory_space=pltpu.SMEM)
 ANY = pl.BlockSpec(memory_space=pl.ANY)
 MEBI = 1024 * 1024
-LIMIT = 60 * MEBI
-ORDERS = ((0, 1), (1, 0))
+LIMIT = 62 * MEBI
+SMALL = 62 * MEBI
+TURNS = 4
+CHAINS = 1
 
 
 def round_up(value, multiple):
@@ -45,9 +47,16 @@
         self.sent = self.returned = 0
         for section in range(3):
             self.out_at.append(self.sent)
+            self.sent += self.counts[section] * (self.out_width(section) // LANES)
+        for section in range(3):
             self.back_at.append(self.returned)
-            self.sent += self.counts[section] * (channels[section] // LANES)
             self.returned += self.counts[section] * (self.back_width(section) // LANES)
+        self.slice_at = self.sent
+        self.slice_width = channels[2] // owners
+        self.sent += self.coarse[2]
+
+    def out_width(self, section):
+        return self.channels[section] if section < 2 else self.width
 
     def back_width(self, section):
         return self.channels[0] if section == 0 else self.width
@@ -162,9 +171,10 @@
 
 
 def pack_kernel(plan, map_ref, *refs):
-    sources, out_ref = refs[:3], refs[3]
-    held, picks, sem_ref = refs[4:7], refs[7:10], refs[10]
+    sources, out_ref = refs[:4], refs[4]
+    held, picks, sem_ref = refs[5:9], refs[9:12], refs[12]
     copies = copies_in(list(zip(sources, held)), sem_ref)
+    four_ref, l4_ref = held[2:]
     for section in range(3):
         columns, count, places = plan.columns[section], plan.counts[section], plan.coarse[section]
         start, offset = entry_vectors(plan, section, (count, min(LANES, places)))
@@ -178,8 +188,16 @@
         count = plan.counts[section]
         pick = picks[section][...].reshape(plan.owners * count, plan.coarse[section])
         copies[section].wait()
-        chosen = contract(pick, held[section][...], 1, 0).astype(BF16)
-        put_pieces(out_ref, plan.out_at[section], chosen, count)
+        values = held[section][...]
+        if section == 2:
+            copies[3].wait()
+            values = contract(values, l4_ref[...], 1, 0).astype(BF16)
+        put_pieces(out_ref, plan.out_at[section], contract(pick, values, 1, 0).astype(BF16), count)
+    count = plan.coarse[2]
+    fill = jnp.zeros((count, LANES - plan.slice_width), BF16)
+    for owner in range(plan.owners):
+        part = four_ref[:, owner * plan.slice_width : (owner + 1) * plan.slice_width]
+        out_ref[owner, plan.slice_at :, :] = jnp.concatenate([part, fill], axis=1)
 
 
 def put_parts(part_refs, even_refs, odd_refs):
@@ -222,17 +240,22 @@
     second.wait()
 
 
+def take_features(plan, arrived_ref, section):
+    return take_pieces(
+        arrived_ref, plan.out_at[section], plan.out_width(section) // LANES, plan.counts[section]
+    )
+
+
 def strip_kernel(plan, turns, chains, core_ref, *refs):
     sent = 2 + 2 * chains
-    sources, outs, held = refs[:11], refs[11 : 11 + sent], refs[11 + sent : 22 + sent]
-    stage, refs = refs[22 + sent : 22 + 2 * sent], refs[22 + 2 * sent :]
-    arrived_ref, l2_ref, l3_ref, l4_ref, up_ref, down_ref = held[:6]
-    straight_ref, hidden_grad_ref, cot_ref, fine_ref, l1_ref = held[6:]
+    sources, outs, held = refs[:10], refs[10 : 10 + sent], refs[10 + sent : 20 + sent]
+    stage, refs = refs[20 + sent : 20 + 2 * sent], refs[20 + 2 * sent :]
+    arrived_ref, l2_ref, l3_ref, up_ref, down_ref = held[:5]
+    straight_ref, hidden_grad_ref, cot_ref, fine_ref, l1_ref = held[5:]
     grad_fine_ref, back_ref = stage[:2]
     coarse_ref, hidden_ref, joined_grad_ref = refs[:3]
-    grad_refs, join_part_ref, one_part_ref = refs[3:6], refs[6], refs[7]
-    part_refs, sem_ref, in_sem, turn_sem = refs[8:11], refs[11], refs[12], refs[13]
-    lateral_refs = (l2_ref, l3_ref, l4_ref)
+    grad_refs = refs[3:6]
+    join_part_ref, two_part_ref, three_part_ref, one_part_ref, out_sem, in_sem, turn_sem = refs[6:]
     owners, per_owner, width = plan.owners, plan.per_owner, plan.width
     core = core_ref[0]
     block = up_ref.shape[1]
@@ -240,44 +263,45 @@
     window = down_ref.shape[2]
     total = cot_ref.shape[0]
     group = owners // turns
-    copies = copies_in(list(zip(sources[:6], held[:6])), in_sem)
+    copies = copies_in(list(zip(sources[:5], held[:5])), in_sem)
     turn_copies = []
     for turn in range(turns):
         many = pl.ds(turn * group * block, group * block)
         for which in (0, 1):
             copy = pltpu.make_async_copy(
-                sources[6 + which].at[many], held[6 + which].at[many], turn_sem.at[which, turn]
+                sources[5 + which].at[many], held[5 + which].at[many], turn_sem.at[which, turn]
             )
             copy.start()
             turn_copies.append(copy)
     late_copies = []
-    for index in (8, 9, 10):
+    for index in (7, 8, 9):
         copy = pltpu.make_async_copy(sources[index], held[index], in_sem.at[index - 2])
         copy.start()
         late_copies.append(copy)
 
     def leave(index):
-        copy = pltpu.make_async_copy(stage[index], outs[index], sem_ref.at[index])
+        copy = pltpu.make_async_copy(stage[index], outs[index], out_sem.at[index])
         copy.start()
         return copy
 
-    def features(section):
-        return take_pieces(
-            arrived_ref, plan.out_at[section], plan.channels[section] // LANES, plan.counts[section]
-        )
-
     copies[0].wait()
+    features = [
+        take_pieces(arrived_ref, plan.out_at[section], plan.out_width(section) // LANES, plan.counts[section])
+        for section in range(3)
+    ]
     projected = []
     for section in range(3):
-        copies[1 + section].wait()
-        product = contract(features(section), lateral_refs[section][...], 1, 0).astype(BF16)
+        product = features[section]
+        if section < 2:
+            copies[1 + section].wait()
+            product = contract(product, (l2_ref, l3_ref)[section][...], 1, 0).astype(BF16)
         projected.append(product.reshape(owners, plan.counts[section], width))
     tail = per_owner - sum(plan.counts)
     if tail:
         projected.append(jnp.zeros((owners, tail, width), BF16))
     coarse_ref[...] = jnp.concatenate(projected, axis=1).reshape(owners * per_owner, width)
+    copies[3].wait()
     copies[4].wait()
-    copies[5].wait()
 
     for turn in range(turns):
         turn_copies[2 * turn].wait()
@@ -298,58 +322,84 @@
     for owner in range(owners):
         kind = 0 if owner == 0 else 2 if owner == owners - 1 else 1
         low = min(max(owner * block - 32, 0), total - window)
-        strip_grad = contract(down_ref[kind], joined_grad_ref[low : low + window, :], 1, 0).astype(BF16)
-        for section in range(3):
+        strip_grad = contract(down_ref[kind], joined_grad_ref[low : low + window, :], 1, 0)
+        for section, ref in enumerate(grad_refs):
             at = plan.starts[section]
-            grad_refs[section][owner] = strip_grad[at : at + plan.counts[section]]
-
-    strip_grads = [
-        ref[...].reshape(owners * count, width) for ref, count in zip(grad_refs, plan.counts)
-    ]
-    put_pieces(back_ref, 0, contract(strip_grads[0], l2_ref[...], 1, 1).astype(BF16), plan.counts[0])
+            ref[owner] = strip_grad[at : at + plan.counts[section]].astype(BF16)
+    strip_grads = [ref[...].reshape(owners * count, width) for ref, count in zip(grad_refs, plan.counts)]
     for section in (1, 2):
         put_pieces(back_ref, plan.back_at[section], strip_grads[section], plan.counts[section])
+    put_pieces(back_ref, 0, contract(strip_grads[0], l2_ref[...], 1, 1).astype(BF16), plan.counts[0])
     leaving = [leave(1)]
-    for section in range(3):
-        part_refs[section][...] = contract(features(section), strip_grads[section], 0, 0)
+    two_part_ref[...] = contract(features[0], strip_grads[0], 0, 0)
+    three_part_ref[...] = contract(features[1], strip_grads[1], 0, 0)
     for copy in late_copies:
         copy.wait()
     join_part_ref[...] = contract(cot_ref[...], hidden_ref[...], 0, 0)
     one_part_ref[...] = contract(fine_ref[...], joined_grad_ref[...], 0, 0)
-
     kept, given = stage[2 : 2 + chains], stage[2 + chains :]
-    ordered_parts = (join_part_ref, *part_refs, one_part_ref)
+    parts = (join_part_ref, two_part_ref, three_part_ref, one_part_ref)
 
     @pl.when(core == 0)
     def _():
-        put_parts(ordered_parts, kept, given)
+        put_parts(parts, kept, given)
 
     @pl.when(core != 0)
     def _():
-        put_parts(ordered_parts, given, kept)
-
-    leaving += [leave(index) for index in range(2, len(stage))]
+        put_parts(parts, given, kept)
+
+    leaving += [leave(index) for index in range(2, sent)]
     grad_fine_ref[...] = contract(joined_grad_ref[...], l1_ref[...], 1, 1).astype(BF16)
     leaving.append(leave(0))
     for copy in leaving:
         copy.wait()
 
 
+def finish_kernel(plan, chains, *refs):
+    count = (len(refs) - 6) // 2
+    sources, outs, held, sem_ref = refs[:count], refs[count : count + 5], refs[count + 5 : -1], refs[-1]
+    copies = copies_in(list(zip(sources, held)), sem_ref)
+    first = 2 * chains
+    for copy in copies[:first]:
+        copy.wait()
+    total = jnp.concatenate(
+        [held[2 * c][...].astype(F32) + held[2 * c + 1][...].astype(F32) for c in range(chains)]
+    )
+    join_ref, two_ref, three_ref, one_ref, four_ref = outs
+    at = 0
+    for ref in (join_ref, two_ref, three_ref, one_ref):
+        ref[...] = total[at : at + ref.shape[0]]
+        at += ref.shape[0]
+    for copy in copies[first:]:
+        copy.wait()
+    slices_ref, pieces = held[first], held[first + 1 :]
+    blocks = jnp.concatenate([piece[...] for piece in pieces])
+    four_ref[...] = contract(slices_ref[...], blocks, 0, 0)[: four_ref.shape[0]]
+
+
+def fold_kernel(plan, returned_ref, fold_ref, out_ref):
+    arrived = take_pieces(returned_ref, plan.back_at[2], plan.back_width(2) // LANES, plan.counts[2])
+    out_ref[...] = contract(fold_ref[...], arrived, 1, 0).astype(BF16)
+
+
 def section_kernel(plan, *refs):
     sources, outs, held, sem_ref = refs[:6], refs[6:9], refs[9:15], refs[15]
     copies = copies_in(list(zip(sources, held)), sem_ref)
-    returned_ref, folds, laterals = held[0], held[1:4], held[4:6]
+    returned_ref, folds, l3_ref, l4_ref, four_ref = held[0], held[1:3], held[3], held[4], held[5]
     copies[0].wait()
-    for section in range(3):
+    for section in range(2):
         arrived = take_pieces(
             returned_ref, plan.back_at[section], plan.back_width(section) // LANES, plan.counts[section]
         )
         copies[1 + section].wait()
         folded = contract(folds[section][...], arrived, 1, 0).astype(BF16)
-        if section > 0:
-            copies[3 + section].wait()
-            folded = contract(folded, laterals[section - 1][...], 1, 1).astype(BF16)
+        if section == 1:
+            copies[3].wait()
+            folded = contract(folded, l3_ref[...], 1, 1).astype(BF16)
         outs[section][...] = folded
+    copies[4].wait()
+    copies[5].wait()
+    outs[2][...] = contract(four_ref[...], l4_ref[...], 1, 1).astype(BF16)
 
 
 def swap(values, bit):
@@ -368,26 +418,44 @@
         self.left = sorted(order, reverse=True)
         self.order = list(order)
 
-    def step(self):
+    def split(self):
         bit = self.order.pop(0)
         axis = self.left.index(bit)
         self.left.pop(axis)
         mine = (lax.axis_index("row") >> bit) & 1
         keep = lax.dynamic_index_in_dim(self.values, mine, axis, keepdims=False)
         give = lax.dynamic_index_in_dim(self.values, 1 - mine, axis, keepdims=False)
-        self.values = plus(keep, swap(give, bit))
-
-
-def reduce_chains(kept, given, bits):
-    chains = []
-    for keep, give, order in zip(kept, given, ORDERS):
-        rest = list(range(1, bits))
-        rest[: len(order)] = [rest[i] for i in order]
-        chains.append(Halving(plus(keep, swap(give, 0)), rest))
-    for _ in range(1, bits):
-        for chain in chains:
-            chain.step()
-    return [chain.values for chain in chains]
+        return keep, give, bit
+
+    def step(self, later=None):
+        keep, give, bit = self.split()
+        if later is not None:
+            give, later = lax.optimization_barrier((give, later))
+        if self.order:
+            self.values = plus(keep, swap(give, bit))
+        else:
+            self.terms = keep, swap(give, bit)
+        return later
+
+
+def level_swaps(level):
+    distances = [0]
+    for bit in level:
+        distances += [d ^ (1 << bit) for d in distances]
+    return distances
+
+
+def gather_level(stacked, level):
+    owners = lax.axis_size("row")
+    distances = level_swaps(level)[1:]
+    return [stacked] + [lax.ppermute(stacked, "row", [(i, i ^ d) for i in range(owners)]) for d in distances]
+
+
+def gather_pattern(levels):
+    pattern = np.zeros((1,), np.int32)
+    for level in levels:
+        pattern = np.concatenate([pattern ^ d for d in level_swaps(level)])
+    return pattern
 
 
 def shape_of(*dims, dtype=BF16):
@@ -426,19 +494,21 @@
     outgoing = pl.pallas_call(
         functools.partial(pack_kernel, plan),
         out_shape=shape_of(owners, plan.sent, LANES),
-        in_specs=[SMEM] + [ANY] * 3,
+        in_specs=[SMEM] + [ANY] * 4,
         out_specs=VMEM,
-        scratch_shapes=[pltpu.VMEM(f.shape, BF16) for f in flats]
+        scratch_shapes=[pltpu.VMEM(x.shape, BF16) for x in (*flats, lateral_four)]
         + [pltpu.VMEM((owners, count, places), BF16) for count, places in zip(plan.counts, plan.coarse)]
-        + [pltpu.SemaphoreType.DMA((3,))],
+        + [pltpu.SemaphoreType.DMA((4,))],
         compiler_params=pltpu.CompilerParams(vmem_limit_bytes=LIMIT),
         name="pack",
-    )(strip_map, *flats)
+    )(strip_map, *flats, lateral_four)
     arrived = exchange(outgoing)
+    folds = [fold_matrix(strip_map, plan, section) for section in range(3)]
+    arrived, folds = lax.optimization_barrier((arrived, folds))
 
     half = owners // 2
-    heights = [x // owners for x in (width, *channels, c1)]
-    chains = len(ORDERS)
+    heights = [x // owners for x in (width, *channels[:2], c1)]
+    chains = CHAINS
     tall = round_up(sum(heights), 8)
     cuts = [round_up(tall * c // chains, 8) for c in range(chains)] + [tall]
     chain_heights = [high - low for low, high in zip(cuts, cuts[1:])]
@@ -461,7 +531,6 @@
         arrived,
         lateral_two,
         lateral_three,
-        lateral_four,
         up,
         down,
         straight,
@@ -473,9 +542,9 @@
     stage = (shape_of(total, c1), shape_of(owners, plan.returned, LANES))
     stage += tuple(shape_of(half, height, width) for height in chain_heights) * 2
     grad_fine, back, *halves = pl.pallas_call(
-        functools.partial(strip_kernel, plan, 4, chains),
+        functools.partial(strip_kernel, plan, TURNS, chains),
         out_shape=stage,
-        in_specs=[SMEM] + [ANY] * 11,
+        in_specs=[SMEM] + [ANY] * 10,
         out_specs=(ANY,) * len(stage),
         scratch_shapes=[pltpu.VMEM(x.shape, x.dtype) for x in operands + stage]
         + [
@@ -484,48 +553,95 @@
             pltpu.VMEM((total, width), BF16),
         ]
         + [pltpu.VMEM((owners, count, width), BF16) for count in plan.counts]
-        + [pltpu.VMEM((x, width), F32) for x in (width, c1, *channels)]
+        + [pltpu.VMEM((x, width), F32) for x in (width, *channels[:2], c1)]
         + [
             pltpu.SemaphoreType.DMA((len(stage),)),
-            pltpu.SemaphoreType.DMA((9,)),
-            pltpu.SemaphoreType.DMA((2, 4)),
+            pltpu.SemaphoreType.DMA((8,)),
+            pltpu.SemaphoreType.DMA((2, TURNS)),
         ],
         compiler_params=pltpu.CompilerParams(vmem_limit_bytes=LIMIT),
         cost_estimate=pl.CostEstimate(
-            flops=4_000_000_000, bytes_accessed=9_000_000, transcendentals=total * width
+            flops=4_000_000_000, bytes_accessed=16_000_000, transcendentals=total * width
         ),
         name="strip_work",
     )(core, *operands)
 
+    levels = tuple(range(bits - 2, bits)), tuple(range(bits - 2))
+    slices = jnp.take(arrived[:, plan.slice_at :], me ^ gather_pattern(levels), axis=0)
+    grad_fine = jnp.transpose(grad_fine.reshape(fine_features.shape), (1, 2, 0))
+    rest = [
+        Halving(plus(keep, swap(give, 0)), range(1, bits))
+        for keep, give in zip(halves[:chains], halves[chains:])
+    ]
+    halved = [chain.split() for chain in rest]
+    halved = [(keep, swap(give, bit)) for keep, give, bit in halved]
     returned = exchange(back)
-    summed = reduce_chains(halves[:chains], halves[chains:], bits)
-    summed = jnp.concatenate(summed, axis=0).astype(F32)
-    ends = np.cumsum([0] + heights).tolist()
-    weight_grads = [summed[low:high] for low, high in zip(ends, ends[1:])]
-
-    operands = (
-        returned,
-        *[fold_matrix(strip_map, plan, section) for section in range(3)],
-        lateral_three,
-        lateral_four,
-    )
+    returned, grad_fine, slices = lax.optimization_barrier((returned, grad_fine, slices))
+
+    folded_four = pl.pallas_call(
+        functools.partial(fold_kernel, plan),
+        out_shape=shape_of(plan.coarse[2], width),
+        in_specs=[VMEM] * 2,
+        out_specs=VMEM,
+        compiler_params=pltpu.CompilerParams(vmem_limit_bytes=8 * MEBI),
+        name="fold_four",
+    )(returned, folds[2])
+    *halved, folded_four = lax.optimization_barrier((*halved, folded_four))
+    for chain, (keep, received) in zip(rest, halved):
+        chain.values = plus(keep, received)
+    operands = (returned, *folds[:2], lateral_three, lateral_four, folded_four)
     grads = pl.pallas_call(
         functools.partial(section_kernel, plan),
         out_shape=tuple(shape_of(*f.shape) for f in flats),
         in_specs=[ANY] * 6,
         out_specs=(VMEM,) * 3,
         scratch_shapes=[pltpu.VMEM(x.shape, BF16) for x in operands] + [pltpu.SemaphoreType.DMA((6,))],
-        compiler_params=pltpu.CompilerParams(vmem_limit_bytes=LIMIT),
+        compiler_params=pltpu.CompilerParams(vmem_limit_bytes=SMALL),
         cost_estimate=pl.CostEstimate(flops=500_000_000, bytes_accessed=6_000_000, transcendentals=0),
         name="section_grads",
     )(*operands)
 
+    gathered = folded_four[None]
+    for turn in range(bits - 2):
+        if turn == 0:
+            gathered = jnp.concatenate(gather_level(gathered, levels[0]))
+            for chain in rest:
+                chain.step()
+        else:
+            for chain in rest:
+                gathered = chain.step(gathered)
+        if turn < bits - 3:
+            *values, grads, gathered = lax.optimization_barrier(
+                (*[chain.values for chain in rest], grads, gathered)
+            )
+            for chain, value in zip(rest, values):
+                chain.values = value
+    gathered = gather_level(gathered, levels[1])
+
+    operands = tuple(term for chain in rest for term in chain.terms)
+    operands += (slices.reshape(-1, LANES), *[g.reshape(-1, width) for g in gathered])
+    results = pl.pallas_call(
+        functools.partial(finish_kernel, plan, chains),
+        out_shape=(
+            *[shape_of(height, width, dtype=F32) for height in heights],
+            shape_of(plan.slice_width, width, dtype=F32),
+        ),
+        in_specs=[ANY] * len(operands),
+        out_specs=(VMEM,) * 5,
+        scratch_shapes=[pltpu.VMEM(x.shape, BF16) for x in operands]
+        + [pltpu.SemaphoreType.DMA((len(operands),))],
+        compiler_params=pltpu.CompilerParams(vmem_limit_bytes=LIMIT),
+        name="finish",
+    )(*operands)
+    join_grad, two_grad, three_grad, one_grad, four_grad = results
     return (
-        grad_fine.reshape(fine_features.shape),
+        jnp.transpose(grad_fine, (2, 0, 1)),
         *[g.reshape(s.shape) for g, s in zip(grads, sections)],
-        weight_grads[0].T,
-        weight_grads[4],
-        *weight_grads[1:4],
+        join_grad.T,
+        one_grad,
+        two_grad,
+        three_grad,
+        four_grad,
     )
 
 

time: 115 us -> 110 us (0.957)
  other arithmetic: 9.85 us -> 4.01 us
  starting transfers between devices: 28.5 us -> 25.8 us
  waiting for transfers between devices: 42.1 us -> 43.7 us
    all_to_all x1, waiting for transfers between devices: 0.01 us -> 14.6 us  [body(): returned = exchange(back)]
    ppermute x8 -> x4, starting transfers between devices: 16.8 us -> 4.71 us  [swap(): lax.ppermute(values, 'row', [(i, i ^ 1 << bit) for i in range(owners)])]
    ppermute x8 -> x4, waiting for transfers between devices: 21 us -> 10.4 us  [swap(): lax.ppermute(values, 'row', [(i, i ^ 1 << bit) for i in range(owners)])]
    ppermute x0 -> x6, starting transfers between devices: none -> 6.25 us  [gather_level(): lax.ppermute(stacked, 'row', [(i, i ^ d) for i in range(owners)])]
    all_to_all x1, waiting for transfers between devices: 21.1 us -> 16.8 us  [body(): arrived = exchange(outgoing)]
    convert_element_type x8 -> x3, other arithmetic: 4.08 us -> 0.47 us  [plus(): return (left.astype(F32) + right.astype(F32)).astype(BF16)]
    all_to_all x1, starting transfers between devices: 4.11 us -> 7.25 us  [body(): returned = exchange(back)]
    unnamed x26 -> x35, local copies, waits for them, and re-layouts: 5.57 us -> 2.56 us
  transfers between devices with their start and end apart: 10 -> 12, of which waited for: 8 -> 5; matrix products, arithmetic and copies ran while one was open for 13% -> 9% of each run, Pallas kernels for 5% -> 9%
where the time goes in v2:
time: 110 us; the launch traced here: 109 us
  waiting for transfers between devices  43.7 us (40%)
  Pallas kernels  26.8 us (24%)
  starting transfers between devices  25.8 us (23%)
  local copies, waits for them, and re-layouts  7.76 us (7%)
  other arithmetic  4.01 us (4%)
  between operations  1.17 us (1%)
    all_to_all x1, waiting for transfers between devices, body(): arrived = exchange(outgoing)  16.8 us
    all_to_all x1, waiting for transfers between devices, body(): returned = exchange(back)  14.6 us
    pallas_call x1, Pallas kernels, body(): pl.pallas_call(functools.partial(strip_kernel, plan, TURNS, chains), out_...  10.8 us
    ppermute x4, waiting for transfers between devices, swap(): lax.ppermute(values, 'row', [(i, i ^ 1 << bit) for i in range(owners)])  10.4 us
    all_to_all x1, starting transfers between devices, body(): arrived = exchange(outgoing)  7.58 us
    all_to_all x1, starting transfers between devices, body(): returned = exchange(back)  7.25 us
    ppermute x6, starting transfers between devices, gather_level(): lax.ppermute(stacked, 'row', [(i, i ^ d) for i in range(owners)])  6.25 us
    pallas_call x1, Pallas kernels, body(): pl.pallas_call(ahead_kernel, out_shape=(shape_of(total, width, dtype=F32)...  5.51 us
  transfers between devices with their start and end apart: 12, of which 5 were waited for; matrix products, arithmetic and copies ran while one was open for 9% of the time, Pallas kernels for 9%

profile of v2, /device:TPU:0, one launch (start us, length us, event | category | flops | bytes accessed | tf_op | source)
XLA Modules:
  0.0 109.2 jit_solution(5752711693671831986)
XLA Ops:
  0.6 4.2 %pack.1 = bf16[16,304,128]{2,1,0:T(8,128)(2,1)} custom-call(s32[16]{0:T(128)} %map_ref.1, bf16[512,384]{1,0:T(8,128)(2,1)} %bitcast.47, bf16[128,768]{1,0:T(8,128)(2,1)} %bitcast.48, bf16[32,1536]{1,0:T(8,128)(2,1)} %bitcast.52, bf16[1536,512]{1,0:T(8,128)(2,1)} %refs_4_.2), custom_call_target="tpu_custom_call" | custom-call | tf_op jit(solution)/shard_map/pack/pallas_call | solution.py:494
  4.8 0.0 copy-start.9
  4.8 0.0 copy-start.10
  4.8 0.0 copy-start.15
  4.9 0.0 copy-start.13
  4.9 0.0 copy-start.14
  4.9 0.0 copy-start.11
  4.9 0.0 copy-start.12
  4.9 0.0 copy-start.3
  4.9 7.6 %all-to-all-start = ((bf16[16,304,128]{2,1,0:T(8,128)(2,1)}), bf16[16,304,128]{2,1,0:T(8,128)(2,1)}, u32[]{:S(2)}, u32[]{:S(2)}) async-start(bf16[16,304,128]{2,1,0:T(8,128)(2,1)} %pack.1), calls=%async_computation | async-start | bytes 2490368 | tf_op jit(solution)/shard_map/all_to_all | solution.py:505
  12.6 0.1 clamp_add_fusion.2
  12.6 0.1 add.141
  12.7 0.0 copy-done.13
  12.7 0.1 clamp_add_fusion.1
  12.8 0.1 add.147
  12.9 0.1 clamp_add_fusion
  13.0 0.1 add.153
  13.1 1.7 %copy.36 = bf16[256,8,192]{2,1,0:T(8,128)(2,1)} copy(bf16[256,8,192]{0,2,1:T(8,128)(2,1)S(1)} %copy-done.3) | data formatting | bytes 1572864 | tf_op args[0]
  14.8 0.6 fusion.2.refs_2_
  15.5 1.1 fusion.refs_1_
  16.6 5.5 %ahead.1 = (f32[2048,512]{1,0:T(8,128)}, f32[2048,512]{1,0:T(8,128)}) custom-call(bf16[192,512]{1,0:T(8,128)(2,1)} %refs_9_.1, bf16[2048,192]{1,0:T(8,128)(2,1)} %bitcast.42, bf16[512,512]{1,0:T(8,128)(2,1)} %refs_2_.2, bf16[2048,512]{1,0:T(8,128)(2,1)} %bitcast.53), custom_call_target="tpu_custom_call" | custom-call | flops 2952790016 | bytes 14000000 | tf_op jit(solution)/shard_map/ahead/pallas_call | solution.py:516
  22.1 16.8 %all-to-all-done.refs_0_ = bf16[16,304,128]{2,1,0:T(8,128)(2,1)} async-done(((bf16[16,304,128]{2,1,0:T(8,128)(2,1)}), bf16[16,304,128]{2,1,0:T(8,128)(2,1)}, u32[]{:S(2)}, u32[]{:S(2)}) %all-to-all-start) | async-done | bytes 1245216 | tf_op jit(solution)/shard_map/all_to_all | solution.py:505
  38.8 10.8 %strip_work.1 = (bf16[2048,192]{1,0:T(8,128)(2,1)}, bf16[16,240,128]{2,1,0:T(8,128)(2,1)}, bf16[8,120,512]{2,1,0:T(8,128)(2,1)}, bf16[8,120,512]{2,1,0:T(8,128)(2,1)}) custom-call(s32[1]{0:T(128)} %bitcast.core_ref, bf16[16,304,128]{2,1,0:T(8,128)(2,1)} %all-to-all-done.refs_0_, bf16[384,512]{1,0:T(8,128)(2,1)} %refs_1_.1, bf16[768,512]{1,0:T(8,128)(2,1)} %refs_3_.4, ...), custom_call_target="tpu_custom_call" | custom-call | flops 4000000000 | bytes 16000000 | tf_op jit(solution)/shard_map/strip_work/pallas_call | solution.py:544
  49.6 0.9 collective-permute-start
  50.5 7.2 %all-to-all-start.1 = ((bf16[16,240,128]{2,1,0:T(8,128)(2,1)}), bf16[16,240,128]{2,1,0:T(8,128)(2,1)S(1)}, u32[]{:S(2)}, u32[]{:S(2)}) async-start(bf16[16,240,128]{2,1,0:T(8,128)(2,1)} %get-tuple-element.43), calls=%async_computation.1 | async-start | bytes 1966080 | tf_op jit(solution)/shard_map/all_to_all | solution.py:578
  57.8 0.0 collective-permute-done
  57.8 0.3 add_convert_fusion
  58.1 0.0 copy-start.16
  58.1 0.1 constant_dynamic-slice_fusion
  58.2 2.0 %collective-permute-start.1 = (bf16[2,2,120,512]{3,2,0,1:T(8,128)(2,1)S(1)}, bf16[2,2,120,512]{3,2,0,1:T(8,128)(2,1)S(1)}, u32[]{:S(2)}, u32[]{:S(2)}) collective-permute-start(bf16[2,2,120,512]{3,2,0,1:T(8,128)(2,1)S(1)} %bitcast.46), channel_id=1, source_target_pairs={{0,2},{1,3},{2,0},{3,1},{4,6},{5,7},{6,4},{7,5},{8,10},{9,11},{10,... | collective-permute-start | bytes 1474568 | tf_op jit(solution)/shard_map/ppermute | solution.py:407
  60.2 0.9 slice.3
  61.1 2.6 %copy.37 = bf16[256,8,192]{0,2,1:T(8,128)(2,1)} copy(bf16[256,8,192]{2,1,0:T(8,128)(2,1)} %bitcast.41) | data formatting | bytes 1572864 | tf_op jit(solution)/shard_map/reshape | solution.py:571
  63.7 0.6 gather_fusion
  64.3 0.8 broadcast_select_fusion
  65.1 14.6 %all-to-all-done.1.returned_ref.refs_0_ = bf16[16,240,128]{2,1,0:T(8,128)(2,1)S(1)} async-done(((bf16[16,240,128]{2,1,0:T(8,128)(2,1)}), bf16[16,240,128]{2,1,0:T(8,128)(2,1)S(1)}, u32[]{:S(2)}, u32[]{:S(2)}) %all-to-all-start.1) | async-done | bytes 983072 | tf_op jit(solution)/shard_map/all_to_all | solution.py:578
  79.7 0.1 fold_four.1.refs_5_
  79.8 0.0 copy-start.1
  79.8 2.1 %collective-permute-done.1 = bf16[2,2,120,512]{3,2,0,1:T(8,128)(2,1)S(1)} collective-permute-done((bf16[2,2,120,512]{3,2,0,1:T(8,128)(2,1)S(1)}, bf16[2,2,120,512]{3,2,0,1:T(8,128)(2,1)S(1)}, u32[]{:S(2)}, u32[]{:S(2)}) %collective-permute-start.1) | collective-permute-done | bytes 491552 | tf_op jit(solution)/shard_map/ppermute | solution.py:407
  81.9 0.1 add_convert_fusion.1
  82.1 1.4 %collective-permute-start.2 = (bf16[2,120,512]{2,1,0:T(8,128)(2,1)S(1)}, bf16[2,120,512]{2,1,0:T(8,128)(2,1)S(1)}, u32[]{:S(2)}, u32[]{:S(2)}) collective-permute-start(bf16[2,120,512]{2,1,0:T(8,128)(2,1)S(1)} %dynamic-slice_bitcast_fusion), channel_id=1, source_target_pairs={{0,4},{1,5},{2,6},{3,7},{4,0},{5,1},{6,2},{7,3},{8,12},{9,13},{10,... | collective-permute-start | bytes 737288 | tf_op jit(solution)/shard_map/ppermute | solution.py:407
  83.5 0.7 collective-permute-start.3
  84.2 2.6 %collective-permute-start.4 = (bf16[1,32,512]{2,1,0:T(8,128)(2,1)S(1)}, bf16[1,32,512]{2,1,0:T(8,128)(2,1)}, u32[]{:S(2)}, u32[]{:S(2)}) collective-permute-start(bf16[1,32,512]{2,1,0:T(8,128)(2,1)S(1)} %bitcast.36), channel_id=1, source_target_pairs={{0,8},{1,9},{2,10},{3,11},{4,12},{5,13},{6,14},{7,15},{8,0},{9,1},... | collective-permute-start | bytes 98312 | tf_op jit(solution)/shard_map/ppermute | solution.py:451
  86.8 1.1 %collective-permute-start.5 = (bf16[1,32,512]{2,1,0:T(8,128)(2,1)S(1)}, bf16[1,32,512]{2,1,0:T(8,128)(2,1)}, u32[]{:S(2)}, u32[]{:S(2)}) collective-permute-start(bf16[1,32,512]{2,1,0:T(8,128)(2,1)S(1)} %bitcast.37), channel_id=1, source_target_pairs={{0,12},{1,13},{2,14},{3,15},{4,8},{5,9},{6,10},{7,11},{8,4},{9,5},... | collective-permute-start | bytes 98312 | tf_op jit(solution)/shard_map/ppermute | solution.py:451
  87.9 4.0 %section_grads.1 = (bf16[512,384]{1,0:T(8,128)(2,1)}, bf16[128,768]{1,0:T(8,128)(2,1)}, bf16[32,1536]{1,0:T(8,128)(2,1)}) custom-call(bf16[16,240,128]{2,1,0:T(8,128)(2,1)} %copy-done, bf16[512,768]{1,0:T(8,128)(2,1)} %fusion.refs_1_, bf16[128,256]{1,0:T(8,128)(2,1)} %fusion.2.refs_2_, bf16[768,512]{1,0:T(8,128)(2,1)} %refs_3_.4, bf16[1536,512]{1,0:T(8,128)(2,1)} %refs_4_.2, ...), custom_call_target="tpu_custom_call" | custom-call | flops 500000000 | bytes 6000000 | tf_op jit(solution)/shard_map/section_grads/pallas_call | solution.py:593
  91.9 0.0 collective-permute-done.3
  91.9 0.0 collective-permute-done.4
  91.9 2.0 %collective-permute-done.5 = bf16[1,32,512]{2,1,0:T(8,128)(2,1)} collective-permute-done((bf16[1,32,512]{2,1,0:T(8,128)(2,1)S(1)}, bf16[1,32,512]{2,1,0:T(8,128)(2,1)}, u32[]{:S(2)}, u32[]{:S(2)}) %collective-permute-start.5) | collective-permute-done | bytes 32800 | tf_op jit(solution)/shard_map/ppermute | solution.py:451
  93.9 0.8 pad_maximum_fusion
  94.7 0.0 collective-permute-done.2
  94.7 0.1 fusion.1
  94.8 0.7 dynamic-slice_bitcast_fusion.1
  95.5 0.0 collective-permute-start.7
  95.5 0.5 collective-permute-start.8
  96.0 1.4 %collective-permute-start.9 = (bf16[4,32,512]{2,1,0:T(8,128)(2,1)S(1)}, bf16[4,32,512]{2,1,0:T(8,128)(2,1)S(1)}, u32[]{:S(2)}, u32[]{:S(2)}) collective-permute-start(bf16[4,32,512]{2,1,0:T(8,128)(2,1)S(1)} %pad_maximum_fusion), channel_id=1, source_target_pairs={{0,3},{1,2},{2,1},{3,0},{4,7},{5,6},{6,5},{7,4},{8,11},{9,10},{10,... | collective-permute-start | bytes 393224 | tf_op jit(solution)/shard_map/ppermute | solution.py:451
  97.3 0.5 collective-permute-start.6
  97.8 8.2 %collective-permute-done.6.refs_1_ = bf16[120,512]{1,0:T(8,128)(2,1)S(1)} collective-permute-done((bf16[120,512]{1,0:T(8,128)(2,1)S(1)}, bf16[120,512]{1,0:T(8,128)(2,1)S(1)}, u32[]{:S(2)}, u32[]{:S(2)}) %collective-permute-start.6) | collective-permute-done | bytes 122912 | tf_op jit(solution)/shard_map/ppermute | solution.py:407
  106.0 0.0 collective-permute-done.7
  106.0 0.0 collective-permute-done.8
  106.1 0.0 collective-permute-done.9
  106.1 0.6 copy-done.8
  106.7 0.1 copy-done.5
  106.7 0.1 copy-done.6
  106.8 0.0 copy-done.7
  106.8 2.2 %finish.1 = (f32[32,512]{1,0:T(8,128)}, f32[24,512]{1,0:T(8,128)}, f32[48,512]{1,0:T(8,128)}, f32[12,512]{1,0:T(8,128)}, f32[96,512]{1,0:T(8,128)}) custom-call(bf16[120,512]{1,0:T(8,128)(2,1)} %get-tuple-element.76.refs_0_, bf16[120,512]{1,0:T(8,128)(2,1)} %copy-done.8, bf16[512,128]{1,0:T(8,128)(2,1)} %bitcast.44, bf16[128,512]{1,0:T(8,128)(2,1)} %bitcast.45, ...), custom_call_target="tpu_custom_call" | custom-call | tf_op jit(solution)/shard_map/finish/pallas_call | solution.py:623
  (26 shorter events, 0.2 us)
Async XLA Ops:
  4.8 7.7 %copy-start.9 = (s32[16]{0:T(128)S(1)}, s32[16]{0:T(128)}, u32[]{:S(2)}) copy-start(s32[16]{0:T(128)} %map_ref.1) | copy-start | bytes 196
  4.8 7.7 %copy-start.10 = (s32[48]{0:T(128)S(1)}, s32[48]{0:T(128)}, u32[]{:S(2)}) copy-start(s32[48]{0:T(128)} %constant.80.clone) | copy-start | bytes 580
  4.8 7.7 %copy-start.15 = (s32[48]{0:T(128)S(1)}, s32[48]{0:T(128)}, u32[]{:S(2)}) copy-start(s32[48]{0:T(128)} %constant.81.clone) | copy-start | bytes 580
  4.9 7.8 %copy-start.13 = (s32[16]{0:T(128)S(1)}, s32[16]{0:T(128)}, u32[]{:S(2)}) copy-start(s32[16]{0:T(128)} %constant.83.clone) | copy-start | bytes 196
  4.9 7.8 %copy-start.14 = (s32[16]{0:T(128)S(1)}, s32[16]{0:T(128)}, u32[]{:S(2)}) copy-start(s32[16]{0:T(128)} %constant.84.clone) | copy-start | bytes 196
  4.9 8.0 %copy-start.11 = (s32[8]{0:T(128)S(1)}, s32[8]{0:T(128)}, u32[]{:S(2)}) copy-start(s32[8]{0:T(128)} %constant.86.clone) | copy-start | bytes 100
  4.9 8.0 %copy-start.12 = (s32[8]{0:T(128)S(1)}, s32[8]{0:T(128)}, u32[]{:S(2)}) copy-start(s32[8]{0:T(128)} %constant.87.clone) | copy-start | bytes 100
  4.9 8.1 %copy-start.3 = (bf16[256,8,192]{0,2,1:T(8,128)(2,1)S(1)}, bf16[256,8,192]{0,2,1:T(8,128)(2,1)}, u32[]{:S(2)}) copy-start(bf16[256,8,192]{0,2,1:T(8,128)(2,1)} %param.23) | copy-start | bytes 2359300
  4.9 33.9 %all-to-all-start = ((bf16[16,304,128]{2,1,0:T(8,128)(2,1)}), bf16[16,304,128]{2,1,0:T(8,128)(2,1)}, u32[]{:S(2)}, u32[]{:S(2)}) async-start(bf16[16,304,128]{2,1,0:T(8,128)(2,1)} %pack.1), calls=%async_computation | async-start | bytes 2490368 | tf_op jit(solution)/shard_map/all_to_all | solution.py:505
  49.6 8.1 %copy-start.2 = (bf16[8,120,512]{2,1,0:T(8,128)(2,1)S(1)}, bf16[8,120,512]{2,1,0:T(8,128)(2,1)}, u32[]{:S(2)}) copy-start(bf16[8,120,512]{2,1,0:T(8,128)(2,1)} %get-tuple-element.46) | copy-start | bytes 2949124
  49.6 8.1 %collective-permute-start = (bf16[8,120,512]{2,1,0:T(8,128)(2,1)}, bf16[8,120,512]{2,1,0:T(8,128)(2,1)S(1)}, u32[]{:S(2)}, u32[]{:S(2)}) collective-permute-start(bf16[8,120,512]{2,1,0:T(8,128)(2,1)} %get-tuple-element.47), channel_id=1, source_target_pairs={{0,1},{1,0},{2,3},{3,2},{4,5},{5,4},{6,7},{7,6},{8,9},{9,8},{10,11... | collective-permute-start | bytes 2949128 | tf_op jit(solution)/shard_map/ppermute | solution.py:407
  50.5 29.2 %all-to-all-start.1 = ((bf16[16,240,128]{2,1,0:T(8,128)(2,1)}), bf16[16,240,128]{2,1,0:T(8,128)(2,1)S(1)}, u32[]{:S(2)}, u32[]{:S(2)}) async-start(bf16[16,240,128]{2,1,0:T(8,128)(2,1)} %get-tuple-element.43), calls=%async_computation.1 | async-start | bytes 1966080 | tf_op jit(solution)/shard_map/all_to_all | solution.py:578
  58.1 2.1 %copy-start.16 = (s32[16]{0:T(128)S(1)}, s32[16]{0:T(128)}, u32[]{:S(2)}) copy-start(s32[16]{0:T(128)} %constant.91.clone) | copy-start | bytes 196
  58.2 23.7 %collective-permute-start.1 = (bf16[2,2,120,512]{3,2,0,1:T(8,128)(2,1)S(1)}, bf16[2,2,120,512]{3,2,0,1:T(8,128)(2,1)S(1)}, u32[]{:S(2)}, u32[]{:S(2)}) collective-permute-start(bf16[2,2,120,512]{3,2,0,1:T(8,128)(2,1)S(1)} %bitcast.46), channel_id=1, source_target_pairs={{0,2},{1,3},{2,0},{3,1},{4,6},{5,7},{6,4},{7,5},{8,10},{9,11},{10,... | collective-permute-start | bytes 1474568 | tf_op jit(solution)/shard_map/ppermute | solution.py:407
  79.7 8.3 %copy-start = (bf16[16,240,128]{2,1,0:T(8,128)(2,1)}, bf16[16,240,128]{2,1,0:T(8,128)(2,1)S(1)}, u32[]{:S(2)}) copy-start(bf16[16,240,128]{2,1,0:T(8,128)(2,1)S(1)} %all-to-all-done.1.returned_ref.refs_0_) | copy-start | bytes 2949124
  79.8 8.1 %copy-start.1 = (bf16[32,512]{1,0:T(8,128)(2,1)}, bf16[32,512]{1,0:T(8,128)(2,1)S(1)}, u32[]{:S(2)}) copy-start(bf16[32,512]{1,0:T(8,128)(2,1)S(1)} %fold_four.1.refs_5_) | copy-start | bytes 98308
  82.1 12.6 %collective-permute-start.2 = (bf16[2,120,512]{2,1,0:T(8,128)(2,1)S(1)}, bf16[2,120,512]{2,1,0:T(8,128)(2,1)S(1)}, u32[]{:S(2)}, u32[]{:S(2)}) collective-permute-start(bf16[2,120,512]{2,1,0:T(8,128)(2,1)S(1)} %dynamic-slice_bitcast_fusion), channel_id=1, source_target_pairs={{0,4},{1,5},{2,6},{3,7},{4,0},{5,1},{6,2},{7,3},{8,12},{9,13},{10,... | collective-permute-start | bytes 737288 | tf_op jit(solution)/shard_map/ppermute | solution.py:407
  83.5 8.4 %collective-permute-start.3 = (bf16[1,32,512]{2,1,0:T(8,128)(2,1)S(1)}, bf16[1,32,512]{2,1,0:T(8,128)(2,1)S(1)}, u32[]{:S(2)}, u32[]{:S(2)}) collective-permute-start(bf16[1,32,512]{2,1,0:T(8,128)(2,1)S(1)} %bitcast.35), channel_id=1, source_target_pairs={{0,4},{1,5},{2,6},{3,7},{4,0},{5,1},{6,2},{7,3},{8,12},{9,13},{10,... | collective-permute-start | bytes 98312 | tf_op jit(solution)/shard_map/ppermute | solution.py:451
  84.2 7.7 %collective-permute-start.4 = (bf16[1,32,512]{2,1,0:T(8,128)(2,1)S(1)}, bf16[1,32,512]{2,1,0:T(8,128)(2,1)}, u32[]{:S(2)}, u32[]{:S(2)}) collective-permute-start(bf16[1,32,512]{2,1,0:T(8,128)(2,1)S(1)} %bitcast.36), channel_id=1, source_target_pairs={{0,8},{1,9},{2,10},{3,11},{4,12},{5,13},{6,14},{7,15},{8,0},{9,1},... | collective-permute-start | bytes 98312 | tf_op jit(solution)/shard_map/ppermute | solution.py:451
  86.8 7.1 %collective-permute-start.5 = (bf16[1,32,512]{2,1,0:T(8,128)(2,1)S(1)}, bf16[1,32,512]{2,1,0:T(8,128)(2,1)}, u32[]{:S(2)}, u32[]{:S(2)}) collective-permute-start(bf16[1,32,512]{2,1,0:T(8,128)(2,1)S(1)} %bitcast.37), channel_id=1, source_target_pairs={{0,12},{1,13},{2,14},{3,15},{4,8},{5,9},{6,10},{7,11},{8,4},{9,5},... | collective-permute-start | bytes 98312 | tf_op jit(solution)/shard_map/ppermute | solution.py:451
  94.7 11.4 %copy-start.4 = (bf16[4,32,512]{2,1,0:T(8,128)(2,1)}, bf16[4,32,512]{2,1,0:T(8,128)(2,1)S(1)}, u32[]{:S(2)}) copy-start(bf16[4,32,512]{2,1,0:T(8,128)(2,1)S(1)} %pad_maximum_fusion) | copy-start | bytes 393220
  95.5 10.6 %collective-permute-start.7 = (bf16[4,32,512]{2,1,0:T(8,128)(2,1)S(1)}, bf16[4,32,512]{2,1,0:T(8,128)(2,1)S(1)}, u32[]{:S(2)}, u32[]{:S(2)}) collective-permute-start(bf16[4,32,512]{2,1,0:T(8,128)(2,1)S(1)} %pad_maximum_fusion), channel_id=1, source_target_pairs={{0,1},{1,0},{2,3},{3,2},{4,5},{5,4},{6,7},{7,6},{8,9},{9,8},{10,11... | collective-permute-start | bytes 393224 | tf_op jit(solution)/shard_map/ppermute | solution.py:451
  95.5 10.6 %collective-permute-start.8 = (bf16[4,32,512]{2,1,0:T(8,128)(2,1)S(1)}, bf16[4,32,512]{2,1,0:T(8,128)(2,1)S(1)}, u32[]{:S(2)}, u32[]{:S(2)}) collective-permute-start(bf16[4,32,512]{2,1,0:T(8,128)(2,1)S(1)} %pad_maximum_fusion), channel_id=1, source_target_pairs={{0,2},{1,3},{2,0},{3,1},{4,6},{5,7},{6,4},{7,5},{8,10},{9,11},{10,... | collective-permute-start | bytes 393224 | tf_op jit(solution)/shard_map/ppermute | solution.py:451
  96.0 10.1 %collective-permute-start.9 = (bf16[4,32,512]{2,1,0:T(8,128)(2,1)S(1)}, bf16[4,32,512]{2,1,0:T(8,128)(2,1)S(1)}, u32[]{:S(2)}, u32[]{:S(2)}) collective-permute-start(bf16[4,32,512]{2,1,0:T(8,128)(2,1)S(1)} %pad_maximum_fusion), channel_id=1, source_target_pairs={{0,3},{1,2},{2,1},{3,0},{4,7},{5,6},{6,5},{7,4},{8,11},{9,10},{10,... | collective-permute-start | bytes 393224 | tf_op jit(solution)/shard_map/ppermute | solution.py:451
  97.3 8.7 %collective-permute-start.6 = (bf16[120,512]{1,0:T(8,128)(2,1)S(1)}, bf16[120,512]{1,0:T(8,128)(2,1)S(1)}, u32[]{:S(2)}, u32[]{:S(2)}) collective-permute-start(bf16[120,512]{1,0:T(8,128)(2,1)S(1)} %get-tuple-element.63), channel_id=1, source_target_pairs={{0,8},{1,9},{2,10},{3,11},{4,12},{5,13},{6,14},{7,15},{8,0},{9,1},... | collective-permute-start | bytes 368648 | tf_op jit(solution)/shard_map/ppermute | solution.py:407
  106.0 0.7 copy-start.8
  106.0 0.7 copy-start.5
  106.1 0.8 copy-start.6
  106.1 0.8 copy-start.7

commit v3 on v2

--- a/solution.py
+++ b/solution.py
@@ -18,6 +18,7 @@
 MEBI = 1024 * 1024
 LIMIT = 62 * MEBI
 SMALL = 62 * MEBI
+STRIP = 58 * MEBI
 TURNS = 4
 CHAINS = 1
 
@@ -228,12 +229,12 @@
     copies = copies_in(list(zip(sources, held)), in_sem)
     copies[0].wait()
     copies[1].wait()
-    stage[0][...] = contract(fine_ref[...], l1_ref[...], 1, 0)
+    stage[0][...] = contract(fine_ref[...], l1_ref[...], 1, 0).astype(BF16)
     first = pltpu.make_async_copy(stage[0], outs[0], out_sem.at[0])
     first.start()
     copies[2].wait()
     copies[3].wait()
-    stage[1][...] = contract(cot_ref[...], join_ref[...], 1, 1)
+    stage[1][...] = contract(cot_ref[...], join_ref[...], 1, 1).astype(BF16)
     second = pltpu.make_async_copy(stage[1], outs[1], out_sem.at[1])
     second.start()
     first.wait()
@@ -248,10 +249,9 @@
 
 def strip_kernel(plan, turns, chains, core_ref, *refs):
     sent = 2 + 2 * chains
-    sources, outs, held = refs[:10], refs[10 : 10 + sent], refs[10 + sent : 20 + sent]
-    stage, refs = refs[20 + sent : 20 + 2 * sent], refs[20 + 2 * sent :]
-    arrived_ref, l2_ref, l3_ref, up_ref, down_ref = held[:5]
-    straight_ref, hidden_grad_ref, cot_ref, fine_ref, l1_ref = held[5:]
+    arrived_ref, sources, outs = refs[0], refs[1:10], refs[10 : 10 + sent]
+    held, stage, refs = refs[10 + sent : 19 + sent], refs[19 + sent : 19 + 2 * sent], refs[19 + 2 * sent :]
+    l2_ref, l3_ref, up_ref, down_ref, straight_ref, hidden_grad_ref, cot_ref, fine_ref, l1_ref = held
     grad_fine_ref, back_ref = stage[:2]
     coarse_ref, hidden_ref, joined_grad_ref = refs[:3]
     grad_refs = refs[3:6]
@@ -263,18 +263,18 @@
     window = down_ref.shape[2]
     total = cot_ref.shape[0]
     group = owners // turns
-    copies = copies_in(list(zip(sources[:5], held[:5])), in_sem)
+    copies = copies_in(list(zip(sources[:4], held[:4])), in_sem)
     turn_copies = []
     for turn in range(turns):
         many = pl.ds(turn * group * block, group * block)
         for which in (0, 1):
             copy = pltpu.make_async_copy(
-                sources[5 + which].at[many], held[5 + which].at[many], turn_sem.at[which, turn]
+                sources[4 + which].at[many], held[4 + which].at[many], turn_sem.at[which, turn]
             )
             copy.start()
             turn_copies.append(copy)
     late_copies = []
-    for index in (7, 8, 9):
+    for index in (6, 7, 8):
         copy = pltpu.make_async_copy(sources[index], held[index], in_sem.at[index - 2])
         copy.start()
         late_copies.append(copy)
@@ -284,7 +284,6 @@
         copy.start()
         return copy
 
-    copies[0].wait()
     features = [
         take_pieces(arrived_ref, plan.out_at[section], plan.out_width(section) // LANES, plan.counts[section])
         for section in range(3)
@@ -293,15 +292,15 @@
     for section in range(3):
         product = features[section]
         if section < 2:
-            copies[1 + section].wait()
+            copies[section].wait()
             product = contract(product, (l2_ref, l3_ref)[section][...], 1, 0).astype(BF16)
         projected.append(product.reshape(owners, plan.counts[section], width))
     tail = per_owner - sum(plan.counts)
     if tail:
         projected.append(jnp.zeros((owners, tail, width), BF16))
     coarse_ref[...] = jnp.concatenate(projected, axis=1).reshape(owners * per_owner, width)
+    copies[2].wait()
     copies[3].wait()
-    copies[4].wait()
 
     for turn in range(turns):
         turn_copies[2 * turn].wait()
@@ -310,14 +309,14 @@
             kind = 0 if owner == 0 else 2 if owner == owners - 1 else 1
             start = min(max(owner - 1, 0), owners - 3) * per_owner
             rows = slice(owner * block, (owner + 1) * block)
-            joined = straight_ref[rows, :] + contract(
+            joined = straight_ref[rows, :].astype(F32) + contract(
                 up_ref[kind], coarse_ref[start : start + reach, :], 1, 0
             )
             gate = 0.5 + 0.5 * jnp.tanh(0.5 * joined)
             hidden = joined * gate
             hidden_ref[rows, :] = hidden.astype(BF16)
             slope = gate + hidden * (1.0 - gate)
-            joined_grad_ref[rows, :] = (hidden_grad_ref[rows, :] * slope).astype(BF16)
+            joined_grad_ref[rows, :] = (hidden_grad_ref[rows, :].astype(F32) * slope).astype(BF16)
 
     for owner in range(owners):
         kind = 0 if owner == 0 else 2 if owner == owners - 1 else 1
@@ -356,23 +355,13 @@
 
 
 def finish_kernel(plan, chains, *refs):
-    count = (len(refs) - 6) // 2
-    sources, outs, held, sem_ref = refs[:count], refs[count : count + 5], refs[count + 5 : -1], refs[-1]
-    copies = copies_in(list(zip(sources, held)), sem_ref)
-    first = 2 * chains
-    for copy in copies[:first]:
-        copy.wait()
-    total = jnp.concatenate(
-        [held[2 * c][...].astype(F32) + held[2 * c + 1][...].astype(F32) for c in range(chains)]
-    )
+    sums, (slices_ref, *pieces), outs = refs[:chains], refs[chains:-5], refs[-5:]
+    total = jnp.concatenate([ref[...] for ref in sums])
     join_ref, two_ref, three_ref, one_ref, four_ref = outs
     at = 0
     for ref in (join_ref, two_ref, three_ref, one_ref):
         ref[...] = total[at : at + ref.shape[0]]
         at += ref.shape[0]
-    for copy in copies[first:]:
-        copy.wait()
-    slices_ref, pieces = held[first], held[first + 1 :]
     blocks = jnp.concatenate([piece[...] for piece in pieces])
     four_ref[...] = contract(slices_ref[...], blocks, 0, 0)[: four_ref.shape[0]]
 
@@ -515,15 +504,15 @@
     early = (lateral_one, fine, join_weight, cot)
     straight, hidden_grad = pl.pallas_call(
         ahead_kernel,
-        out_shape=(shape_of(total, width, dtype=F32),) * 2,
+        out_shape=(shape_of(total, width),) * 2,
         in_specs=[ANY] * 4,
         out_specs=(ANY,) * 2,
         scratch_shapes=[pltpu.VMEM(x.shape, BF16) for x in early]
-        + [pltpu.VMEM((total, width), F32)] * 2
+        + [pltpu.VMEM((total, width), BF16)] * 2
         + [pltpu.SemaphoreType.DMA((4,)), pltpu.SemaphoreType.DMA((2,))],
         compiler_params=pltpu.CompilerParams(vmem_limit_bytes=LIMIT),
         cost_estimate=pl.CostEstimate(
-            flops=4 * total * width * (width + c1), bytes_accessed=14_000_000, transcendentals=0
+            flops=4 * total * width * (width + c1), bytes_accessed=8_000_000, transcendentals=0
         ),
         name="ahead",
     )(*early)
@@ -544,9 +533,9 @@
     grad_fine, back, *halves = pl.pallas_call(
         functools.partial(strip_kernel, plan, TURNS, chains),
         out_shape=stage,
-        in_specs=[SMEM] + [ANY] * 10,
+        in_specs=[SMEM, VMEM] + [ANY] * 9,
         out_specs=(ANY,) * len(stage),
-        scratch_shapes=[pltpu.VMEM(x.shape, x.dtype) for x in operands + stage]
+        scratch_shapes=[pltpu.VMEM(x.shape, x.dtype) for x in operands[1:] + stage]
         + [
             pltpu.VMEM((owners * plan.per_owner, width), BF16),
             pltpu.VMEM((total, width), BF16),
@@ -556,10 +545,10 @@
         + [pltpu.VMEM((x, width), F32) for x in (width, *channels[:2], c1)]
         + [
             pltpu.SemaphoreType.DMA((len(stage),)),
-            pltpu.SemaphoreType.DMA((8,)),
+            pltpu.SemaphoreType.DMA((7,)),
             pltpu.SemaphoreType.DMA((2, TURNS)),
         ],
-        compiler_params=pltpu.CompilerParams(vmem_limit_bytes=LIMIT),
+        compiler_params=pltpu.CompilerParams(vmem_limit_bytes=STRIP),
         cost_estimate=pl.CostEstimate(
             flops=4_000_000_000, bytes_accessed=16_000_000, transcendentals=total * width
         ),
@@ -618,7 +607,9 @@
                 chain.values = value
     gathered = gather_level(gathered, levels[1])
 
-    operands = tuple(term for chain in rest for term in chain.terms)
+    sums = [keep.astype(F32) + received.astype(F32) for keep, received in (chain.terms for chain in rest)]
+    *sums, gathered = lax.optimization_barrier((*sums, gathered))
+    operands = tuple(sums)
     operands += (slices.reshape(-1, LANES), *[g.reshape(-1, width) for g in gathered])
     results = pl.pallas_call(
         functools.partial(finish_kernel, plan, chains),
@@ -626,11 +617,9 @@
             *[shape_of(height, width, dtype=F32) for height in heights],
             shape_of(plan.slice_width, width, dtype=F32),
         ),
-        in_specs=[ANY] * len(operands),
+        in_specs=[VMEM] * len(operands),
         out_specs=(VMEM,) * 5,
-        scratch_shapes=[pltpu.VMEM(x.shape, BF16) for x in operands]
-        + [pltpu.SemaphoreType.DMA((len(operands),))],
-        compiler_params=pltpu.CompilerParams(vmem_limit_bytes=LIMIT),
+        compiler_params=pltpu.CompilerParams(vmem_limit_bytes=16 * MEBI),
         name="finish",
     )(*operands)
     join_grad, two_grad, three_grad, one_grad, four_grad = results

time: 110 us -> 106 us (0.964)
  Pallas kernels: 26.8 us -> 25.2 us
  local copies, waits for them, and re-layouts: 7.76 us -> 6.37 us
    ppermute x4, waiting for transfers between devices: 10.4 us -> 6.71 us  [swap(): lax.ppermute(values, 'row', [(i, i ^ 1 << bit) for i in range(owners)])]
    ppermute x6, waiting for transfers between devices: 1.97 us -> 3.69 us  [gather_level(): lax.ppermute(stacked, 'row', [(i, i ^ d) for i in range(owners)])]
    pallas_call x1, Pallas kernels: 2.24 us -> 0.92 us  [body(): pl.pallas_call(functools.partial(finish_kernel, plan, chains), out_shape=...]
    unnamed x35 -> x27, local copies, waits for them, and re-layouts: 2.56 us -> 1.91 us
  transfers between devices with their start and end apart: 12 -> 12, of which waited for: 5 -> 6; matrix products, arithmetic and copies ran while one was open for 9% -> 9% of each run, Pallas kernels for 9% -> 8%
where the time goes in v3:
time: 106 us
  waiting for transfers between devices  43 us (41%)
  starting transfers between devices  25.9 us (24%)
  Pallas kernels  25.2 us (24%)
  local copies, waits for them, and re-layouts  6.37 us (6%)
  other arithmetic  4.29 us (4%)
    all_to_all x1, waiting for transfers between devices, body(): arrived = exchange(outgoing)  17.4 us
    all_to_all x1, waiting for transfers between devices, body(): returned = exchange(back)  15.2 us
    pallas_call x1, Pallas kernels, body(): pl.pallas_call(functools.partial(strip_kernel, plan, TURNS, chains), out_...  11 us
    all_to_all x1, starting transfers between devices, body(): arrived = exchange(outgoing)  7.58 us
    all_to_all x1, starting transfers between devices, body(): returned = exchange(back)  7.26 us
    ppermute x4, waiting for transfers between devices, swap(): lax.ppermute(values, 'row', [(i, i ^ 1 << bit) for i in range(owners)])  6.71 us
    ppermute x6, starting transfers between devices, gather_level(): lax.ppermute(stacked, 'row', [(i, i ^ d) for i in range(owners)])  6.25 us
    pallas_call x1, Pallas kernels, body(): pl.pallas_call(ahead_kernel, out_shape=(shape_of(total, width),) * 2, in_...  4.85 us
  transfers between devices with their start and end apart: 12, of which 6 were waited for; matrix products, arithmetic and copies ran while one was open for 9% of the time, Pallas kernels for 8%

profile of v3, /device:TPU:0, one launch (start us, length us, event | category | flops | bytes accessed | tf_op | source)
XLA Modules:
  0.0 105.8 jit_solution(10400092878989433685)
XLA Ops:
  0.6 4.3 %pack.1 = bf16[16,304,128]{2,1,0:T(8,128)(2,1)} custom-call(s32[16]{0:T(128)} %map_ref.1, bf16[512,384]{1,0:T(8,128)(2,1)} %bitcast.51, bf16[128,768]{1,0:T(8,128)(2,1)} %bitcast.52, bf16[32,1536]{1,0:T(8,128)(2,1)} %bitcast.53, bf16[1536,512]{1,0:T(8,128)(2,1)} %refs_4_.2), custom_call_target="tpu_custom_call" | custom-call | tf_op jit(solution)/shard_map/pack/pallas_call | solution.py:483
  4.9 0.0 copy-start.4
  4.9 0.0 copy-start.5
  4.9 0.0 copy-start.10
  5.0 0.0 copy-start.8
  5.0 0.0 copy-start.9
  5.0 0.0 copy-start.6
  5.0 0.0 copy-start.7
  5.0 0.0 copy-start.3
  5.0 7.6 %all-to-all-start = ((bf16[16,304,128]{2,1,0:T(8,128)(2,1)}), bf16[16,304,128]{2,1,0:T(8,128)(2,1)}, u32[]{:S(2)}, u32[]{:S(2)}) async-start(bf16[16,304,128]{2,1,0:T(8,128)(2,1)} %pack.1), calls=%async_computation | async-start | bytes 2490368 | tf_op jit(solution)/shard_map/all_to_all | solution.py:494
  12.6 0.0 copy-done.4
  12.6 0.0 copy-done.5
  12.7 0.1 clamp_add_fusion.2
  12.7 0.1 add.144
  12.8 0.1 clamp_add_fusion.1
  12.9 0.1 add.150
  13.0 0.1 clamp_add_fusion
  13.1 0.1 add.156
  13.2 1.8 %copy.36 = bf16[256,8,192]{2,1,0:T(8,128)(2,1)} copy(bf16[256,8,192]{0,2,1:T(8,128)(2,1)S(1)} %copy-done.3) | data formatting | bytes 1572864 | tf_op args[0]
  14.9 0.6 fusion.2.refs_2_
  15.6 1.1 %fusion.refs_1_ = bf16[512,768]{1,0:T(8,128)(2,1)} fusion(s32[768]{0:T(1024)S(1)} %add.144), kind=kLoop, calls=%fused_computation.3 | loop fusion | flops 786432 | bytes 789504 | tf_op jit(solution)/shard_map/convert_element_type | solution.py:129
  16.7 4.9 %ahead.1 = (bf16[2048,512]{1,0:T(8,128)(2,1)}, bf16[2048,512]{1,0:T(8,128)(2,1)}) custom-call(bf16[192,512]{1,0:T(8,128)(2,1)} %refs_9_.1, bf16[2048,192]{1,0:T(8,128)(2,1)} %bitcast.48, bf16[512,512]{1,0:T(8,128)(2,1)} %refs_2_.2, bf16[2048,512]{1,0:T(8,128)(2,1)} %bitcast.54), custom_call_target="tpu_custom_call" | custom-call | flops 2952790016 | bytes 8000000 | tf_op jit(solution)/shard_map/ahead/pallas_call | solution.py:505
  21.5 17.4 %all-to-all-done.refs_0_ = bf16[16,304,128]{2,1,0:T(8,128)(2,1)} async-done(((bf16[16,304,128]{2,1,0:T(8,128)(2,1)}), bf16[16,304,128]{2,1,0:T(8,128)(2,1)}, u32[]{:S(2)}, u32[]{:S(2)}) %all-to-all-start) | async-done | bytes 1245216 | tf_op jit(solution)/shard_map/all_to_all | solution.py:494
  38.9 11.0 %strip_work.1 = (bf16[2048,192]{1,0:T(8,128)(2,1)}, bf16[16,240,128]{2,1,0:T(8,128)(2,1)}, bf16[8,120,512]{2,1,0:T(8,128)(2,1)}, bf16[8,120,512]{2,1,0:T(8,128)(2,1)}) custom-call(s32[1]{0:T(128)} %bitcast.core_ref, bf16[16,304,128]{2,1,0:T(8,128)(2,1)} %all-to-all-done.refs_0_, bf16[384,512]{1,0:T(8,128)(2,1)} %refs_1_.1, bf16[768,512]{1,0:T(8,128)(2,1)} %refs_3_.4, ...), custom_call_target="tpu_custom_call" | custom-call | flops 4000000000 | bytes 16000000 | tf_op jit(solution)/shard_map/strip_work/pallas_call | solution.py:533
  50.0 0.0 copy-start.2
  50.0 0.9 collective-permute-start
  50.9 7.3 %all-to-all-start.1 = ((bf16[16,240,128]{2,1,0:T(8,128)(2,1)}), bf16[16,240,128]{2,1,0:T(8,128)(2,1)S(1)}, u32[]{:S(2)}, u32[]{:S(2)}) async-start(bf16[16,240,128]{2,1,0:T(8,128)(2,1)} %get-tuple-element.48), calls=%async_computation.1 | async-start | bytes 1966080 | tf_op jit(solution)/shard_map/all_to_all | solution.py:567
  58.1 0.0 collective-permute-done
  58.2 0.0 copy-done.2
  58.2 0.3 add_convert_fusion
  58.4 0.0 copy-start.11
  58.4 0.1 constant_dynamic-slice_fusion
  58.6 2.0 %collective-permute-start.1 = (bf16[2,2,120,512]{3,2,0,1:T(8,128)(2,1)S(1)}, bf16[2,2,120,512]{3,2,0,1:T(8,128)(2,1)S(1)}, u32[]{:S(2)}, u32[]{:S(2)}) collective-permute-start(bf16[2,2,120,512]{3,2,0,1:T(8,128)(2,1)S(1)} %bitcast.50), channel_id=1, source_target_pairs={{0,2},{1,3},{2,0},{3,1},{4,6},{5,7},{6,4},{7,5},{8,10},{9,11},{10,... | collective-permute-start | bytes 1474568 | tf_op jit(solution)/shard_map/ppermute | solution.py:396
  60.5 0.0 copy-done.11
  60.6 0.9 slice.3
  61.5 2.6 %copy.37 = bf16[256,8,192]{0,2,1:T(8,128)(2,1)} copy(bf16[256,8,192]{2,1,0:T(8,128)(2,1)} %bitcast.47) | data formatting | bytes 1572864 | tf_op jit(solution)/shard_map/reshape | solution.py:560
  64.1 0.6 gather_fusion
  64.7 0.1 broadcast_select_fusion
  64.8 15.2 %all-to-all-done.1.returned_ref.refs_0_ = bf16[16,240,128]{2,1,0:T(8,128)(2,1)S(1)} async-done(((bf16[16,240,128]{2,1,0:T(8,128)(2,1)}), bf16[16,240,128]{2,1,0:T(8,128)(2,1)S(1)}, u32[]{:S(2)}, u32[]{:S(2)}) %all-to-all-start.1) | async-done | bytes 983072 | tf_op jit(solution)/shard_map/all_to_all | solution.py:567
  80.0 0.1 fold_four.1.refs_5_
  80.2 0.0 copy-start.1
  80.2 2.1 %collective-permute-done.1 = bf16[2,2,120,512]{3,2,0,1:T(8,128)(2,1)S(1)} collective-permute-done((bf16[2,2,120,512]{3,2,0,1:T(8,128)(2,1)S(1)}, bf16[2,2,120,512]{3,2,0,1:T(8,128)(2,1)S(1)}, u32[]{:S(2)}, u32[]{:S(2)}) %collective-permute-start.1) | collective-permute-done | bytes 491552 | tf_op jit(solution)/shard_map/ppermute | solution.py:396
  82.3 0.1 add_convert_fusion.1
  82.5 1.4 %collective-permute-start.2 = (bf16[2,120,512]{2,1,0:T(8,128)(2,1)S(1)}, bf16[2,120,512]{2,1,0:T(8,128)(2,1)}, u32[]{:S(2)}, u32[]{:S(2)}) collective-permute-start(bf16[2,120,512]{2,1,0:T(8,128)(2,1)S(1)} %dynamic-slice_bitcast_fusion), channel_id=1, source_target_pairs={{0,4},{1,5},{2,6},{3,7},{4,0},{5,1},{6,2},{7,3},{8,12},{9,13},{10,... | collective-permute-start | bytes 737288 | tf_op jit(solution)/shard_map/ppermute | solution.py:396
  83.9 0.7 collective-permute-start.3
  84.6 2.6 %collective-permute-start.4 = (bf16[1,32,512]{2,1,0:T(8,128)(2,1)S(1)}, bf16[1,32,512]{2,1,0:T(8,128)(2,1)S(1)}, u32[]{:S(2)}, u32[]{:S(2)}) collective-permute-start(bf16[1,32,512]{2,1,0:T(8,128)(2,1)S(1)} %bitcast.39), channel_id=1, source_target_pairs={{0,8},{1,9},{2,10},{3,11},{4,12},{5,13},{6,14},{7,15},{8,0},{9,1},... | collective-permute-start | bytes 98312 | tf_op jit(solution)/shard_map/ppermute | solution.py:440
  87.1 1.1 %collective-permute-start.5 = (bf16[1,32,512]{2,1,0:T(8,128)(2,1)S(1)}, bf16[1,32,512]{2,1,0:T(8,128)(2,1)S(1)}, u32[]{:S(2)}, u32[]{:S(2)}) collective-permute-start(bf16[1,32,512]{2,1,0:T(8,128)(2,1)S(1)} %bitcast.40), channel_id=1, source_target_pairs={{0,12},{1,13},{2,14},{3,15},{4,8},{5,9},{6,10},{7,11},{8,4},{9,5},... | collective-permute-start | bytes 98312 | tf_op jit(solution)/shard_map/ppermute | solution.py:440
  88.3 0.0 copy-done.1
  88.3 4.0 %section_grads.1 = (bf16[512,384]{1,0:T(8,128)(2,1)}, bf16[128,768]{1,0:T(8,128)(2,1)}, bf16[32,1536]{1,0:T(8,128)(2,1)}) custom-call(bf16[16,240,128]{2,1,0:T(8,128)(2,1)} %copy-done, bf16[512,768]{1,0:T(8,128)(2,1)} %fusion.refs_1_, bf16[128,256]{1,0:T(8,128)(2,1)} %fusion.2.refs_2_, bf16[768,512]{1,0:T(8,128)(2,1)} %refs_3_.4, bf16[1536,512]{1,0:T(8,128)(2,1)} %refs_4_.2, ...), custom_call_target="tpu_custom_call" | custom-call | flops 500000000 | bytes 6000000 | tf_op jit(solution)/shard_map/section_grads/pallas_call | solution.py:582
  92.3 0.0 collective-permute-done.3
  92.3 0.0 collective-permute-done.4
  92.3 1.8 %collective-permute-done.5 = bf16[1,32,512]{2,1,0:T(8,128)(2,1)S(1)} collective-permute-done((bf16[1,32,512]{2,1,0:T(8,128)(2,1)S(1)}, bf16[1,32,512]{2,1,0:T(8,128)(2,1)S(1)}, u32[]{:S(2)}, u32[]{:S(2)}) %collective-permute-start.5) | collective-permute-done | bytes 32800 | tf_op jit(solution)/shard_map/ppermute | solution.py:440
  94.2 0.8 pad_maximum_fusion
  94.9 0.0 collective-permute-done.2
  95.0 1.0 fusion.1
  96.0 0.5 collective-permute-start.6
  96.5 0.0 collective-permute-start.7
  96.5 1.4 %collective-permute-start.8 = (bf16[4,32,512]{2,1,0:T(8,128)(2,1)S(1)}, bf16[4,32,512]{2,1,0:T(8,128)(2,1)S(1)}, u32[]{:S(2)}, u32[]{:S(2)}) collective-permute-start(bf16[4,32,512]{2,1,0:T(8,128)(2,1)S(1)} %pad_maximum_fusion), channel_id=1, source_target_pairs={{0,2},{1,3},{2,0},{3,1},{4,6},{5,7},{6,4},{7,5},{8,10},{9,11},{10,... | collective-permute-start | bytes 393224 | tf_op jit(solution)/shard_map/ppermute | solution.py:440
  97.9 0.4 collective-permute-start.9
  98.4 4.6 %collective-permute-done.6 = bf16[120,512]{1,0:T(8,128)(2,1)S(1)} collective-permute-done((bf16[120,512]{1,0:T(8,128)(2,1)S(1)}, bf16[120,512]{1,0:T(8,128)(2,1)S(1)}, u32[]{:S(2)}, u32[]{:S(2)}) %collective-permute-start.6) | collective-permute-done | bytes 122912 | tf_op jit(solution)/shard_map/ppermute | solution.py:396
  103.0 0.0 collective-permute-done.7
  103.0 0.0 collective-permute-done.8
  103.0 1.8 %collective-permute-done.9 = bf16[4,32,512]{2,1,0:T(8,128)(2,1)S(1)} collective-permute-done((bf16[4,32,512]{2,1,0:T(8,128)(2,1)S(1)}, bf16[4,32,512]{2,1,0:T(8,128)(2,1)S(1)}, u32[]{:S(2)}, u32[]{:S(2)}) %collective-permute-start.9) | collective-permute-done | bytes 131104 | tf_op jit(solution)/shard_map/ppermute | solution.py:440
  104.9 0.9 finish.1
  (17 shorter events, 0.2 us)
Async XLA Ops:
  4.9 7.7 %copy-start.4 = (s32[16]{0:T(128)S(1)}, s32[16]{0:T(128)}, u32[]{:S(2)}) copy-start(s32[16]{0:T(128)} %map_ref.1) | copy-start | bytes 196
  4.9 7.7 %copy-start.5 = (s32[48]{0:T(128)S(1)}, s32[48]{0:T(128)}, u32[]{:S(2)}) copy-start(s32[48]{0:T(128)} %constant.80.clone) | copy-start | bytes 580
  4.9 7.7 %copy-start.10 = (s32[48]{0:T(128)S(1)}, s32[48]{0:T(128)}, u32[]{:S(2)}) copy-start(s32[48]{0:T(128)} %constant.81.clone) | copy-start | bytes 580
  5.0 7.8 %copy-start.8 = (s32[16]{0:T(128)S(1)}, s32[16]{0:T(128)}, u32[]{:S(2)}) copy-start(s32[16]{0:T(128)} %constant.83.clone) | copy-start | bytes 196
  5.0 7.8 %copy-start.9 = (s32[16]{0:T(128)S(1)}, s32[16]{0:T(128)}, u32[]{:S(2)}) copy-start(s32[16]{0:T(128)} %constant.84.clone) | copy-start | bytes 196
  5.0 8.0 %copy-start.6 = (s32[8]{0:T(128)S(1)}, s32[8]{0:T(128)}, u32[]{:S(2)}) copy-start(s32[8]{0:T(128)} %constant.86.clone) | copy-start | bytes 100
  5.0 8.0 %copy-start.7 = (s32[8]{0:T(128)S(1)}, s32[8]{0:T(128)}, u32[]{:S(2)}) copy-start(s32[8]{0:T(128)} %constant.87.clone) | copy-start | bytes 100
  5.0 8.1 %copy-start.3 = (bf16[256,8,192]{0,2,1:T(8,128)(2,1)S(1)}, bf16[256,8,192]{0,2,1:T(8,128)(2,1)}, u32[]{:S(2)}) copy-start(bf16[256,8,192]{0,2,1:T(8,128)(2,1)} %param.23) | copy-start | bytes 2359300
  5.0 33.9 %all-to-all-start = ((bf16[16,304,128]{2,1,0:T(8,128)(2,1)}), bf16[16,304,128]{2,1,0:T(8,128)(2,1)}, u32[]{:S(2)}, u32[]{:S(2)}) async-start(bf16[16,304,128]{2,1,0:T(8,128)(2,1)} %pack.1), calls=%async_computation | async-start | bytes 2490368 | tf_op jit(solution)/shard_map/all_to_all | solution.py:494
  50.0 8.2 %copy-start.2 = (bf16[8,120,512]{2,1,0:T(8,128)(2,1)S(1)}, bf16[8,120,512]{2,1,0:T(8,128)(2,1)}, u32[]{:S(2)}) copy-start(bf16[8,120,512]{2,1,0:T(8,128)(2,1)} %get-tuple-element.51) | copy-start | bytes 2949124
  50.0 8.1 %collective-permute-start = (bf16[8,120,512]{2,1,0:T(8,128)(2,1)}, bf16[8,120,512]{2,1,0:T(8,128)(2,1)S(1)}, u32[]{:S(2)}, u32[]{:S(2)}) collective-permute-start(bf16[8,120,512]{2,1,0:T(8,128)(2,1)} %get-tuple-element.52), channel_id=1, source_target_pairs={{0,1},{1,0},{2,3},{3,2},{4,5},{5,4},{6,7},{7,6},{8,9},{9,8},{10,11... | collective-permute-start | bytes 2949128 | tf_op jit(solution)/shard_map/ppermute | solution.py:396
  50.9 29.2 %all-to-all-start.1 = ((bf16[16,240,128]{2,1,0:T(8,128)(2,1)}), bf16[16,240,128]{2,1,0:T(8,128)(2,1)S(1)}, u32[]{:S(2)}, u32[]{:S(2)}) async-start(bf16[16,240,128]{2,1,0:T(8,128)(2,1)} %get-tuple-element.48), calls=%async_computation.1 | async-start | bytes 1966080 | tf_op jit(solution)/shard_map/all_to_all | solution.py:567
  58.4 2.1 %copy-start.11 = (s32[16]{0:T(128)S(1)}, s32[16]{0:T(128)}, u32[]{:S(2)}) copy-start(s32[16]{0:T(128)} %constant.91.clone) | copy-start | bytes 196
  58.6 23.7 %collective-permute-start.1 = (bf16[2,2,120,512]{3,2,0,1:T(8,128)(2,1)S(1)}, bf16[2,2,120,512]{3,2,0,1:T(8,128)(2,1)S(1)}, u32[]{:S(2)}, u32[]{:S(2)}) collective-permute-start(bf16[2,2,120,512]{3,2,0,1:T(8,128)(2,1)S(1)} %bitcast.50), channel_id=1, source_target_pairs={{0,2},{1,3},{2,0},{3,1},{4,6},{5,7},{6,4},{7,5},{8,10},{9,11},{10,... | collective-permute-start | bytes 1474568 | tf_op jit(solution)/shard_map/ppermute | solution.py:396
  80.0 8.3 %copy-start = (bf16[16,240,128]{2,1,0:T(8,128)(2,1)}, bf16[16,240,128]{2,1,0:T(8,128)(2,1)S(1)}, u32[]{:S(2)}) copy-start(bf16[16,240,128]{2,1,0:T(8,128)(2,1)S(1)} %all-to-all-done.1.returned_ref.refs_0_) | copy-start | bytes 2949124
  80.2 8.1 %copy-start.1 = (bf16[32,512]{1,0:T(8,128)(2,1)}, bf16[32,512]{1,0:T(8,128)(2,1)S(1)}, u32[]{:S(2)}) copy-start(bf16[32,512]{1,0:T(8,128)(2,1)S(1)} %fold_four.1.refs_5_) | copy-start | bytes 98308
  82.5 12.5 %collective-permute-start.2 = (bf16[2,120,512]{2,1,0:T(8,128)(2,1)S(1)}, bf16[2,120,512]{2,1,0:T(8,128)(2,1)}, u32[]{:S(2)}, u32[]{:S(2)}) collective-permute-start(bf16[2,120,512]{2,1,0:T(8,128)(2,1)S(1)} %dynamic-slice_bitcast_fusion), channel_id=1, source_target_pairs={{0,4},{1,5},{2,6},{3,7},{4,0},{5,1},{6,2},{7,3},{8,12},{9,13},{10,... | collective-permute-start | bytes 737288 | tf_op jit(solution)/shard_map/ppermute | solution.py:396
  83.9 8.4 %collective-permute-start.3 = (bf16[1,32,512]{2,1,0:T(8,128)(2,1)S(1)}, bf16[1,32,512]{2,1,0:T(8,128)(2,1)S(1)}, u32[]{:S(2)}, u32[]{:S(2)}) collective-permute-start(bf16[1,32,512]{2,1,0:T(8,128)(2,1)S(1)} %bitcast.38), channel_id=1, source_target_pairs={{0,4},{1,5},{2,6},{3,7},{4,0},{5,1},{6,2},{7,3},{8,12},{9,13},{10,... | collective-permute-start | bytes 98312 | tf_op jit(solution)/shard_map/ppermute | solution.py:440
  84.6 7.7 %collective-permute-start.4 = (bf16[1,32,512]{2,1,0:T(8,128)(2,1)S(1)}, bf16[1,32,512]{2,1,0:T(8,128)(2,1)S(1)}, u32[]{:S(2)}, u32[]{:S(2)}) collective-permute-start(bf16[1,32,512]{2,1,0:T(8,128)(2,1)S(1)} %bitcast.39), channel_id=1, source_target_pairs={{0,8},{1,9},{2,10},{3,11},{4,12},{5,13},{6,14},{7,15},{8,0},{9,1},... | collective-permute-start | bytes 98312 | tf_op jit(solution)/shard_map/ppermute | solution.py:440
  87.1 7.0 %collective-permute-start.5 = (bf16[1,32,512]{2,1,0:T(8,128)(2,1)S(1)}, bf16[1,32,512]{2,1,0:T(8,128)(2,1)S(1)}, u32[]{:S(2)}, u32[]{:S(2)}) collective-permute-start(bf16[1,32,512]{2,1,0:T(8,128)(2,1)S(1)} %bitcast.40), channel_id=1, source_target_pairs={{0,12},{1,13},{2,14},{3,15},{4,8},{5,9},{6,10},{7,11},{8,4},{9,5},... | collective-permute-start | bytes 98312 | tf_op jit(solution)/shard_map/ppermute | solution.py:440
  96.0 7.0 %collective-permute-start.6 = (bf16[120,512]{1,0:T(8,128)(2,1)S(1)}, bf16[120,512]{1,0:T(8,128)(2,1)S(1)}, u32[]{:S(2)}, u32[]{:S(2)}) collective-permute-start(bf16[120,512]{1,0:T(8,128)(2,1)S(1)} %dynamic-slice_bitcast_fusion.1), channel_id=1, source_target_pairs={{0,8},{1,9},{2,10},{3,11},{4,12},{5,13},{6,14},{7,15},{8,0},{9,1},... | collective-permute-start | bytes 368648 | tf_op jit(solution)/shard_map/ppermute | solution.py:396
  96.5 6.5 %collective-permute-start.7 = (bf16[4,32,512]{2,1,0:T(8,128)(2,1)S(1)}, bf16[4,32,512]{2,1,0:T(8,128)(2,1)S(1)}, u32[]{:S(2)}, u32[]{:S(2)}) collective-permute-start(bf16[4,32,512]{2,1,0:T(8,128)(2,1)S(1)} %pad_maximum_fusion), channel_id=1, source_target_pairs={{0,1},{1,0},{2,3},{3,2},{4,5},{5,4},{6,7},{7,6},{8,9},{9,8},{10,11... | collective-permute-start | bytes 393224 | tf_op jit(solution)/shard_map/ppermute | solution.py:440
  96.5 6.5 %collective-permute-start.8 = (bf16[4,32,512]{2,1,0:T(8,128)(2,1)S(1)}, bf16[4,32,512]{2,1,0:T(8,128)(2,1)S(1)}, u32[]{:S(2)}, u32[]{:S(2)}) collective-permute-start(bf16[4,32,512]{2,1,0:T(8,128)(2,1)S(1)} %pad_maximum_fusion), channel_id=1, source_target_pairs={{0,2},{1,3},{2,0},{3,1},{4,6},{5,7},{6,4},{7,5},{8,10},{9,11},{10,... | collective-permute-start | bytes 393224 | tf_op jit(solution)/shard_map/ppermute | solution.py:440
  97.9 6.9 %collective-permute-start.9 = (bf16[4,32,512]{2,1,0:T(8,128)(2,1)S(1)}, bf16[4,32,512]{2,1,0:T(8,128)(2,1)S(1)}, u32[]{:S(2)}, u32[]{:S(2)}) collective-permute-start(bf16[4,32,512]{2,1,0:T(8,128)(2,1)S(1)} %pad_maximum_fusion), channel_id=1, source_target_pairs={{0,3},{1,2},{2,1},{3,0},{4,7},{5,6},{6,5},{7,4},{8,11},{9,10},{10,... | collective-permute-start | bytes 393224 | tf_op jit(solution)/shard_map/ppermute | solution.py:440

commit v4 on v3

--- a/solution.py
+++ b/solution.py
@@ -436,8 +436,13 @@
 
 def gather_level(stacked, level):
     owners = lax.axis_size("row")
-    distances = level_swaps(level)[1:]
-    return [stacked] + [lax.ppermute(stacked, "row", [(i, i ^ d) for i in range(owners)]) for d in distances]
+    blocks = {0: stacked}
+    for d in level_swaps(level)[1:]:
+        if d > 1 and d % 2 == 1:
+            blocks[d] = swap(blocks[d - 1], 0)
+        else:
+            blocks[d] = lax.ppermute(stacked, "row", [(i, i ^ d) for i in range(owners)])
+    return list(blocks.values())
 
 
 def gather_pattern(levels):

time: 106 us -> 105 us (level)
    ppermute x4 -> x5, waiting for transfers between devices: 6.71 us -> 4.72 us  [swap(): lax.ppermute(values, 'row', [(i, i ^ 1 << bit) for i in range(owners)])]
    ppermute x6 -> x5, starting transfers between devices: 6.25 us -> 4.94 us  [gather_level(): lax.ppermute(stacked, 'row', [(i, i ^ d) for i in range(owners)])]
    ppermute x6 -> x5, waiting for transfers between devices: 3.69 us -> 4.95 us  [gather_level(): lax.ppermute(stacked, 'row', [(i, i ^ d) for i in range(owners)])]
    ppermute x4 -> x5, starting transfers between devices: 4.78 us -> 5.64 us  [swap(): lax.ppermute(values, 'row', [(i, i ^ 1 << bit) for i in range(owners)])]
  transfers between devices with their start and end apart: 12 -> 12, of which waited for: 6 -> 6; matrix products, arithmetic and copies ran while one was open for 9% -> 9% of each run, Pallas kernels for 8% -> 9%
where the time goes in v4:
time: 105 us
  waiting for transfers between devices  42.3 us (40%)
  starting transfers between devices  25.4 us (24%)
  Pallas kernels  25.2 us (24%)
  local copies, waits for them, and re-layouts  6.37 us (6%)
  other arithmetic  4.29 us (4%)
    all_to_all x1, waiting for transfers between devices, body(): arrived = exchange(outgoing)  17.4 us
    all_to_all x1, waiting for transfers between devices, body(): returned = exchange(back)  15.2 us
    pallas_call x1, Pallas kernels, body(): pl.pallas_call(functools.partial(strip_kernel, plan, TURNS, chains), out_...  11 us
    all_to_all x1, starting transfers between devices, body(): arrived = exchange(outgoing)  7.58 us
    all_to_all x1, starting transfers between devices, body(): returned = exchange(back)  7.26 us
    ppermute x5, starting transfers between devices, swap(): lax.ppermute(values, 'row', [(i, i ^ 1 << bit) for i in range(owners)])  5.64 us
    ppermute x5, waiting for transfers between devices, gather_level(): lax.ppermute(stacked, 'row', [(i, i ^ d) for i in range(owners)])  4.95 us
    ppermute x5, starting transfers between devices, gather_level(): lax.ppermute(stacked, 'row', [(i, i ^ d) for i in range(owners)])  4.94 us
  transfers between devices with their start and end apart: 12, of which 6 were waited for; matrix products, arithmetic and copies ran while one was open for 9% of the time, Pallas kernels for 9%

profile of v4, /device:TPU:0, one launch (start us, length us, event | category | flops | bytes accessed | tf_op | source)
XLA Modules:
  0.0 104.6 jit_solution(11635610877095162538)
XLA Ops:
  0.6 4.3 %pack.1 = bf16[16,304,128]{2,1,0:T(8,128)(2,1)} custom-call(s32[16]{0:T(128)} %map_ref.1, bf16[512,384]{1,0:T(8,128)(2,1)} %bitcast.51, bf16[128,768]{1,0:T(8,128)(2,1)} %bitcast.52, bf16[32,1536]{1,0:T(8,128)(2,1)} %bitcast.53, bf16[1536,512]{1,0:T(8,128)(2,1)} %refs_4_.2), custom_call_target="tpu_custom_call" | custom-call | tf_op jit(solution)/shard_map/pack/pallas_call | solution.py:488
  4.9 0.0 copy-start.4
  4.9 0.0 copy-start.5
  4.9 0.0 copy-start.10
  5.0 0.0 copy-start.8
  5.0 0.0 copy-start.9
  5.0 0.0 copy-start.6
  5.0 0.0 copy-start.7
  5.0 0.0 copy-start.3
  5.0 7.6 %all-to-all-start = ((bf16[16,304,128]{2,1,0:T(8,128)(2,1)}), bf16[16,304,128]{2,1,0:T(8,128)(2,1)}, u32[]{:S(2)}, u32[]{:S(2)}) async-start(bf16[16,304,128]{2,1,0:T(8,128)(2,1)} %pack.1), calls=%async_computation | async-start | bytes 2490368 | tf_op jit(solution)/shard_map/all_to_all | solution.py:499
  12.6 0.0 copy-done.4
  12.6 0.0 copy-done.5
  12.6 0.0 copy-done.10
  12.7 0.1 clamp_add_fusion.2
  12.7 0.1 add.144
  12.8 0.0 copy-done.8
  12.8 0.0 copy-done.9
  12.8 0.1 clamp_add_fusion.1
  12.9 0.1 add.150
  13.0 0.1 clamp_add_fusion
  13.1 0.1 add.156
  13.2 1.8 %copy.36 = bf16[256,8,192]{2,1,0:T(8,128)(2,1)} copy(bf16[256,8,192]{0,2,1:T(8,128)(2,1)S(1)} %copy-done.3) | data formatting | bytes 1572864 | tf_op args[0]
  14.9 0.6 fusion.2.refs_2_
  15.6 1.1 %fusion.refs_1_ = bf16[512,768]{1,0:T(8,128)(2,1)} fusion(s32[768]{0:T(1024)S(1)} %add.144), kind=kLoop, calls=%fused_computation.3 | loop fusion | flops 786432 | bytes 789504 | tf_op jit(solution)/shard_map/convert_element_type | solution.py:129
  16.7 4.9 %ahead.1 = (bf16[2048,512]{1,0:T(8,128)(2,1)}, bf16[2048,512]{1,0:T(8,128)(2,1)}) custom-call(bf16[192,512]{1,0:T(8,128)(2,1)} %refs_9_.1, bf16[2048,192]{1,0:T(8,128)(2,1)} %bitcast.48, bf16[512,512]{1,0:T(8,128)(2,1)} %refs_2_.2, bf16[2048,512]{1,0:T(8,128)(2,1)} %bitcast.54), custom_call_target="tpu_custom_call" | custom-call | flops 2952790016 | bytes 8000000 | tf_op jit(solution)/shard_map/ahead/pallas_call | solution.py:510
  21.5 17.4 %all-to-all-done.refs_0_ = bf16[16,304,128]{2,1,0:T(8,128)(2,1)} async-done(((bf16[16,304,128]{2,1,0:T(8,128)(2,1)}), bf16[16,304,128]{2,1,0:T(8,128)(2,1)}, u32[]{:S(2)}, u32[]{:S(2)}) %all-to-all-start) | async-done | bytes 1245216 | tf_op jit(solution)/shard_map/all_to_all | solution.py:499
  38.9 11.0 %strip_work.1 = (bf16[2048,192]{1,0:T(8,128)(2,1)}, bf16[16,240,128]{2,1,0:T(8,128)(2,1)}, bf16[8,120,512]{2,1,0:T(8,128)(2,1)}, bf16[8,120,512]{2,1,0:T(8,128)(2,1)}) custom-call(s32[1]{0:T(128)} %bitcast.core_ref, bf16[16,304,128]{2,1,0:T(8,128)(2,1)} %all-to-all-done.refs_0_, bf16[384,512]{1,0:T(8,128)(2,1)} %refs_1_.1, bf16[768,512]{1,0:T(8,128)(2,1)} %refs_3_.4, ...), custom_call_target="tpu_custom_call" | custom-call | flops 4000000000 | bytes 16000000 | tf_op jit(solution)/shard_map/strip_work/pallas_call | solution.py:538
  50.0 0.9 collective-permute-start
  50.9 7.3 %all-to-all-start.1 = ((bf16[16,240,128]{2,1,0:T(8,128)(2,1)}), bf16[16,240,128]{2,1,0:T(8,128)(2,1)S(1)}, u32[]{:S(2)}, u32[]{:S(2)}) async-start(bf16[16,240,128]{2,1,0:T(8,128)(2,1)} %get-tuple-element.48), calls=%async_computation.1 | async-start | bytes 1966080 | tf_op jit(solution)/shard_map/all_to_all | solution.py:572
  58.1 0.0 collective-permute-done
  58.2 0.3 add_convert_fusion
  58.4 0.0 copy-start.11
  58.4 0.1 constant_dynamic-slice_fusion
  58.6 2.0 %collective-permute-start.1 = (bf16[2,2,120,512]{3,2,0,1:T(8,128)(2,1)S(1)}, bf16[2,2,120,512]{3,2,0,1:T(8,128)(2,1)S(1)}, u32[]{:S(2)}, u32[]{:S(2)}) collective-permute-start(bf16[2,2,120,512]{3,2,0,1:T(8,128)(2,1)S(1)} %bitcast.50), channel_id=1, source_target_pairs={{0,2},{1,3},{2,0},{3,1},{4,6},{5,7},{6,4},{7,5},{8,10},{9,11},{10,... | collective-permute-start | bytes 1474568 | tf_op jit(solution)/shard_map/ppermute | solution.py:396
  60.6 0.9 slice.3
  61.5 2.6 %copy.37 = bf16[256,8,192]{0,2,1:T(8,128)(2,1)} copy(bf16[256,8,192]{2,1,0:T(8,128)(2,1)} %bitcast.47) | data formatting | bytes 1572864 | tf_op jit(solution)/shard_map/reshape | solution.py:565
  64.1 0.6 gather_fusion
  64.7 0.1 broadcast_select_fusion
  64.8 15.2 %all-to-all-done.1.returned_ref.refs_0_ = bf16[16,240,128]{2,1,0:T(8,128)(2,1)S(1)} async-done(((bf16[16,240,128]{2,1,0:T(8,128)(2,1)}), bf16[16,240,128]{2,1,0:T(8,128)(2,1)S(1)}, u32[]{:S(2)}, u32[]{:S(2)}) %all-to-all-start.1) | async-done | bytes 983072 | tf_op jit(solution)/shard_map/all_to_all | solution.py:572
  80.0 0.1 fold_four.1.refs_5_
  80.2 0.0 copy-start.1
  80.2 2.1 %collective-permute-done.1 = bf16[2,2,120,512]{3,2,0,1:T(8,128)(2,1)S(1)} collective-permute-done((bf16[2,2,120,512]{3,2,0,1:T(8,128)(2,1)S(1)}, bf16[2,2,120,512]{3,2,0,1:T(8,128)(2,1)S(1)}, u32[]{:S(2)}, u32[]{:S(2)}) %collective-permute-start.1) | collective-permute-done | bytes 491552 | tf_op jit(solution)/shard_map/ppermute | solution.py:396
  82.3 0.1 add_convert_fusion.1
  82.5 1.4 %collective-permute-start.2 = (bf16[2,120,512]{2,1,0:T(8,128)(2,1)S(1)}, bf16[2,120,512]{2,1,0:T(8,128)(2,1)}, u32[]{:S(2)}, u32[]{:S(2)}) collective-permute-start(bf16[2,120,512]{2,1,0:T(8,128)(2,1)S(1)} %dynamic-slice_bitcast_fusion), channel_id=1, source_target_pairs={{0,4},{1,5},{2,6},{3,7},{4,0},{5,1},{6,2},{7,3},{8,12},{9,13},{10,... | collective-permute-start | bytes 737288 | tf_op jit(solution)/shard_map/ppermute | solution.py:396
  83.9 0.7 collective-permute-start.3
  84.6 2.6 %collective-permute-start.4 = (bf16[1,32,512]{2,1,0:T(8,128)(2,1)S(1)}, bf16[1,32,512]{2,1,0:T(8,128)(2,1)S(1)}, u32[]{:S(2)}, u32[]{:S(2)}) collective-permute-start(bf16[1,32,512]{2,1,0:T(8,128)(2,1)S(1)} %bitcast.39), channel_id=1, source_target_pairs={{0,8},{1,9},{2,10},{3,11},{4,12},{5,13},{6,14},{7,15},{8,0},{9,1},... | collective-permute-start | bytes 98312 | tf_op jit(solution)/shard_map/ppermute | solution.py:444
  87.1 1.1 %collective-permute-start.5 = (bf16[1,32,512]{2,1,0:T(8,128)(2,1)S(1)}, bf16[1,32,512]{2,1,0:T(8,128)(2,1)S(1)}, u32[]{:S(2)}, u32[]{:S(2)}) collective-permute-start(bf16[1,32,512]{2,1,0:T(8,128)(2,1)S(1)} %bitcast.40), channel_id=1, source_target_pairs={{0,12},{1,13},{2,14},{3,15},{4,8},{5,9},{6,10},{7,11},{8,4},{9,5},... | collective-permute-start | bytes 98312 | tf_op jit(solution)/shard_map/ppermute | solution.py:444
  88.3 0.0 copy-done
  88.3 4.0 %section_grads.1 = (bf16[512,384]{1,0:T(8,128)(2,1)}, bf16[128,768]{1,0:T(8,128)(2,1)}, bf16[32,1536]{1,0:T(8,128)(2,1)}) custom-call(bf16[16,240,128]{2,1,0:T(8,128)(2,1)} %copy-done, bf16[512,768]{1,0:T(8,128)(2,1)} %fusion.refs_1_, bf16[128,256]{1,0:T(8,128)(2,1)} %fusion.2.refs_2_, bf16[768,512]{1,0:T(8,128)(2,1)} %refs_3_.4, bf16[1536,512]{1,0:T(8,128)(2,1)} %refs_4_.2, ...), custom_call_target="tpu_custom_call" | custom-call | flops 500000000 | bytes 6000000 | tf_op jit(solution)/shard_map/section_grads/pallas_call | solution.py:587
  92.3 0.0 collective-permute-done.3
  92.3 0.0 collective-permute-done.4
  92.3 1.8 %collective-permute-done.5 = bf16[1,32,512]{2,1,0:T(8,128)(2,1)S(1)} collective-permute-done((bf16[1,32,512]{2,1,0:T(8,128)(2,1)S(1)}, bf16[1,32,512]{2,1,0:T(8,128)(2,1)S(1)}, u32[]{:S(2)}, u32[]{:S(2)}) %collective-permute-start.5) | collective-permute-done | bytes 32800 | tf_op jit(solution)/shard_map/ppermute | solution.py:444
  94.2 0.8 pad_maximum_fusion
  94.9 0.0 collective-permute-done.2
  95.0 1.0 fusion.1
  96.0 0.6 collective-permute-start.8
  96.5 1.4 %collective-permute-start.6 = (bf16[120,512]{1,0:T(8,128)(2,1)S(1)}, bf16[120,512]{1,0:T(8,128)(2,1)S(1)}, u32[]{:S(2)}, u32[]{:S(2)}) collective-permute-start(bf16[120,512]{1,0:T(8,128)(2,1)S(1)} %dynamic-slice_bitcast_fusion.1), channel_id=1, source_target_pairs={{0,8},{1,9},{2,10},{3,11},{4,12},{5,13},{6,14},{7,15},{8,0},{9,1},... | collective-permute-start | bytes 368648 | tf_op jit(solution)/shard_map/ppermute | solution.py:396
  97.9 0.0 collective-permute-start.7
  97.9 3.1 %collective-permute-done.8 = bf16[4,32,512]{2,1,0:T(8,128)(2,1)S(1)} collective-permute-done((bf16[4,32,512]{2,1,0:T(8,128)(2,1)S(1)}, bf16[4,32,512]{2,1,0:T(8,128)(2,1)S(1)}, u32[]{:S(2)}, u32[]{:S(2)}) %collective-permute-start.8) | collective-permute-done | bytes 131104 | tf_op jit(solution)/shard_map/ppermute | solution.py:444
  101.0 0.0 collective-permute-start.9
  101.0 2.6 %collective-permute-done.6 = bf16[120,512]{1,0:T(8,128)(2,1)S(1)} collective-permute-done((bf16[120,512]{1,0:T(8,128)(2,1)S(1)}, bf16[120,512]{1,0:T(8,128)(2,1)S(1)}, u32[]{:S(2)}, u32[]{:S(2)}) %collective-permute-start.6) | collective-permute-done | bytes 122912 | tf_op jit(solution)/shard_map/ppermute | solution.py:396
  103.6 0.0 collective-permute-done.7
  103.7 0.0 collective-permute-done.9
  103.7 0.9 finish.1
  (17 shorter events, 0.2 us)
Async XLA Ops:
  4.9 7.7 %copy-start.4 = (s32[16]{0:T(128)S(1)}, s32[16]{0:T(128)}, u32[]{:S(2)}) copy-start(s32[16]{0:T(128)} %map_ref.1) | copy-start | bytes 196
  4.9 7.7 %copy-start.5 = (s32[48]{0:T(128)S(1)}, s32[48]{0:T(128)}, u32[]{:S(2)}) copy-start(s32[48]{0:T(128)} %constant.80.clone) | copy-start | bytes 580
  4.9 7.7 %copy-start.10 = (s32[48]{0:T(128)S(1)}, s32[48]{0:T(128)}, u32[]{:S(2)}) copy-start(s32[48]{0:T(128)} %constant.81.clone) | copy-start | bytes 580
  5.0 7.8 %copy-start.8 = (s32[16]{0:T(128)S(1)}, s32[16]{0:T(128)}, u32[]{:S(2)}) copy-start(s32[16]{0:T(128)} %constant.83.clone) | copy-start | bytes 196
  5.0 7.8 %copy-start.9 = (s32[16]{0:T(128)S(1)}, s32[16]{0:T(128)}, u32[]{:S(2)}) copy-start(s32[16]{0:T(128)} %constant.84.clone) | copy-start | bytes 196
  5.0 8.0 %copy-start.6 = (s32[8]{0:T(128)S(1)}, s32[8]{0:T(128)}, u32[]{:S(2)}) copy-start(s32[8]{0:T(128)} %constant.86.clone) | copy-start | bytes 100
  5.0 8.0 %copy-start.7 = (s32[8]{0:T(128)S(1)}, s32[8]{0:T(128)}, u32[]{:S(2)}) copy-start(s32[8]{0:T(128)} %constant.87.clone) | copy-start | bytes 100
  5.0 8.1 %copy-start.3 = (bf16[256,8,192]{0,2,1:T(8,128)(2,1)S(1)}, bf16[256,8,192]{0,2,1:T(8,128)(2,1)}, u32[]{:S(2)}) copy-start(bf16[256,8,192]{0,2,1:T(8,128)(2,1)} %param.23) | copy-start | bytes 2359300
  5.0 33.9 %all-to-all-start = ((bf16[16,304,128]{2,1,0:T(8,128)(2,1)}), bf16[16,304,128]{2,1,0:T(8,128)(2,1)}, u32[]{:S(2)}, u32[]{:S(2)}) async-start(bf16[16,304,128]{2,1,0:T(8,128)(2,1)} %pack.1), calls=%async_computation | async-start | bytes 2490368 | tf_op jit(solution)/shard_map/all_to_all | solution.py:499
  50.0 8.2 %copy-start.2 = (bf16[8,120,512]{2,1,0:T(8,128)(2,1)S(1)}, bf16[8,120,512]{2,1,0:T(8,128)(2,1)}, u32[]{:S(2)}) copy-start(bf16[8,120,512]{2,1,0:T(8,128)(2,1)} %get-tuple-element.51) | copy-start | bytes 2949124
  50.0 8.1 %collective-permute-start = (bf16[8,120,512]{2,1,0:T(8,128)(2,1)}, bf16[8,120,512]{2,1,0:T(8,128)(2,1)S(1)}, u32[]{:S(2)}, u32[]{:S(2)}) collective-permute-start(bf16[8,120,512]{2,1,0:T(8,128)(2,1)} %get-tuple-element.52), channel_id=1, source_target_pairs={{0,1},{1,0},{2,3},{3,2},{4,5},{5,4},{6,7},{7,6},{8,9},{9,8},{10,11... | collective-permute-start | bytes 2949128 | tf_op jit(solution)/shard_map/ppermute | solution.py:396
  50.9 29.2 %all-to-all-start.1 = ((bf16[16,240,128]{2,1,0:T(8,128)(2,1)}), bf16[16,240,128]{2,1,0:T(8,128)(2,1)S(1)}, u32[]{:S(2)}, u32[]{:S(2)}) async-start(bf16[16,240,128]{2,1,0:T(8,128)(2,1)} %get-tuple-element.48), calls=%async_computation.1 | async-start | bytes 1966080 | tf_op jit(solution)/shard_map/all_to_all | solution.py:572
  58.4 2.1 %copy-start.11 = (s32[16]{0:T(128)S(1)}, s32[16]{0:T(128)}, u32[]{:S(2)}) copy-start(s32[16]{0:T(128)} %constant.91.clone) | copy-start | bytes 196
  58.6 23.7 %collective-permute-start.1 = (bf16[2,2,120,512]{3,2,0,1:T(8,128)(2,1)S(1)}, bf16[2,2,120,512]{3,2,0,1:T(8,128)(2,1)S(1)}, u32[]{:S(2)}, u32[]{:S(2)}) collective-permute-start(bf16[2,2,120,512]{3,2,0,1:T(8,128)(2,1)S(1)} %bitcast.50), channel_id=1, source_target_pairs={{0,2},{1,3},{2,0},{3,1},{4,6},{5,7},{6,4},{7,5},{8,10},{9,11},{10,... | collective-permute-start | bytes 1474568 | tf_op jit(solution)/shard_map/ppermute | solution.py:396
  80.0 8.3 %copy-start = (bf16[16,240,128]{2,1,0:T(8,128)(2,1)}, bf16[16,240,128]{2,1,0:T(8,128)(2,1)S(1)}, u32[]{:S(2)}) copy-start(bf16[16,240,128]{2,1,0:T(8,128)(2,1)S(1)} %all-to-all-done.1.returned_ref.refs_0_) | copy-start | bytes 2949124
  80.2 8.1 %copy-start.1 = (bf16[32,512]{1,0:T(8,128)(2,1)}, bf16[32,512]{1,0:T(8,128)(2,1)S(1)}, u32[]{:S(2)}) copy-start(bf16[32,512]{1,0:T(8,128)(2,1)S(1)} %fold_four.1.refs_5_) | copy-start | bytes 98308
  82.5 12.5 %collective-permute-start.2 = (bf16[2,120,512]{2,1,0:T(8,128)(2,1)S(1)}, bf16[2,120,512]{2,1,0:T(8,128)(2,1)}, u32[]{:S(2)}, u32[]{:S(2)}) collective-permute-start(bf16[2,120,512]{2,1,0:T(8,128)(2,1)S(1)} %dynamic-slice_bitcast_fusion), channel_id=1, source_target_pairs={{0,4},{1,5},{2,6},{3,7},{4,0},{5,1},{6,2},{7,3},{8,12},{9,13},{10,... | collective-permute-start | bytes 737288 | tf_op jit(solution)/shard_map/ppermute | solution.py:396
  83.9 8.4 %collective-permute-start.3 = (bf16[1,32,512]{2,1,0:T(8,128)(2,1)S(1)}, bf16[1,32,512]{2,1,0:T(8,128)(2,1)S(1)}, u32[]{:S(2)}, u32[]{:S(2)}) collective-permute-start(bf16[1,32,512]{2,1,0:T(8,128)(2,1)S(1)} %bitcast.38), channel_id=1, source_target_pairs={{0,4},{1,5},{2,6},{3,7},{4,0},{5,1},{6,2},{7,3},{8,12},{9,13},{10,... | collective-permute-start | bytes 98312 | tf_op jit(solution)/shard_map/ppermute | solution.py:444
  84.6 7.7 %collective-permute-start.4 = (bf16[1,32,512]{2,1,0:T(8,128)(2,1)S(1)}, bf16[1,32,512]{2,1,0:T(8,128)(2,1)S(1)}, u32[]{:S(2)}, u32[]{:S(2)}) collective-permute-start(bf16[1,32,512]{2,1,0:T(8,128)(2,1)S(1)} %bitcast.39), channel_id=1, source_target_pairs={{0,8},{1,9},{2,10},{3,11},{4,12},{5,13},{6,14},{7,15},{8,0},{9,1},... | collective-permute-start | bytes 98312 | tf_op jit(solution)/shard_map/ppermute | solution.py:444
  87.1 7.0 %collective-permute-start.5 = (bf16[1,32,512]{2,1,0:T(8,128)(2,1)S(1)}, bf16[1,32,512]{2,1,0:T(8,128)(2,1)S(1)}, u32[]{:S(2)}, u32[]{:S(2)}) collective-permute-start(bf16[1,32,512]{2,1,0:T(8,128)(2,1)S(1)} %bitcast.40), channel_id=1, source_target_pairs={{0,12},{1,13},{2,14},{3,15},{4,8},{5,9},{6,10},{7,11},{8,4},{9,5},... | collective-permute-start | bytes 98312 | tf_op jit(solution)/shard_map/ppermute | solution.py:444
  96.0 5.0 %collective-permute-start.8 = (bf16[4,32,512]{2,1,0:T(8,128)(2,1)S(1)}, bf16[4,32,512]{2,1,0:T(8,128)(2,1)S(1)}, u32[]{:S(2)}, u32[]{:S(2)}) collective-permute-start(bf16[4,32,512]{2,1,0:T(8,128)(2,1)S(1)} %pad_maximum_fusion), channel_id=1, source_target_pairs={{0,2},{1,3},{2,0},{3,1},{4,6},{5,7},{6,4},{7,5},{8,10},{9,11},{10,... | collective-permute-start | bytes 393224 | tf_op jit(solution)/shard_map/ppermute | solution.py:444
  96.5 7.1 %collective-permute-start.6 = (bf16[120,512]{1,0:T(8,128)(2,1)S(1)}, bf16[120,512]{1,0:T(8,128)(2,1)S(1)}, u32[]{:S(2)}, u32[]{:S(2)}) collective-permute-start(bf16[120,512]{1,0:T(8,128)(2,1)S(1)} %dynamic-slice_bitcast_fusion.1), channel_id=1, source_target_pairs={{0,8},{1,9},{2,10},{3,11},{4,12},{5,13},{6,14},{7,15},{8,0},{9,1},... | collective-permute-start | bytes 368648 | tf_op jit(solution)/shard_map/ppermute | solution.py:396
  97.9 5.7 %collective-permute-start.7 = (bf16[4,32,512]{2,1,0:T(8,128)(2,1)S(1)}, bf16[4,32,512]{2,1,0:T(8,128)(2,1)S(1)}, u32[]{:S(2)}, u32[]{:S(2)}) collective-permute-start(bf16[4,32,512]{2,1,0:T(8,128)(2,1)S(1)} %pad_maximum_fusion), channel_id=1, source_target_pairs={{0,1},{1,0},{2,3},{3,2},{4,5},{5,4},{6,7},{7,6},{8,9},{9,8},{10,11... | collective-permute-start | bytes 393224 | tf_op jit(solution)/shard_map/ppermute | solution.py:444
  101.0 2.6 %collective-permute-start.9 = (bf16[4,32,512]{2,1,0:T(8,128)(2,1)S(1)}, bf16[4,32,512]{2,1,0:T(8,128)(2,1)S(1)}, u32[]{:S(2)}, u32[]{:S(2)}) collective-permute-start(bf16[4,32,512]{2,1,0:T(8,128)(2,1)S(1)} %collective-permute-done.8), channel_id=1, source_target_pairs={{0,1},{1,0},{2,3},{3,2},{4,5},{5,4},{6,7},{7,6},{8,9},{9,8},{10,11... | collective-permute-start | bytes 393224 | tf_op jit(solution)/shard_map/ppermute | solution.py:396

commit v5 on v4

--- a/solution.py
+++ b/solution.py
@@ -54,7 +54,11 @@
             self.returned += self.counts[section] * (self.back_width(section) // LANES)
         self.slice_at = self.sent
         self.slice_width = channels[2] // owners
-        self.sent += self.coarse[2]
+        spare = LANES - self.slice_width
+        cut = self.slice_width // spare if spare and self.slice_width % spare == 0 else 0
+        folded = self.coarse[2] // (cut + 1) if cut and self.coarse[2] % (8 * (cut + 1)) == 0 else 0
+        self.folded, self.cut, self.spare = folded, cut if folded else 0, spare
+        self.sent += self.coarse[2] - folded
 
     def out_width(self, section):
         return self.channels[section] if section < 2 else self.width
@@ -194,11 +198,16 @@
             copies[3].wait()
             values = contract(values, l4_ref[...], 1, 0).astype(BF16)
         put_pieces(out_ref, plan.out_at[section], contract(pick, values, 1, 0).astype(BF16), count)
-    count = plan.coarse[2]
-    fill = jnp.zeros((count, LANES - plan.slice_width), BF16)
+    count = plan.coarse[2] - plan.folded
+    fill = jnp.zeros((count, plan.spare), BF16)
     for owner in range(plan.owners):
         part = four_ref[:, owner * plan.slice_width : (owner + 1) * plan.slice_width]
-        out_ref[owner, plan.slice_at :, :] = jnp.concatenate([part, fill], axis=1)
+        if plan.folded:
+            last = part[count:]
+            fill = jnp.concatenate(
+                [last[:, piece * plan.spare : (piece + 1) * plan.spare] for piece in range(plan.cut)]
+            )
+        out_ref[owner, plan.slice_at :, :] = jnp.concatenate([part[:count], fill], axis=1)
 
 
 def put_parts(part_refs, even_refs, odd_refs):
@@ -450,6 +459,14 @@
     for level in levels:
         pattern = np.concatenate([pattern ^ d for d in level_swaps(level)])
     return pattern
+
+
+def unfold_slices(plan, slices):
+    parts = [slices[..., : plan.slice_width]]
+    if plan.folded:
+        spare = slices[..., plan.slice_width :].reshape(plan.owners, plan.cut, plan.folded, plan.spare)
+        parts.append(jnp.moveaxis(spare, 1, 2).reshape(plan.owners, plan.folded, plan.slice_width))
+    return jnp.concatenate(parts, axis=1).reshape(-1, plan.slice_width)
 
 
 def shape_of(*dims, dtype=BF16):
@@ -561,7 +578,7 @@
     )(core, *operands)
 
     levels = tuple(range(bits - 2, bits)), tuple(range(bits - 2))
-    slices = jnp.take(arrived[:, plan.slice_at :], me ^ gather_pattern(levels), axis=0)
+    slices = unfold_slices(plan, jnp.take(arrived[:, plan.slice_at :], me ^ gather_pattern(levels), axis=0))
     grad_fine = jnp.transpose(grad_fine.reshape(fine_features.shape), (1, 2, 0))
     rest = [
         Halving(plus(keep, swap(give, 0)), range(1, bits))
@@ -615,7 +632,7 @@
     sums = [keep.astype(F32) + received.astype(F32) for keep, received in (chain.terms for chain in rest)]
     *sums, gathered = lax.optimization_barrier((*sums, gathered))
     operands = tuple(sums)
-    operands += (slices.reshape(-1, LANES), *[g.reshape(-1, width) for g in gathered])
+    operands += (slices, *[g.reshape(-1, width) for g in gathered])
     results = pl.pallas_call(
         functools.partial(finish_kernel, plan, chains),
         out_shape=(

time: 105 us -> 105 us (level)
  waiting for transfers between devices: 42.3 us -> 40.8 us
  transfers between devices with their start and end apart: 12 -> 12, of which waited for: 6 -> 6; matrix products, arithmetic and copies ran while one was open for 9% -> 10% of each run, Pallas kernels for 9% -> 9%
where the time goes in v5:
time: 105 us; the launch traced here: 104 us
  waiting for transfers between devices  40.8 us (39%)
  starting transfers between devices  25.5 us (24%)
  Pallas kernels  25.2 us (24%)
  local copies, waits for them, and re-layouts  7.26 us (7%)
  other arithmetic  4.33 us (4%)
    all_to_all x1, waiting for transfers between devices, body(): arrived = exchange(outgoing)  16.9 us
    all_to_all x1, waiting for transfers between devices, body(): returned = exchange(back)  14.3 us
    pallas_call x1, Pallas kernels, body(): pl.pallas_call(functools.partial(strip_kernel, plan, TURNS, chains), out_...  11 us
    all_to_all x1, starting transfers between devices, body(): arrived = exchange(outgoing)  7.58 us
    all_to_all x1, starting transfers between devices, body(): returned = exchange(back)  7.18 us
    ppermute x5, starting transfers between devices, swap(): lax.ppermute(values, 'row', [(i, i ^ 1 << bit) for i in range(owners)])  5.72 us
    ppermute x5, starting transfers between devices, gather_level(): lax.ppermute(stacked, 'row', [(i, i ^ d) for i in range(owners)])  5 us
    pallas_call x1, Pallas kernels, body(): pl.pallas_call(ahead_kernel, out_shape=(shape_of(total, width),) * 2, in_...  4.84 us
  transfers between devices with their start and end apart: 12, of which 6 were waited for; matrix products, arithmetic and copies ran while one was open for 10% of the time, Pallas kernels for 9%

profile of v5, /device:TPU:0, one launch (start us, length us, event | category | flops | bytes accessed | tf_op | source)
XLA Modules:
  0.0 104.0 jit_solution(4487836346093812749)
XLA Ops:
  0.6 4.3 %pack.1 = bf16[16,296,128]{2,1,0:T(8,128)(2,1)} custom-call(s32[16]{0:T(128)} %map_ref.1, bf16[512,384]{1,0:T(8,128)(2,1)} %bitcast.59, bf16[128,768]{1,0:T(8,128)(2,1)} %bitcast.60, bf16[32,1536]{1,0:T(8,128)(2,1)} %bitcast.61, bf16[1536,512]{1,0:T(8,128)(2,1)} %refs_4_.2), custom_call_target="tpu_custom_call" | custom-call | tf_op jit(solution)/shard_map/pack/pallas_call | solution.py:505
  4.9 0.0 copy-start.5
  4.9 0.0 copy-start.6
  4.9 0.0 copy-start.11
  4.9 0.0 copy-start.9
  5.0 0.0 copy-start.10
  5.0 0.0 copy-start.7
  5.0 0.0 copy-start.8
  5.0 0.0 copy-start.3
  5.0 7.6 %all-to-all-start = ((bf16[16,296,128]{2,1,0:T(8,128)(2,1)}), bf16[16,296,128]{2,1,0:T(8,128)(2,1)}, u32[]{:S(2)}, u32[]{:S(2)}) async-start(bf16[16,296,128]{2,1,0:T(8,128)(2,1)} %pack.1), calls=%async_computation | async-start | bytes 2424832 | tf_op jit(solution)/shard_map/all_to_all | solution.py:516
  12.6 0.1 clamp_add_fusion.2
  12.7 0.1 add.144
  12.8 0.0 copy-done.10
  12.8 0.1 clamp_add_fusion.1
  12.9 0.1 add.150
  13.0 0.0 copy-done.8
  13.0 0.1 clamp_add_fusion
  13.0 0.1 add.156
  13.2 1.7 %copy.37 = bf16[256,8,192]{2,1,0:T(8,128)(2,1)} copy(bf16[256,8,192]{0,2,1:T(8,128)(2,1)S(1)} %copy-done.3) | data formatting | bytes 1572864 | tf_op args[0]
  14.9 0.6 fusion.2.refs_2_
  15.6 1.1 %fusion.refs_1_ = bf16[512,768]{1,0:T(8,128)(2,1)} fusion(s32[768]{0:T(1024)S(1)} %add.144), kind=kLoop, calls=%fused_computation.3 | loop fusion | flops 786432 | bytes 789504 | tf_op jit(solution)/shard_map/convert_element_type | solution.py:133
  16.7 4.8 %ahead.1 = (bf16[2048,512]{1,0:T(8,128)(2,1)}, bf16[2048,512]{1,0:T(8,128)(2,1)}) custom-call(bf16[192,512]{1,0:T(8,128)(2,1)} %refs_9_.1, bf16[2048,192]{1,0:T(8,128)(2,1)} %bitcast.54, bf16[512,512]{1,0:T(8,128)(2,1)} %refs_2_.2, bf16[2048,512]{1,0:T(8,128)(2,1)} %bitcast.62), custom_call_target="tpu_custom_call" | custom-call | flops 2952790016 | bytes 8000000 | tf_op jit(solution)/shard_map/ahead/pallas_call | solution.py:527
  21.5 16.9 %all-to-all-done.refs_0_ = bf16[16,296,128]{2,1,0:T(8,128)(2,1)} async-done(((bf16[16,296,128]{2,1,0:T(8,128)(2,1)}), bf16[16,296,128]{2,1,0:T(8,128)(2,1)}, u32[]{:S(2)}, u32[]{:S(2)}) %all-to-all-start) | async-done | bytes 1212448 | tf_op jit(solution)/shard_map/all_to_all | solution.py:516
  38.4 11.0 %strip_work.1 = (bf16[2048,192]{1,0:T(8,128)(2,1)}, bf16[16,240,128]{2,1,0:T(8,128)(2,1)}, bf16[8,120,512]{2,1,0:T(8,128)(2,1)}, bf16[8,120,512]{2,1,0:T(8,128)(2,1)}) custom-call(s32[1]{0:T(128)} %bitcast.core_ref, bf16[16,296,128]{2,1,0:T(8,128)(2,1)} %all-to-all-done.refs_0_, bf16[384,512]{1,0:T(8,128)(2,1)} %refs_1_.1, bf16[768,512]{1,0:T(8,128)(2,1)} %refs_3_.4, ...), custom_call_target="tpu_custom_call" | custom-call | flops 4000000000 | bytes 16000000 | tf_op jit(solution)/shard_map/strip_work/pallas_call | solution.py:555
  49.4 0.0 copy-start.12
  49.4 0.8 collective-permute-start
  50.3 7.2 %all-to-all-start.1 = ((bf16[16,240,128]{2,1,0:T(8,128)(2,1)}), bf16[16,240,128]{2,1,0:T(8,128)(2,1)S(1)}, u32[]{:S(2)}, u32[]{:S(2)}) async-start(bf16[16,240,128]{2,1,0:T(8,128)(2,1)} %get-tuple-element.48), calls=%async_computation.1 | async-start | bytes 1966080 | tf_op jit(solution)/shard_map/all_to_all | solution.py:589
  57.5 0.9 slice.9
  58.4 1.2 %gather_fusion = bf16[16,24,128]{2,1,0:T(8,128)(2,1)} fusion(bf16[16,24,128]{2,1,0:T(8,128)(2,1)S(1)} %slice.9, s32[1024]{0:T(1024)S(1)} %pad_clamp_fusion), kind=kCustom, calls=%fused_computation | custom fusion | bytes 196672 | tf_op jit(solution)/shard_map/jit(_take)/gather | solution.py:581
  59.6 0.0 collective-permute-done
  59.6 0.3 add_convert_fusion
  59.9 0.0 copy-start.4
  59.9 0.1 constant_dynamic-slice_fusion
  60.0 2.0 %collective-permute-start.1 = (bf16[2,2,120,512]{3,2,0,1:T(8,128)(2,1)S(1)}, bf16[2,2,120,512]{3,2,0,1:T(8,128)(2,1)S(1)}, u32[]{:S(2)}, u32[]{:S(2)}) collective-permute-start(bf16[2,2,120,512]{3,2,0,1:T(8,128)(2,1)S(1)} %bitcast.58), channel_id=1, source_target_pairs={{0,2},{1,3},{2,0},{3,1},{4,6},{5,7},{6,4},{7,5},{8,10},{9,11},{10,... | collective-permute-start | bytes 1474568 | tf_op jit(solution)/shard_map/ppermute | solution.py:405
  62.0 0.1 broadcast_select_fusion
  62.1 0.1 slice_bitcast_fusion
  62.2 0.1 copy.49
  62.3 0.1 reshape.178
  62.4 2.6 %copy.38 = bf16[256,8,192]{0,2,1:T(8,128)(2,1)} copy(bf16[256,8,192]{2,1,0:T(8,128)(2,1)} %bitcast.53) | data formatting | bytes 1572864 | tf_op jit(solution)/shard_map/reshape | solution.py:582
  65.1 14.3 %all-to-all-done.1.returned_ref.refs_0_ = bf16[16,240,128]{2,1,0:T(8,128)(2,1)S(1)} async-done(((bf16[16,240,128]{2,1,0:T(8,128)(2,1)}), bf16[16,240,128]{2,1,0:T(8,128)(2,1)S(1)}, u32[]{:S(2)}, u32[]{:S(2)}) %all-to-all-start.1) | async-done | bytes 983072 | tf_op jit(solution)/shard_map/all_to_all | solution.py:589
  79.4 0.1 fold_four.1.refs_5_
  79.5 0.0 copy-start.1
  79.5 2.1 %collective-permute-done.1 = bf16[2,2,120,512]{3,2,0,1:T(8,128)(2,1)S(1)} collective-permute-done((bf16[2,2,120,512]{3,2,0,1:T(8,128)(2,1)S(1)}, bf16[2,2,120,512]{3,2,0,1:T(8,128)(2,1)S(1)}, u32[]{:S(2)}, u32[]{:S(2)}) %collective-permute-start.1) | collective-permute-done | bytes 491552 | tf_op jit(solution)/shard_map/ppermute | solution.py:405
  81.6 0.1 add_convert_fusion.1
  81.8 1.6 %collective-permute-start.2 = (bf16[2,120,512]{2,1,0:T(8,128)(2,1)S(1)}, bf16[2,120,512]{2,1,0:T(8,128)(2,1)}, u32[]{:S(2)}, u32[]{:S(2)}) collective-permute-start(bf16[2,120,512]{2,1,0:T(8,128)(2,1)S(1)} %dynamic-slice_bitcast_fusion), channel_id=1, source_target_pairs={{0,4},{1,5},{2,6},{3,7},{4,0},{5,1},{6,2},{7,3},{8,12},{9,13},{10,... | collective-permute-start | bytes 737288 | tf_op jit(solution)/shard_map/ppermute | solution.py:405
  83.4 0.5 collective-permute-start.3
  83.9 2.6 %collective-permute-start.4 = (bf16[1,32,512]{2,1,0:T(8,128)(2,1)S(1)}, bf16[1,32,512]{2,1,0:T(8,128)(2,1)S(1)}, u32[]{:S(2)}, u32[]{:S(2)}) collective-permute-start(bf16[1,32,512]{2,1,0:T(8,128)(2,1)S(1)} %bitcast.45), channel_id=1, source_target_pairs={{0,8},{1,9},{2,10},{3,11},{4,12},{5,13},{6,14},{7,15},{8,0},{9,1},... | collective-permute-start | bytes 98312 | tf_op jit(solution)/shard_map/ppermute | solution.py:453
  86.5 1.3 %collective-permute-start.5 = (bf16[1,32,512]{2,1,0:T(8,128)(2,1)S(1)}, bf16[1,32,512]{2,1,0:T(8,128)(2,1)S(1)}, u32[]{:S(2)}, u32[]{:S(2)}) collective-permute-start(bf16[1,32,512]{2,1,0:T(8,128)(2,1)S(1)} %bitcast.46), channel_id=1, source_target_pairs={{0,12},{1,13},{2,14},{3,15},{4,8},{5,9},{6,10},{7,11},{8,4},{9,5},... | collective-permute-start | bytes 98312 | tf_op jit(solution)/shard_map/ppermute | solution.py:453
  87.8 4.0 %section_grads.1 = (bf16[512,384]{1,0:T(8,128)(2,1)}, bf16[128,768]{1,0:T(8,128)(2,1)}, bf16[32,1536]{1,0:T(8,128)(2,1)}) custom-call(bf16[16,240,128]{2,1,0:T(8,128)(2,1)} %copy-done, bf16[512,768]{1,0:T(8,128)(2,1)} %fusion.refs_1_, bf16[128,256]{1,0:T(8,128)(2,1)} %fusion.2.refs_2_, bf16[768,512]{1,0:T(8,128)(2,1)} %refs_3_.4, bf16[1536,512]{1,0:T(8,128)(2,1)} %refs_4_.2, ...), custom_call_target="tpu_custom_call" | custom-call | flops 500000000 | bytes 6000000 | tf_op jit(solution)/shard_map/section_grads/pallas_call | solution.py:604
  91.8 0.0 collective-permute-done.3
  91.8 0.0 collective-permute-done.4
  91.8 1.7 %collective-permute-done.5 = bf16[1,32,512]{2,1,0:T(8,128)(2,1)S(1)} collective-permute-done((bf16[1,32,512]{2,1,0:T(8,128)(2,1)S(1)}, bf16[1,32,512]{2,1,0:T(8,128)(2,1)S(1)}, u32[]{:S(2)}, u32[]{:S(2)}) %collective-permute-start.5) | collective-permute-done | bytes 32800 | tf_op jit(solution)/shard_map/ppermute | solution.py:453
  93.5 0.8 pad_maximum_fusion.1
  94.2 0.0 collective-permute-done.2
  94.3 1.0 fusion.1
  95.3 0.6 collective-permute-start.8
  95.9 1.3 %collective-permute-start.6 = (bf16[120,512]{1,0:T(8,128)(2,1)S(1)}, bf16[120,512]{1,0:T(8,128)(2,1)S(1)}, u32[]{:S(2)}, u32[]{:S(2)}) collective-permute-start(bf16[120,512]{1,0:T(8,128)(2,1)S(1)} %dynamic-slice_bitcast_fusion.1), channel_id=1, source_target_pairs={{0,8},{1,9},{2,10},{3,11},{4,12},{5,13},{6,14},{7,15},{8,0},{9,1},... | collective-permute-start | bytes 368648 | tf_op jit(solution)/shard_map/ppermute | solution.py:405
  97.2 0.0 collective-permute-start.7
  97.2 3.1 %collective-permute-done.8 = bf16[4,32,512]{2,1,0:T(8,128)(2,1)S(1)} collective-permute-done((bf16[4,32,512]{2,1,0:T(8,128)(2,1)S(1)}, bf16[4,32,512]{2,1,0:T(8,128)(2,1)S(1)}, u32[]{:S(2)}, u32[]{:S(2)}) %collective-permute-start.8) | collective-permute-done | bytes 131104 | tf_op jit(solution)/shard_map/ppermute | solution.py:453
  100.3 0.0 collective-permute-start.9
  100.3 2.7 %collective-permute-done.6 = bf16[120,512]{1,0:T(8,128)(2,1)S(1)} collective-permute-done((bf16[120,512]{1,0:T(8,128)(2,1)S(1)}, bf16[120,512]{1,0:T(8,128)(2,1)S(1)}, u32[]{:S(2)}, u32[]{:S(2)}) %collective-permute-start.6) | collective-permute-done | bytes 122912 | tf_op jit(solution)/shard_map/ppermute | solution.py:405
  103.1 0.0 collective-permute-done.7
  103.1 0.0 collective-permute-done.9
  103.1 0.9 finish.1
  (23 shorter events, 0.2 us)
Async XLA Ops:
  4.9 7.7 %copy-start.5 = (s32[16]{0:T(128)S(1)}, s32[16]{0:T(128)}, u32[]{:S(2)}) copy-start(s32[16]{0:T(128)} %map_ref.1) | copy-start | bytes 196
  4.9 7.7 %copy-start.6 = (s32[48]{0:T(128)S(1)}, s32[48]{0:T(128)}, u32[]{:S(2)}) copy-start(s32[48]{0:T(128)} %constant.80.clone) | copy-start | bytes 580
  4.9 7.7 %copy-start.11 = (s32[48]{0:T(128)S(1)}, s32[48]{0:T(128)}, u32[]{:S(2)}) copy-start(s32[48]{0:T(128)} %constant.81.clone) | copy-start | bytes 580
  4.9 7.8 %copy-start.9 = (s32[16]{0:T(128)S(1)}, s32[16]{0:T(128)}, u32[]{:S(2)}) copy-start(s32[16]{0:T(128)} %constant.83.clone) | copy-start | bytes 196
  5.0 7.8 %copy-start.10 = (s32[16]{0:T(128)S(1)}, s32[16]{0:T(128)}, u32[]{:S(2)}) copy-start(s32[16]{0:T(128)} %constant.84.clone) | copy-start | bytes 196
  5.0 8.0 %copy-start.7 = (s32[8]{0:T(128)S(1)}, s32[8]{0:T(128)}, u32[]{:S(2)}) copy-start(s32[8]{0:T(128)} %constant.86.clone) | copy-start | bytes 100
  5.0 8.0 %copy-start.8 = (s32[8]{0:T(128)S(1)}, s32[8]{0:T(128)}, u32[]{:S(2)}) copy-start(s32[8]{0:T(128)} %constant.87.clone) | copy-start | bytes 100
  5.0 8.1 %copy-start.3 = (bf16[256,8,192]{0,2,1:T(8,128)(2,1)S(1)}, bf16[256,8,192]{0,2,1:T(8,128)(2,1)}, u32[]{:S(2)}) copy-start(bf16[256,8,192]{0,2,1:T(8,128)(2,1)} %param.23) | copy-start | bytes 2359300
  5.0 33.3 %all-to-all-start = ((bf16[16,296,128]{2,1,0:T(8,128)(2,1)}), bf16[16,296,128]{2,1,0:T(8,128)(2,1)}, u32[]{:S(2)}, u32[]{:S(2)}) async-start(bf16[16,296,128]{2,1,0:T(8,128)(2,1)} %pack.1), calls=%async_computation | async-start | bytes 2424832 | tf_op jit(solution)/shard_map/all_to_all | solution.py:516
  49.4 8.1 %copy-start.12 = (s32[16]{0:T(128)S(1)}, s32[16]{0:T(128)}, u32[]{:S(2)}) copy-start(s32[16]{0:T(128)} %constant.91.clone) | copy-start | bytes 196
  49.4 10.2 %copy-start.2 = (bf16[8,120,512]{2,1,0:T(8,128)(2,1)S(1)}, bf16[8,120,512]{2,1,0:T(8,128)(2,1)}, u32[]{:S(2)}) copy-start(bf16[8,120,512]{2,1,0:T(8,128)(2,1)} %get-tuple-element.51) | copy-start | bytes 2949124
  49.4 10.2 %collective-permute-start = (bf16[8,120,512]{2,1,0:T(8,128)(2,1)}, bf16[8,120,512]{2,1,0:T(8,128)(2,1)S(1)}, u32[]{:S(2)}, u32[]{:S(2)}) collective-permute-start(bf16[8,120,512]{2,1,0:T(8,128)(2,1)} %get-tuple-element.52), channel_id=1, source_target_pairs={{0,1},{1,0},{2,3},{3,2},{4,5},{5,4},{6,7},{7,6},{8,9},{9,8},{10,11... | collective-permute-start | bytes 2949128 | tf_op jit(solution)/shard_map/ppermute | solution.py:405
  50.3 29.1 %all-to-all-start.1 = ((bf16[16,240,128]{2,1,0:T(8,128)(2,1)}), bf16[16,240,128]{2,1,0:T(8,128)(2,1)S(1)}, u32[]{:S(2)}, u32[]{:S(2)}) async-start(bf16[16,240,128]{2,1,0:T(8,128)(2,1)} %get-tuple-element.48), calls=%async_computation.1 | async-start | bytes 1966080 | tf_op jit(solution)/shard_map/all_to_all | solution.py:589
  59.9 2.1 %copy-start.4 = (bf16[16,24,128]{2,1,0:T(8,128)(2,1)S(1)}, bf16[16,24,128]{2,1,0:T(8,128)(2,1)}, u32[]{:S(2)}) copy-start(bf16[16,24,128]{2,1,0:T(8,128)(2,1)} %gather_fusion) | copy-start | bytes 294916
  60.0 21.6 %collective-permute-start.1 = (bf16[2,2,120,512]{3,2,0,1:T(8,128)(2,1)S(1)}, bf16[2,2,120,512]{3,2,0,1:T(8,128)(2,1)S(1)}, u32[]{:S(2)}, u32[]{:S(2)}) collective-permute-start(bf16[2,2,120,512]{3,2,0,1:T(8,128)(2,1)S(1)} %bitcast.58), channel_id=1, source_target_pairs={{0,2},{1,3},{2,0},{3,1},{4,6},{5,7},{6,4},{7,5},{8,10},{9,11},{10,... | collective-permute-start | bytes 1474568 | tf_op jit(solution)/shard_map/ppermute | solution.py:405
  79.4 8.4 %copy-start = (bf16[16,240,128]{2,1,0:T(8,128)(2,1)}, bf16[16,240,128]{2,1,0:T(8,128)(2,1)S(1)}, u32[]{:S(2)}) copy-start(bf16[16,240,128]{2,1,0:T(8,128)(2,1)S(1)} %all-to-all-done.1.returned_ref.refs_0_) | copy-start | bytes 2949124
  79.5 8.3 %copy-start.1 = (bf16[32,512]{1,0:T(8,128)(2,1)}, bf16[32,512]{1,0:T(8,128)(2,1)S(1)}, u32[]{:S(2)}) copy-start(bf16[32,512]{1,0:T(8,128)(2,1)S(1)} %fold_four.1.refs_5_) | copy-start | bytes 98308
  81.8 12.5 %collective-permute-start.2 = (bf16[2,120,512]{2,1,0:T(8,128)(2,1)S(1)}, bf16[2,120,512]{2,1,0:T(8,128)(2,1)}, u32[]{:S(2)}, u32[]{:S(2)}) collective-permute-start(bf16[2,120,512]{2,1,0:T(8,128)(2,1)S(1)} %dynamic-slice_bitcast_fusion), channel_id=1, source_target_pairs={{0,4},{1,5},{2,6},{3,7},{4,0},{5,1},{6,2},{7,3},{8,12},{9,13},{10,... | collective-permute-start | bytes 737288 | tf_op jit(solution)/shard_map/ppermute | solution.py:405
  83.4 8.4 %collective-permute-start.3 = (bf16[1,32,512]{2,1,0:T(8,128)(2,1)S(1)}, bf16[1,32,512]{2,1,0:T(8,128)(2,1)S(1)}, u32[]{:S(2)}, u32[]{:S(2)}) collective-permute-start(bf16[1,32,512]{2,1,0:T(8,128)(2,1)S(1)} %bitcast.44), channel_id=1, source_target_pairs={{0,4},{1,5},{2,6},{3,7},{4,0},{5,1},{6,2},{7,3},{8,12},{9,13},{10,... | collective-permute-start | bytes 98312 | tf_op jit(solution)/shard_map/ppermute | solution.py:453
  83.9 7.9 %collective-permute-start.4 = (bf16[1,32,512]{2,1,0:T(8,128)(2,1)S(1)}, bf16[1,32,512]{2,1,0:T(8,128)(2,1)S(1)}, u32[]{:S(2)}, u32[]{:S(2)}) collective-permute-start(bf16[1,32,512]{2,1,0:T(8,128)(2,1)S(1)} %bitcast.45), channel_id=1, source_target_pairs={{0,8},{1,9},{2,10},{3,11},{4,12},{5,13},{6,14},{7,15},{8,0},{9,1},... | collective-permute-start | bytes 98312 | tf_op jit(solution)/shard_map/ppermute | solution.py:453
  86.5 7.0 %collective-permute-start.5 = (bf16[1,32,512]{2,1,0:T(8,128)(2,1)S(1)}, bf16[1,32,512]{2,1,0:T(8,128)(2,1)S(1)}, u32[]{:S(2)}, u32[]{:S(2)}) collective-permute-start(bf16[1,32,512]{2,1,0:T(8,128)(2,1)S(1)} %bitcast.46), channel_id=1, source_target_pairs={{0,12},{1,13},{2,14},{3,15},{4,8},{5,9},{6,10},{7,11},{8,4},{9,5},... | collective-permute-start | bytes 98312 | tf_op jit(solution)/shard_map/ppermute | solution.py:453
  95.3 5.0 %collective-permute-start.8 = (bf16[4,32,512]{2,1,0:T(8,128)(2,1)S(1)}, bf16[4,32,512]{2,1,0:T(8,128)(2,1)S(1)}, u32[]{:S(2)}, u32[]{:S(2)}) collective-permute-start(bf16[4,32,512]{2,1,0:T(8,128)(2,1)S(1)} %pad_maximum_fusion.1), channel_id=1, source_target_pairs={{0,2},{1,3},{2,0},{3,1},{4,6},{5,7},{6,4},{7,5},{8,10},{9,11},{10,... | collective-permute-start | bytes 393224 | tf_op jit(solution)/shard_map/ppermute | solution.py:453
  95.9 7.1 %collective-permute-start.6 = (bf16[120,512]{1,0:T(8,128)(2,1)S(1)}, bf16[120,512]{1,0:T(8,128)(2,1)S(1)}, u32[]{:S(2)}, u32[]{:S(2)}) collective-permute-start(bf16[120,512]{1,0:T(8,128)(2,1)S(1)} %dynamic-slice_bitcast_fusion.1), channel_id=1, source_target_pairs={{0,8},{1,9},{2,10},{3,11},{4,12},{5,13},{6,14},{7,15},{8,0},{9,1},... | collective-permute-start | bytes 368648 | tf_op jit(solution)/shard_map/ppermute | solution.py:405
  97.2 5.8 %collective-permute-start.7 = (bf16[4,32,512]{2,1,0:T(8,128)(2,1)S(1)}, bf16[4,32,512]{2,1,0:T(8,128)(2,1)S(1)}, u32[]{:S(2)}, u32[]{:S(2)}) collective-permute-start(bf16[4,32,512]{2,1,0:T(8,128)(2,1)S(1)} %pad_maximum_fusion.1), channel_id=1, source_target_pairs={{0,1},{1,0},{2,3},{3,2},{4,5},{5,4},{6,7},{7,6},{8,9},{9,8},{10,11... | collective-permute-start | bytes 393224 | tf_op jit(solution)/shard_map/ppermute | solution.py:453
  100.3 2.8 %collective-permute-start.9 = (bf16[4,32,512]{2,1,0:T(8,128)(2,1)S(1)}, bf16[4,32,512]{2,1,0:T(8,128)(2,1)S(1)}, u32[]{:S(2)}, u32[]{:S(2)}) collective-permute-start(bf16[4,32,512]{2,1,0:T(8,128)(2,1)S(1)} %collective-permute-done.8), channel_id=1, source_target_pairs={{0,1},{1,0},{2,3},{3,2},{4,5},{5,4},{6,7},{7,6},{8,9},{9,8},{10,11... | collective-permute-start | bytes 393224 | tf_op jit(solution)/shard_map/ppermute | solution.py:405
